TPU v7x, 32 devices: a whole 2x2x4 slice. The times are simulated.
32 devices in a mesh: grp: 2 (over x), dev: 16 (over z, y, core).
Axes of the slice: x: 2, y: 2, z: 4, core: 2. Of those that a mesh axis runs over, the one named last changes fastest.
Arguments:
- diag_inverse: bfloat16 [64, 512, 512], P(('grp', 'dev')), may hold values from -1 to 1.5, as said below
- lower_block: bfloat16 [64, 512, 512], P(('grp', 'dev')), may hold values from -0.15625 to 0.15625
- upper_block: bfloat16 [64, 512, 512], P(('grp', 'dev')), may hold values from -0.15625 to 0.15625
- right_side: bfloat16 [64, 512, 128], P(('grp', 'dev')), may hold values from -6 to 6
Outputs:
- solution: bfloat16 [64, 512, 128], P(('grp', 'dev'))
Inputs may be any that keep to these rules, and one draw needn't show every extreme that they name: diag_inverse holds the given inverses of the diagonal blocks.
All inputs are finite; a program needn't handle non-finite values.
Results may differ from a plain program's by a relative error of at most 0.013.
Values may be sent and summed in bfloat16 or wider, within the bound.
No kernel may reach another device: no remote copies, remote signals or barrier semaphores. Data moves between devices by JAX's collectives and lax.ppermute only.
A program may use at most 64 MiB of HBM per device.

v0:
```python
import jax
import jax.numpy as jnp
from jax import lax
from jax.sharding import PartitionSpec as P


def passed_along(block, axis, distance):
    devices = range(lax.axis_size(axis))
    route = [(i - distance, i) for i in devices if i - distance in devices]
    return lax.ppermute(block, axis, route)


def reduce_panel(middle, left_panel, right_panel, order):
    left_spike = middle[:, :order]
    right_spike = middle[:, order : 2 * order]
    own_rhs = middle[:, 2 * order :]
    from_left = jnp.dot(left_spike, left_panel, preferred_element_type=jnp.float32)
    from_right = jnp.dot(right_spike, right_panel, preferred_element_type=jnp.float32)
    coupling = from_left[:, order : 2 * order] + from_right[:, :order]
    scaling = (jnp.eye(order, dtype=jnp.float32) + coupling).astype(jnp.bfloat16)
    outer_left = from_left[:, :order].astype(jnp.bfloat16)
    outer_right = from_right[:, order : 2 * order].astype(jnp.bfloat16)
    remaining = (
        own_rhs.astype(jnp.float32) - from_left[:, 2 * order :] - from_right[:, 2 * order :]
    ).astype(jnp.bfloat16)
    combined = jnp.concatenate([-outer_left, -outer_right, remaining], axis=1)
    return jnp.dot(scaling, combined, preferred_element_type=jnp.float32).astype(jnp.bfloat16)


def apply_panel(middle, left_values, right_values, order):
    left_spike = middle[:, :order]
    right_spike = middle[:, order : 2 * order]
    own_rhs = middle[:, 2 * order :].astype(jnp.float32)
    total = own_rhs - jnp.dot(left_spike, left_values, preferred_element_type=jnp.float32)
    total = total - jnp.dot(right_spike, right_values, preferred_element_type=jnp.float32)
    return total.astype(jnp.bfloat16)


def make_panels(diag_inverse, lower_block, upper_block, right_side):
    rows_made = []
    for row in range(diag_inverse.shape[0]):
        stacked = jnp.concatenate([lower_block[row], upper_block[row], right_side[row]], axis=1)
        rows_made.append(
            jnp.dot(diag_inverse[row], stacked, preferred_element_type=jnp.float32).astype(
                jnp.bfloat16
            )
        )
    return jnp.stack(rows_made)


def body(diag_inverse, lower_block, upper_block, right_side):
    order = diag_inverse.shape[1]
    own_panels = make_panels(diag_inverse, lower_block, upper_block, right_side)
    before = passed_along(own_panels[1], ("grp", "dev"), 1)
    level_one = reduce_panel(own_panels[0], before, own_panels[1], order)
    beside = [passed_along(level_one, ("grp", "dev"), offset) for offset in (1, -1)]
    level_two = reduce_panel(level_one, beside[0], beside[1], order)
    coarse = level_two[:, 2 * order :]
    coarse_side = [passed_along(coarse, ("grp", "dev"), offset) for offset in (2, -2)]
    even_values = apply_panel(level_two, coarse_side[0], coarse_side[1], order)
    next_even = passed_along(even_values, ("grp", "dev"), -1)
    odd_values = apply_panel(own_panels[1], even_values, next_even, order)
    return jnp.stack([even_values, odd_values])


def solution(mesh):
    return jax.shard_map(
        body,
        mesh=mesh,
        in_specs=(
            P(("grp", "dev"), None, None),
            P(("grp", "dev"), None, None),
            P(("grp", "dev"), None, None),
            P(("grp", "dev"), None, None),
        ),
        out_specs=P(("grp", "dev"), None, None),
        check_vma=False,
    )
```

profile of v0, /device:TPU:29, one launch (start us, length us, event | category | flops | bytes accessed | tf_op | source)
XLA Modules:
  0.0 91.7 jit_solution(11851883617137850407)
XLA Ops:
  0.0 1.0 %slice_bitcast_fusion.5 = (bf16[512,128]{1,0:T(8,128)(2,1)S(1)}, bf16[512,128]{1,0:T(8,128)(2,1)S(1)}) fusion(bf16[2,512,128]{2,1,0:T(8,128)(2,1)} %param.7), kind=kLoop, calls=%fused_computation.74 | loop fusion | bytes 524288 | tf_op jit(solution)/shard_map/squeeze | solution.py:42
  1.0 0.0 copy-start.2
  1.0 1.7 %slice_bitcast_fusion.2 = (bf16[512,512]{1,0:T(8,128)(2,1)S(1)}, bf16[512,512]{1,0:T(8,128)(2,1)S(1)}, bf16[512,512]{1,0:T(8,128)(2,1)S(1)}, bf16[512,512]{1,0:T(8,128)(2,1)S(1)}) fusion(bf16[2,512,512]{2,1,0:T(8,128)(2,1)} %param.6, bf16[2,512,512]{2,1,0:T(8,128)(2,1)} %param.5), kind=kLoop, calls=%fused_computation.66 | loop fusion | bytes 4194304 | tf_op jit(solution)/shard_map/squeeze | solution.py:42
  2.7 0.1 copy-done.2
  2.8 0.8 convolution_convert_fusion.2
  3.7 3.3 %collective-permute-start = (bf16[512,1152]{0,1:T(8,128)(2,1)S(1)}, bf16[512,1152]{0,1:T(8,128)(2,1)}, u32[]{:S(2)}, u32[]{:S(2)}) collective-permute-start(bf16[512,1152]{0,1:T(8,128)(2,1)S(1)} %bitcast.32), channel_id=1, source_target_pairs={{0,1},{1,2},{2,3},{3,4},{4,5},{5,6},{6,7},{7,8},{8,9},{9,10},{10,1... | collective-permute-start | bytes 3538952 | tf_op jit(solution)/shard_map/ppermute | solution.py:10
  7.0 0.8 fusion
  7.8 0.0 copy-start.1
  7.8 0.9 fusion.42
  8.7 0.1 copy-done.1
  8.8 0.7 slice.141
  9.6 1.8 %copy.20 = f32[512,128]{0,1:T(8,128)} copy(f32[512,128]{1,0:T(8,128)} %slice.141) | data formatting | bytes 524288
  11.3 0.9 fusion.28
  12.2 7.9 %collective-permute-done = bf16[512,1152]{0,1:T(8,128)(2,1)} collective-permute-done((bf16[512,1152]{0,1:T(8,128)(2,1)S(1)}, bf16[512,1152]{0,1:T(8,128)(2,1)}, u32[]{:S(2)}, u32[]{:S(2)}) %collective-permute-start) | collective-permute-done | bytes 1179680 | tf_op jit(solution)/shard_map/ppermute | solution.py:10
  20.1 2.3 %fusion.44 = f32[512,1152]{1,0:T(8,128)S(1)} fusion(bf16[512,1152]{0,1:T(8,128)(2,1)} %collective-permute-done, bf16[512,1152]{0,1:T(8,128)(2,1)} %copy-done.1), kind=kOutput, calls=%fused_computation.58 | convolution fusion | flops 603979776 | bytes 4063232 | tf_op jit(solution)/shard_map/dot_general | solution.py:17
  22.4 0.0 copy-start
  22.4 0.8 slice.140
  23.2 0.7 copy-done
  23.9 0.8 fusion.27
  24.8 1.8 %copy.19 = f32[512,128]{0,1:T(8,128)} copy(f32[512,128]{1,0:T(8,128)} %slice.140) | data formatting | bytes 524288
  26.5 1.8 %subtract_convert_fusion = bf16[512,128]{0,1:T(8,128)(2,1)} fusion(f32[512,128]{0,1:T(8,128)} %copy.20, f32[512,128]{0,1:T(8,128)} %copy.19, bf16[512,1152]{0,1:T(8,128)(2,1)} %copy-done.1), kind=kLoop, calls=%fused_computation.72 | loop fusion | flops 262144 | bytes 786432 | tf_op jit(solution)/shard_map/convert_element_type | solution.py:25
  28.3 1.7 %copy.7 = bf16[512,128]{1,0:T(8,128)(2,1)} copy(bf16[512,128]{0,1:T(8,128)(2,1)} %subtract_convert_fusion) | data formatting | bytes 262144 | tf_op jit(solution)/shard_map/convert_element_type | solution.py:25
  30.0 2.4 %convolution_convert_fusion.1 = bf16[512,1152]{1,0:T(8,128)(2,1)S(1)} fusion(bf16[512,128]{1,0:T(8,128)(2,1)} %copy.7, bf16[512,512]{1,0:T(8,128)(2,1)} %fusion.28, bf16[512,512]{1,0:T(8,128)(2,1)} %fusion.27, f32[512,1152]{1,0:T(8,128)S(1)} %fusion.42, f32[512,1152]{1,0:T(8,128)} %copy-done), kind=kOutput, calls=%fused_computation.1 | convolution fusion | flops 609419264 | bytes 4456448 | tf_op jit(solution)/shard_map/dot_general | solution.py:27
  32.4 3.8 %collective-permute-start.2 = (bf16[512,1152]{1,0:T(8,128)(2,1)S(1)}, bf16[512,1152]{1,0:T(8,128)(2,1)S(1)}, u32[]{:S(2)}, u32[]{:S(2)}) collective-permute-start(bf16[512,1152]{1,0:T(8,128)(2,1)S(1)} %convolution_convert_fusion.1), channel_id=1, source_target_pairs={{1,0},{2,1},{3,2},{4,3},{5,4},{6,5},{7,6},{8,7},{9,8},{10,9},{11,1... | collective-permute-start | bytes 3538952 | tf_op jit(solution)/shard_map/ppermute | solution.py:10
  36.2 6.2 %collective-permute-start.1 = (bf16[512,1152]{1,0:T(8,128)(2,1)S(1)}, bf16[512,1152]{1,0:T(8,128)(2,1)S(1)}, u32[]{:S(2)}, u32[]{:S(2)}) collective-permute-start(bf16[512,1152]{1,0:T(8,128)(2,1)S(1)} %convolution_convert_fusion.1), channel_id=1, source_target_pairs={{0,1},{1,2},{2,3},{3,4},{4,5},{5,6},{6,7},{7,8},{8,9},{9,10},{10,1... | collective-permute-start | bytes 3538952 | tf_op jit(solution)/shard_map/ppermute | solution.py:10
  42.4 12.0 %collective-permute-done.2 = bf16[512,1152]{1,0:T(8,128)(2,1)S(1)} collective-permute-done((bf16[512,1152]{1,0:T(8,128)(2,1)S(1)}, bf16[512,1152]{1,0:T(8,128)(2,1)S(1)}, u32[]{:S(2)}, u32[]{:S(2)}) %collective-permute-start.2) | collective-permute-done | bytes 1179680 | tf_op jit(solution)/shard_map/ppermute | solution.py:10
  54.5 0.8 fusion.38
  55.3 0.1 fusion.30
  55.4 0.2 collective-permute-done.1
  55.5 0.8 fusion.40
  56.4 0.1 fusion.29
  56.5 0.8 convolution_convert_fusion
  57.3 11.6 %collective-permute-start.4 = (bf16[512,128]{0,1:T(8,128)(2,1)S(1)}, bf16[512,128]{0,1:T(8,128)(2,1)S(1)}, u32[]{:S(2)}, u32[]{:S(2)}) collective-permute-start(bf16[512,128]{0,1:T(8,128)(2,1)S(1)} %slice.151), channel_id=1, source_target_pairs={{2,0},{3,1},{4,2},{5,3},{6,4},{7,5},{8,6},{9,7},{10,8},{11,9},{12,... | collective-permute-start | bytes 393224 | tf_op jit(solution)/shard_map/ppermute | solution.py:10
  68.9 2.2 %collective-permute-start.3 = (bf16[512,128]{0,1:T(8,128)(2,1)S(1)}, bf16[512,128]{0,1:T(8,128)(2,1)S(1)}, u32[]{:S(2)}, u32[]{:S(2)}) collective-permute-start(bf16[512,128]{0,1:T(8,128)(2,1)S(1)} %slice.151), channel_id=1, source_target_pairs={{0,2},{1,3},{2,4},{3,5},{4,6},{5,7},{6,8},{7,9},{8,10},{9,11},{10,... | collective-permute-start | bytes 393224 | tf_op jit(solution)/shard_map/ppermute | solution.py:10
  71.2 0.4 collective-permute-done.4
  71.6 0.2 fusion.35
  71.8 2.8 %collective-permute-done.3 = bf16[512,128]{0,1:T(8,128)(2,1)S(1)} collective-permute-done((bf16[512,128]{0,1:T(8,128)(2,1)S(1)}, bf16[512,128]{0,1:T(8,128)(2,1)S(1)}, u32[]{:S(2)}, u32[]{:S(2)}) %collective-permute-start.3) | collective-permute-done | bytes 131104 | tf_op jit(solution)/shard_map/ppermute | solution.py:10
  74.7 0.2 fusion.23
  74.9 7.4 %collective-permute-start.5 = (bf16[512,128]{0,1:T(8,128)(2,1)S(1)}, bf16[512,128]{0,1:T(8,128)(2,1)S(1)}, u32[]{:S(2)}, u32[]{:S(2)}) collective-permute-start(bf16[512,128]{0,1:T(8,128)(2,1)S(1)} %fusion.23), channel_id=1, source_target_pairs={{1,0},{2,1},{3,2},{4,3},{5,4},{6,5},{7,6},{8,7},{9,8},{10,9},{11,1... | collective-permute-start | bytes 393224 | tf_op jit(solution)/shard_map/ppermute | solution.py:10
  82.3 0.2 convolution_subtract_fusion.1
  82.5 8.0 %collective-permute-done.5 = bf16[512,128]{0,1:T(8,128)(2,1)S(1)} collective-permute-done((bf16[512,128]{0,1:T(8,128)(2,1)S(1)}, bf16[512,128]{0,1:T(8,128)(2,1)S(1)}, u32[]{:S(2)}, u32[]{:S(2)}) %collective-permute-start.5) | collective-permute-done | bytes 131104 | tf_op jit(solution)/shard_map/ppermute | solution.py:10
  90.6 0.2 fusion.24
  90.8 0.8 copy.13
  (3 shorter events, 0.1 us)
Async XLA Ops:
  1.0 1.9 %copy-start.2 = (bf16[2,512,512]{2,1,0:T(8,128)(2,1)S(1)}, bf16[2,512,512]{2,1,0:T(8,128)(2,1)}, u32[]{:S(2)}) copy-start(bf16[2,512,512]{2,1,0:T(8,128)(2,1)} %param.4) | copy-start | bytes 3145732
  3.7 16.4 %collective-permute-start = (bf16[512,1152]{0,1:T(8,128)(2,1)S(1)}, bf16[512,1152]{0,1:T(8,128)(2,1)}, u32[]{:S(2)}, u32[]{:S(2)}) collective-permute-start(bf16[512,1152]{0,1:T(8,128)(2,1)S(1)} %bitcast.32), channel_id=1, source_target_pairs={{0,1},{1,2},{2,3},{3,4},{4,5},{5,6},{6,7},{7,8},{8,9},{9,10},{10,1... | collective-permute-start | bytes 3538952 | tf_op jit(solution)/shard_map/ppermute | solution.py:10
  7.8 1.0 %copy-start.1 = (bf16[512,1152]{0,1:T(8,128)(2,1)}, bf16[512,1152]{0,1:T(8,128)(2,1)S(1)}, u32[]{:S(2)}) copy-start(bf16[512,1152]{0,1:T(8,128)(2,1)S(1)} %fusion) | copy-start | bytes 3538948
  22.4 1.5 %copy-start = (f32[512,1152]{1,0:T(8,128)}, f32[512,1152]{1,0:T(8,128)S(1)}, u32[]{:S(2)}) copy-start(f32[512,1152]{1,0:T(8,128)S(1)} %fusion.44) | copy-start | bytes 7077892
  32.4 22.1 %collective-permute-start.2 = (bf16[512,1152]{1,0:T(8,128)(2,1)S(1)}, bf16[512,1152]{1,0:T(8,128)(2,1)S(1)}, u32[]{:S(2)}, u32[]{:S(2)}) collective-permute-start(bf16[512,1152]{1,0:T(8,128)(2,1)S(1)} %convolution_convert_fusion.1), channel_id=1, source_target_pairs={{1,0},{2,1},{3,2},{4,3},{5,4},{6,5},{7,6},{8,7},{9,8},{10,9},{11,1... | collective-permute-start | bytes 3538952 | tf_op jit(solution)/shard_map/ppermute | solution.py:10
  36.2 19.3 %collective-permute-start.1 = (bf16[512,1152]{1,0:T(8,128)(2,1)S(1)}, bf16[512,1152]{1,0:T(8,128)(2,1)S(1)}, u32[]{:S(2)}, u32[]{:S(2)}) collective-permute-start(bf16[512,1152]{1,0:T(8,128)(2,1)S(1)} %convolution_convert_fusion.1), channel_id=1, source_target_pairs={{0,1},{1,2},{2,3},{3,4},{4,5},{5,6},{6,7},{7,8},{8,9},{9,10},{10,1... | collective-permute-start | bytes 3538952 | tf_op jit(solution)/shard_map/ppermute | solution.py:10
  57.3 14.3 %collective-permute-start.4 = (bf16[512,128]{0,1:T(8,128)(2,1)S(1)}, bf16[512,128]{0,1:T(8,128)(2,1)S(1)}, u32[]{:S(2)}, u32[]{:S(2)}) collective-permute-start(bf16[512,128]{0,1:T(8,128)(2,1)S(1)} %slice.151), channel_id=1, source_target_pairs={{2,0},{3,1},{4,2},{5,3},{6,4},{7,5},{8,6},{9,7},{10,8},{11,9},{12,... | collective-permute-start | bytes 393224 | tf_op jit(solution)/shard_map/ppermute | solution.py:10
  68.9 5.7 %collective-permute-start.3 = (bf16[512,128]{0,1:T(8,128)(2,1)S(1)}, bf16[512,128]{0,1:T(8,128)(2,1)S(1)}, u32[]{:S(2)}, u32[]{:S(2)}) collective-permute-start(bf16[512,128]{0,1:T(8,128)(2,1)S(1)} %slice.151), channel_id=1, source_target_pairs={{0,2},{1,3},{2,4},{3,5},{4,6},{5,7},{6,8},{7,9},{8,10},{9,11},{10,... | collective-permute-start | bytes 393224 | tf_op jit(solution)/shard_map/ppermute | solution.py:10
  74.9 15.7 %collective-permute-start.5 = (bf16[512,128]{0,1:T(8,128)(2,1)S(1)}, bf16[512,128]{0,1:T(8,128)(2,1)S(1)}, u32[]{:S(2)}, u32[]{:S(2)}) collective-permute-start(bf16[512,128]{0,1:T(8,128)(2,1)S(1)} %fusion.23), channel_id=1, source_target_pairs={{1,0},{2,1},{3,2},{4,3},{5,4},{6,5},{7,6},{8,7},{9,8},{10,9},{11,1... | collective-permute-start | bytes 393224 | tf_op jit(solution)/shard_map/ppermute | solution.py:10
where the time goes:
time: 92.1 us; the launch traced here: 91.7 us
  starting transfers between devices  34.5 us (37%)
  waiting for transfers between devices  31.4 us (34%)
  local copies, waits for them, and re-layouts  11.2 us (12%)
  matrix products  10.7 us (12%)
  other arithmetic  3.64 us (4%)
    ppermute x6, starting transfers between devices, passed_along(): return lax.ppermute(block, axis, route)  34.5 us
    ppermute x6, waiting for transfers between devices, passed_along(): return lax.ppermute(block, axis, route)  31.4 us
    unnamed x8, local copies, waits for them, and re-layouts  4.51 us
    dot_general x2, matrix products, reduce_panel(): jnp.dot(scaling, combined, preferred_element_type=jnp.float32)  3.23 us
    dot_general x2, matrix products, reduce_panel(): jnp.dot(left_spike, left_panel, preferred_element_type=jnp.float32)  3.16 us
  transfers between devices with their start and end apart: 6, of which 6 were waited for; matrix products, arithmetic and copies ran while one was open for 7% of the time, Pallas kernels for 0%

commit v1 on v0

v1 whole, which is shorter than its diff:
```python
import functools

import jax
import jax.numpy as jnp
from jax import lax
from jax.experimental import pallas as pl
from jax.experimental.pallas import tpu as pltpu
from jax.sharding import PartitionSpec as P

AXES = ("grp", "dev")
BF16 = jnp.bfloat16
F32 = jnp.float32
EVEN, ODD = 0, 1


def dot(a, b):
    return jnp.dot(a, b, preferred_element_type=F32)


def on_parity(parity, kernel):
    def guarded(*refs):
        @pl.when(lax.rem(lax.axis_index(AXES), 2) == parity)
        def _():
            kernel(*refs)

    return guarded


def local_call(kernel, outs, ins, flops, in_hbm=0, scratch=()):
    vmem = pl.BlockSpec(memory_space=pltpu.VMEM)
    anywhere = pl.BlockSpec(memory_space=pl.ANY)
    many = len(outs) > 1
    return pl.pallas_call(
        kernel,
        out_shape=outs if many else outs[0],
        in_specs=[anywhere] * in_hbm + [vmem] * (len(ins) - in_hbm),
        out_specs=[vmem] * len(outs) if many else vmem,
        scratch_shapes=list(scratch),
        compiler_params=pltpu.CompilerParams(vmem_limit_bytes=16 * 1024 * 1024),
        cost_estimate=pl.CostEstimate(flops=flops, bytes_accessed=0, transcendentals=0),
    )(*ins)


def bf16_array(rows, columns):
    return jax.ShapeDtypeStruct((rows, columns), BF16)


def f32_array(rows, columns):
    return jax.ShapeDtypeStruct((rows, columns), F32)


def fetch(source, row, target, sem):
    copy = pltpu.make_async_copy(source.at[row], target, sem)
    copy.start()
    return copy


def second_row(order, diag, upper, right, out, diag_b, upper_b, right_b, sems):
    copies = [
        fetch(diag, 1, diag_b, sems.at[0]),
        fetch(upper, 1, upper_b, sems.at[1]),
        fetch(right, 1, right_b, sems.at[2]),
    ]
    copies[0].wait()
    copies[1].wait()
    out[:, :order] = dot(diag_b[...], upper_b[...]).astype(BF16)
    copies[2].wait()
    out[:, order:] = dot(diag_b[...], right_b[...]).astype(BF16)


def second_row_rest(order, diag, upper, right, made, out, diag_b, upper_b, right_b, sems):
    odd = lax.rem(lax.axis_index(AXES), 2) == ODD

    @pl.when(odd)
    def _():
        copy = pltpu.make_async_copy(made, out, sems.at[0])
        copy.start()
        copy.wait()

    @pl.when(jnp.logical_not(odd))
    def _():
        second_row(order, diag, upper, right, out, diag_b, upper_b, right_b, sems)


def own_products(
    order, diag, lower, upper, right, vg_b, w_a, w_b, m, n, r,
    diag_a, lower_a, upper_a, right_a, diag_b, lower_b, sems,
):
    d_a = fetch(diag, 0, diag_a, sems.at[0])
    u_a = fetch(upper, 0, upper_a, sems.at[1])
    d_b = fetch(diag, 1, diag_b, sems.at[2])
    l_b = fetch(lower, 1, lower_b, sems.at[3])
    l_a = fetch(lower, 0, lower_a, sems.at[4])
    r_a = fetch(right, 0, right_a, sems.at[5])
    d_a.wait()
    u_a.wait()
    v_a = dot(diag_a[...], upper_a[...]).astype(BF16)
    d_b.wait()
    l_b.wait()
    w_b[...] = dot(diag_b[...], lower_b[...]).astype(BF16)
    l_a.wait()
    w_a[...] = dot(diag_a[...], lower_a[...]).astype(BF16)
    r_a.wait()
    g_a = dot(diag_a[...], right_a[...]).astype(BF16)
    n[...] = dot(v_a, vg_b[:, :order]).astype(BF16)
    r[...] = g_a.astype(F32) - dot(v_a, vg_b[:, order:])
    m[...] = dot(v_a, w_b[...])


def scale_one(order, w_a, m, r, vg_left, scale, tg):
    eye = (
        lax.broadcasted_iota(jnp.int32, (order, order), 0)
        == lax.broadcasted_iota(jnp.int32, (order, order), 1)
    ).astype(F32)
    scale[...] = (eye + (dot(w_a[...], vg_left[:, :order]) + m[...])).astype(BF16)
    rest = (r[...] - dot(w_a[...], vg_left[:, order:])).astype(BF16)
    tg[:, :order] = dot(scale[...], w_a[...]).astype(BF16)
    tg[:, order:] = dot(scale[...], rest).astype(BF16)


def spikes_one(order, scale, n, w_b, tg, v_one, w_vg):
    v_one[...] = (-dot(scale[...], n[...])).astype(BF16)
    w_vg[:, :order] = dot(w_b[...], v_one[...]).astype(BF16)
    w_vg[:, order:] = dot(w_b[...], tg[:, order:]).astype(BF16)


def level_one_odd(order, w_a, m, r, vg_left, n, w_b, tg, v_one, w_vg, scale):
    scale_one(order, w_a, m, r, vg_left, scale, tg)
    spikes_one(order, scale, n, w_b, tg, v_one, w_vg)


def scaled_two(order, v, tg, v_one, w_b, w_vg_left, t_right):
    v16 = v.astype(BF16)
    t = tg[:, :order]
    from_left = dot(t, dot(w_vg_left[:, :order], v16).astype(BF16))
    own = dot(w_b[...], v16).astype(BF16)
    from_right = dot(v_one[...], dot(t_right[:, :order], own).astype(BF16))
    return v - from_left - from_right


def right_side_two(order, tg, v_one, w_vg_left, tg_right):
    return (
        tg[:, order:].astype(F32)
        + dot(tg[:, :order], w_vg_left[:, order:])
        - dot(v_one[...], tg_right[:, order:])
    )


def level_two(order, tg, v_one, w_b, w_vg_left, tg_right, g_two, w_g):
    h = right_side_two(order, tg, v_one, w_vg_left, tg_right)
    g_two[...] = scaled_two(order, h, tg, v_one, w_b, w_vg_left, tg_right).astype(BF16)
    w_g[...] = dot(w_b[...], g_two[...]).astype(BF16)


def level_two_odd(order, tg, v_one, w_b, w_vg_left, tg_right, g_right, g_v, w_g):
    h = right_side_two(order, tg, v_one, w_vg_left, tg_right)
    g_v[:, : h.shape[1]] = scaled_two(order, h, tg, v_one, w_b, w_vg_left, tg_right).astype(BF16)
    w_g[...] = dot(w_b[...], g_v[:, : h.shape[1]]).astype(BF16)
    g_v[:, h.shape[1] :] = dot(v_one[...], g_right[...]).astype(BF16)


def pass_right(order, tg, w_b, from_left, out):
    out[...] = dot(w_b[...], (-dot(tg[:, :order], from_left[...])).astype(BF16)).astype(BF16)


def pass_left(v_one, g_v, out):
    out[...] = dot(v_one[...], g_v[:, : out.shape[1]]).astype(BF16)


def top_value(order, g, tg, v_one, w_b, w_vg_left, t_right, p, q):
    h = dot(v_one[...], q) - dot(tg[:, :order], p[...])
    scaled = scaled_two(order, h, tg, v_one, w_b, w_vg_left, t_right)
    return (g.astype(F32) + scaled).astype(BF16)


def top_even(order, g_two, tg, v_one, w_b, w_vg_left, t_right, p, g_v, x):
    columns = x.shape[1]
    x[...] = top_value(
        order, g_two[...], tg, v_one, w_b, w_vg_left, t_right, p, g_v[:, columns:]
    )


def top_odd(order, g_v, tg, v_one, w_b, w_vg_left, t_right, p, q, x):
    columns = x.shape[1]
    x[...] = top_value(
        order, g_v[:, :columns], tg, v_one, w_b, w_vg_left, t_right, p, q[...]
    )


def finish(order, vg_b, w_b, x_even, x_odd, x_next_odd, x_next_even, out):
    odd = lax.rem(lax.axis_index(AXES), 2) == ODD

    def rows(x, x_next):
        out[0] = x[...]
        out[1] = (
            vg_b[:, order:].astype(F32) - dot(w_b[...], x[...]) - dot(vg_b[:, :order], x_next[...])
        ).astype(BF16)

    @pl.when(odd)
    def _():
        rows(x_odd, x_next_even)

    @pl.when(jnp.logical_not(odd))
    def _():
        rows(x_even, x_next_odd)


def body(diag, lower, upper, right):
    order, rhs = diag.shape[1], right.shape[2]
    count = lax.axis_size(AXES)
    evens, odds = range(0, count, 2), range(1, count, 2)
    pairs_right = [(i, i + 1) for i in evens if i + 1 < count]
    pairs_left = [(i + 1, i) for i in evens if i + 1 < count]
    gaps_right = [(i, i + 1) for i in odds if i + 1 < count]
    gaps_left = [(i + 1, i) for i in odds if i + 1 < count]

    def sent(block, route):
        return lax.ppermute(block, AXES, route)

    part = functools.partial
    square = 2 * order**3
    thin = 2 * order * order * rhs
    block = pltpu.VMEM((order, order), BF16)
    side = pltpu.VMEM((order, rhs), BF16)
    wide = bf16_array(order, order + rhs)
    full = bf16_array(order, order)
    slim = bf16_array(order, rhs)
    twin = bf16_array(order, 2 * rhs)

    row_scratch = (block, block, side, pltpu.SemaphoreType.DMA((3,)))
    vg_odd = local_call(
        on_parity(ODD, part(second_row, order)),
        [wide], [diag, upper, right], square + thin, 3, row_scratch,
    )
    vg_gap = sent(vg_odd, gaps_right)
    vg_b = local_call(
        part(second_row_rest, order),
        [wide], [diag, upper, right, vg_odd], square + thin, 4, row_scratch,
    )
    vg_pair = sent(vg_b, pairs_right)
    w_a, w_b, m, n, r = local_call(
        part(own_products, order),
        [full, full, f32_array(order, order), full, f32_array(order, rhs)],
        [diag, lower, upper, right, vg_b], 5 * square + 2 * thin, 4,
        (block, block, block, side, block, block, pltpu.SemaphoreType.DMA((6,))),
    )

    tg_odd, v_odd, w_vg_odd = local_call(
        on_parity(ODD, part(level_one_odd, order)),
        [wide, full, wide], [w_a, m, r, vg_pair, n, w_b], 4 * square + 3 * thin, 0, (block,),
    )
    w_vg_gap = sent(w_vg_odd, gaps_right)
    tg_pair = sent(tg_odd, pairs_left)

    scale_even, tg_even = local_call(
        on_parity(EVEN, part(scale_one, order)),
        [full, wide], [w_a, m, r, vg_gap], 2 * square + 2 * thin,
    )
    tg_gap = sent(tg_even, gaps_left)
    v_even, w_vg_even = local_call(
        on_parity(EVEN, part(spikes_one, order)),
        [full, wide], [scale_even, n, w_b, tg_even], 2 * square + thin,
    )
    w_vg_pair = sent(w_vg_even, pairs_right)

    g_even, w_g_even = local_call(
        on_parity(EVEN, part(level_two, order)),
        [slim, slim], [tg_even, v_even, w_b, w_vg_gap, tg_pair], 8 * thin,
    )
    g_gap = sent(g_even, gaps_left)
    a_pair = sent(w_g_even, pairs_right)
    p_odd = local_call(
        on_parity(ODD, part(pass_right, order)), [slim], [tg_odd, w_b, a_pair], 2 * thin
    )
    p_gap = sent(p_odd, gaps_right)

    g_v_odd, w_g_odd = local_call(
        on_parity(ODD, part(level_two_odd, order)),
        [twin, slim], [tg_odd, v_odd, w_b, w_vg_pair, tg_gap, g_gap], 9 * thin,
    )
    g_v_pair = sent(g_v_odd, pairs_left)
    a_gap = sent(w_g_odd, gaps_right)

    q_even = local_call(on_parity(EVEN, pass_left), [slim], [v_even, g_v_pair], thin)
    q_gap = sent(q_even, gaps_left)
    x_even = local_call(
        on_parity(EVEN, part(top_even, order)),
        [slim], [g_even, tg_even, v_even, w_b, w_vg_gap, tg_pair, p_gap, g_v_pair], 7 * thin,
    )
    x_gap = sent(x_even, gaps_left)
    p_even = local_call(
        on_parity(EVEN, part(pass_right, order)), [slim], [tg_even, w_b, a_gap], 2 * thin
    )
    p_pair = sent(p_even, pairs_right)
    x_odd = local_call(
        on_parity(ODD, part(top_odd, order)),
        [slim], [g_v_odd, tg_odd, v_odd, w_b, w_vg_pair, tg_gap, p_pair, q_gap], 7 * thin,
    )
    x_pair = sent(x_odd, pairs_left)
    return local_call(
        part(finish, order),
        [jax.ShapeDtypeStruct((2, order, rhs), BF16)],
        [vg_b, w_b, x_even, x_odd, x_pair, x_gap], 2 * thin,
    )


def solution(mesh):
    split = P(AXES, None, None)
    return jax.shard_map(
        body, mesh=mesh, in_specs=(split,) * 4, out_specs=split, check_vma=False
    )
```

time: 92.1 us -> 66.3 us (0.72)
  Pallas kernels: 0 us -> 11.9 us
  matrix products: 10.7 us -> 0 us
  starting transfers between devices: 34.5 us -> 24.4 us
  local copies, waits for them, and re-layouts: 11.2 us -> 3.4 us
  waiting for transfers between devices: 31.4 us -> 25.9 us
  other arithmetic: 3.64 us -> 0 us
    pallas_call x0 -> x14, Pallas kernels: none -> 11.9 us  [local_call(): pl.pallas_call(kernel, out_shape=outs if many else outs[0], in_specs=[any...]
    dot_general x12 -> x0, matrix products: 10.7 us -> none  [the longest x2 3.23 us: reduce_panel(): jnp.dot(scaling, combined, preferred_element_type=jnp.float32)]
    ppermute x6 -> x15, starting transfers between devices: 34.5 us -> 24.4 us  [sent(): return lax.ppermute(block, AXES, route)]
    ppermute x6 -> x15, waiting for transfers between devices: 31.4 us -> 25.9 us  [sent(): return lax.ppermute(block, AXES, route)]
    squeeze x2 -> x0, local copies, waits for them, and re-layouts: 2.73 us -> none  [the longest x1 1.74 us: make_panels(): upper_block[row]]
    convert_element_type x2 -> x0, other arithmetic: 1.81 us -> none  [reduce_panel(): remaining = (own_rhs.astype(jnp.float32) - from_left[:, 2 * order:] - fro...]
    neg x4 -> x0, other arithmetic: 1.8 us -> none  [reduce_panel(): combined = jnp.concatenate([-outer_left, -outer_right, remaining], axis=1)]
    convert_element_type x1 -> x0, local copies, waits for them, and re-layouts: 1.66 us -> none  [reduce_panel(): remaining = (own_rhs.astype(jnp.float32) - from_left[:, 2 * order:] - fro...]
  transfers between devices with their start and end apart: 6 -> 15, of which waited for: 6 -> 7; matrix products, arithmetic and copies ran while one was open for 7% -> 0% of each run, Pallas kernels for 0% -> 11%
where the time goes in v1:
time: 66.3 us; the launch traced here: 65.8 us
  waiting for transfers between devices  25.9 us (39%)
  starting transfers between devices  24.4 us (37%)
  Pallas kernels  11.9 us (18%)
  local copies, waits for them, and re-layouts  3.4 us (5%)
    ppermute x15, waiting for transfers between devices, sent(): return lax.ppermute(block, AXES, route)  25.9 us
    ppermute x15, starting transfers between devices, sent(): return lax.ppermute(block, AXES, route)  24.4 us
    pallas_call x14, Pallas kernels, local_call(): pl.pallas_call(kernel, out_shape=outs if many else outs[0], in_specs=[any...  11.9 us
    unnamed x8, local copies, waits for them, and re-layouts  3.4 us
  transfers between devices with their start and end apart: 15, of which 7 were waited for; matrix products, arithmetic and copies ran while one was open for 0% of the time, Pallas kernels for 11%

profile of v1, /device:TPU:29, one launch (start us, length us, event | category | flops | bytes accessed | tf_op | source)
XLA Modules:
  0.0 65.8 jit_solution(14285582583332611195)
XLA Ops:
  0.0 0.0 copy-start
  0.0 1.2 %copy-done = bf16[2,512,512]{2,1,0:T(8,128)(2,1)S(1)} copy-done((bf16[2,512,512]{2,1,0:T(8,128)(2,1)S(1)}, bf16[2,512,512]{2,1,0:T(8,128)(2,1)}, u32[]{:S(2)}) %copy-start) | copy-done | bytes 1048600
  1.2 0.0 copy-start.1
  1.2 1.2 %copy-done.1 = bf16[2,512,512]{2,1,0:T(8,128)(2,1)S(1)} copy-done((bf16[2,512,512]{2,1,0:T(8,128)(2,1)S(1)}, bf16[2,512,512]{2,1,0:T(8,128)(2,1)}, u32[]{:S(2)}) %copy-start.1) | copy-done | bytes 1048600
  2.5 0.0 copy-start.2
  2.5 0.9 %copy-done.2 = bf16[2,512,128]{2,1,0:T(8,128)(2,1)S(1)} copy-done((bf16[2,512,128]{2,1,0:T(8,128)(2,1)S(1)}, bf16[2,512,128]{2,1,0:T(8,128)(2,1)}, u32[]{:S(2)}) %copy-start.2) | copy-done | bytes 262168
  3.4 1.3 %shard_map.46.made = bf16[512,640]{1,0:T(8,128)(2,1)S(1)} custom-call(bf16[2,512,512]{2,1,0:T(8,128)(2,1)S(1)} %copy-done, bf16[2,512,512]{2,1,0:T(8,128)(2,1)S(1)} %copy-done.1, bf16[2,512,128]{2,1,0:T(8,128)(2,1)S(1)} %copy-done.2), custom_call_target="tpu_custom_call" | custom-call | flops 335544320 | tf_op jit(solution)/shard_map/pallas_call | solution.py:33
  4.7 0.0 copy-start.3
  4.7 0.3 shard_map.47.vg_b
  4.9 1.4 %collective-permute-start.1 = (bf16[512,640]{1,0:T(8,128)(2,1)S(1)}, bf16[512,640]{1,0:T(8,128)(2,1)S(1)}, u32[]{:S(2)}, u32[]{:S(2)}) collective-permute-start(bf16[512,640]{1,0:T(8,128)(2,1)S(1)} %shard_map.47.vg_b), channel_id=1, source_target_pairs={{0,1},{2,3},{4,5},{6,7},{8,9},{10,11},{12,13},{14,15},{16,17},{18,... | collective-permute-start | bytes 1966088 | tf_op jit(solution)/shard_map/ppermute | solution.py:218
  6.4 3.8 %collective-permute-start = (bf16[512,640]{1,0:T(8,128)(2,1)S(1)}, bf16[512,640]{1,0:T(8,128)(2,1)S(1)}, u32[]{:S(2)}, u32[]{:S(2)}) collective-permute-start(bf16[512,640]{1,0:T(8,128)(2,1)S(1)} %shard_map.46.made), channel_id=1, source_target_pairs={{1,2},{3,4},{5,6},{7,8},{9,10},{11,12},{13,14},{15,16},{17,18},{19... | collective-permute-start | bytes 1966088 | tf_op jit(solution)/shard_map/ppermute | solution.py:218
  10.2 0.0 copy-done.3
  10.2 2.7 %shard_map.48 = (bf16[512,512]{1,0:T(8,128)(2,1)S(1)}, bf16[512,512]{1,0:T(8,128)(2,1)S(1)}, f32[512,512]{1,0:T(8,128)S(1)}, bf16[512,512]{1,0:T(8,128)(2,1)S(1)}, f32[512,128]{1,0:T(8,128)S(1)}) custom-call(bf16[2,512,512]{2,1,0:T(8,128)(2,1)S(1)} %copy-done, bf16[2,512,512]{2,1,0:T(8,128)(2,1)S(1)} %copy-done.3, bf16[2,512,512]{2,1,0:T(8,128)(2,1)S(1)} %copy-done.1, ...), custom_call_target="tpu_custom_call" | custom-call | flops 1476395008 | tf_op jit(solution)/shard_map/pallas_call | solution.py:33
  12.9 0.0 collective-permute-done.1.refs_3_
  12.9 1.7 %shard_map.51 = (bf16[512,640]{1,0:T(8,128)(2,1)S(1)}, bf16[512,512]{1,0:T(8,128)(2,1)S(1)}, bf16[512,640]{1,0:T(8,128)(2,1)S(1)}) custom-call(bf16[512,512]{1,0:T(8,128)(2,1)S(1)} %get-tuple-element.22.refs_0_, f32[512,512]{1,0:T(8,128)S(1)} %get-tuple-element.23.refs_1_, f32[512,128]{1,0:T(8,128)S(1)} %get-tuple-element.24.refs_2_, ...), custom_call_target="tpu_custom_call" | custom-call | flops 1275068416 | tf_op jit(solution)/shard_map/pallas_call | solution.py:33
  14.7 1.3 %collective-permute-start.2 = (bf16[512,640]{1,0:T(8,128)(2,1)S(1)}, bf16[512,640]{1,0:T(8,128)(2,1)S(1)}, u32[]{:S(2)}, u32[]{:S(2)}) collective-permute-start(bf16[512,640]{1,0:T(8,128)(2,1)S(1)} %get-tuple-element.29), channel_id=1, source_target_pairs={{1,2},{3,4},{5,6},{7,8},{9,10},{11,12},{13,14},{15,16},{17,18},{19... | collective-permute-start | bytes 1966088 | tf_op jit(solution)/shard_map/ppermute | solution.py:218
  16.0 1.3 %collective-permute-start.3 = (bf16[512,640]{1,0:T(8,128)(2,1)S(1)}, bf16[512,640]{1,0:T(8,128)(2,1)S(1)}, u32[]{:S(2)}, u32[]{:S(2)}) collective-permute-start(bf16[512,640]{1,0:T(8,128)(2,1)S(1)} %get-tuple-element.30.refs_0_.refs_1_), channel_id=1, source_target_pairs={{1,0},{3,2},{5,4},{7,6},{9,8},{11,10},{13,12},{15,14},{17,16},{19,... | collective-permute-start | bytes 1966088 | tf_op jit(solution)/shard_map/ppermute | solution.py:218
  17.3 0.3 collective-permute-done.refs_3_
  17.7 1.3 %collective-permute-start.6 = (bf16[512,640]{1,0:T(8,128)(2,1)S(1)}, bf16[512,640]{1,0:T(8,128)(2,1)S(1)}, u32[]{:S(2)}, u32[]{:S(2)}) collective-permute-start(bf16[512,640]{1,0:T(8,128)(2,1)S(1)} %get-tuple-element.34), channel_id=1, source_target_pairs={{0,1},{2,3},{4,5},{6,7},{8,9},{10,11},{12,13},{14,15},{16,17},{18,... | collective-permute-start | bytes 1966088 | tf_op jit(solution)/shard_map/ppermute | solution.py:218
  19.0 1.3 %collective-permute-start.7 = (bf16[512,640]{1,0:T(8,128)(2,1)S(1)}, bf16[512,640]{1,0:T(8,128)(2,1)S(1)}, u32[]{:S(2)}, u32[]{:S(2)}) collective-permute-start(bf16[512,640]{1,0:T(8,128)(2,1)S(1)} %get-tuple-element.25.refs_3_.refs_0_.refs_1_), channel_id=1, source_target_pairs={{2,1},{4,3},{6,5},{8,7},{10,9},{12,11},{14,13},{16,15},{18,17},{20... | collective-permute-start | bytes 1966088 | tf_op jit(solution)/shard_map/ppermute | solution.py:218
  20.3 4.4 %collective-permute-done.2.refs_3_.refs_4_ = bf16[512,640]{1,0:T(8,128)(2,1)S(1)} collective-permute-done((bf16[512,640]{1,0:T(8,128)(2,1)S(1)}, bf16[512,640]{1,0:T(8,128)(2,1)S(1)}, u32[]{:S(2)}, u32[]{:S(2)}) %collective-permute-start.2) | collective-permute-done | bytes 655392 | tf_op jit(solution)/shard_map/ppermute | solution.py:218
  24.7 0.0 collective-permute-done.3.refs_4_.refs_5_
  24.7 1.3 %collective-permute-start.8 = (bf16[512,128]{1,0:T(8,128)(2,1)S(1)}, bf16[512,128]{1,0:T(8,128)(2,1)S(1)}, u32[]{:S(2)}, u32[]{:S(2)}) collective-permute-start(bf16[512,128]{1,0:T(8,128)(2,1)S(1)} %get-tuple-element.31.refs_0_), channel_id=1, source_target_pairs={{2,1},{4,3},{6,5},{8,7},{10,9},{12,11},{14,13},{16,15},{18,17},{20... | collective-permute-start | bytes 393224 | tf_op jit(solution)/shard_map/ppermute | solution.py:218
  26.0 0.0 collective-permute-done.6.refs_3_.refs_4_
  26.0 10.6 %collective-permute-done.7.refs_4_.refs_5_ = bf16[512,640]{1,0:T(8,128)(2,1)S(1)} collective-permute-done((bf16[512,640]{1,0:T(8,128)(2,1)S(1)}, bf16[512,640]{1,0:T(8,128)(2,1)S(1)}, u32[]{:S(2)}, u32[]{:S(2)}) %collective-permute-start.7) | collective-permute-done | bytes 655392 | tf_op jit(solution)/shard_map/ppermute | solution.py:218
  36.6 1.4 %collective-permute-done.8.refs_5_ = bf16[512,128]{1,0:T(8,128)(2,1)S(1)} collective-permute-done((bf16[512,128]{1,0:T(8,128)(2,1)S(1)}, bf16[512,128]{1,0:T(8,128)(2,1)S(1)}, u32[]{:S(2)}, u32[]{:S(2)}) %collective-permute-start.8) | collective-permute-done | bytes 131104 | tf_op jit(solution)/shard_map/ppermute | solution.py:218
  38.0 2.2 %shard_map.54 = (bf16[512,256]{1,0:T(8,128)(2,1)S(1)}, bf16[512,128]{1,0:T(8,128)(2,1)S(1)}) custom-call(bf16[512,640]{1,0:T(8,128)(2,1)S(1)} %get-tuple-element.30.refs_0_.refs_1_, bf16[512,512]{1,0:T(8,128)(2,1)S(1)} %get-tuple-element.33.refs_1_.refs_2_, bf16[512,512]{1,0:T(8,128)(2,1)S(1)} %get-tuple-element.21.refs_2_.refs_5_.refs_1_.refs_3_.w_b, ...), custom_call_target="tpu_custom_call" | custom-call | flops 603979776 | tf_op jit(solution)/shard_map/pallas_call | solution.py:33
  40.2 1.3 %collective-permute-start.9 = (bf16[512,256]{1,0:T(8,128)(2,1)S(1)}, bf16[512,256]{1,0:T(8,128)(2,1)S(1)}, u32[]{:S(2)}, u32[]{:S(2)}) collective-permute-start(bf16[512,256]{1,0:T(8,128)(2,1)S(1)} %get-tuple-element.35.refs_0_), channel_id=1, source_target_pairs={{1,0},{3,2},{5,4},{7,6},{9,8},{11,10},{13,12},{15,14},{17,16},{19,... | collective-permute-start | bytes 786440 | tf_op jit(solution)/shard_map/ppermute | solution.py:218
  41.5 1.3 %collective-permute-start.4 = (bf16[512,128]{1,0:T(8,128)(2,1)S(1)}, bf16[512,128]{1,0:T(8,128)(2,1)S(1)}, u32[]{:S(2)}, u32[]{:S(2)}) collective-permute-start(bf16[512,128]{1,0:T(8,128)(2,1)S(1)} %get-tuple-element.32), channel_id=1, source_target_pairs={{0,1},{2,3},{4,5},{6,7},{8,9},{10,11},{12,13},{14,15},{16,17},{18,... | collective-permute-start | bytes 393224 | tf_op jit(solution)/shard_map/ppermute | solution.py:218
  42.8 3.6 %collective-permute-start.10 = (bf16[512,128]{1,0:T(8,128)(2,1)S(1)}, bf16[512,128]{1,0:T(8,128)(2,1)S(1)}, u32[]{:S(2)}, u32[]{:S(2)}) collective-permute-start(bf16[512,128]{1,0:T(8,128)(2,1)S(1)} %get-tuple-element.36), channel_id=1, source_target_pairs={{1,2},{3,4},{5,6},{7,8},{9,10},{11,12},{13,14},{15,16},{17,18},{19... | collective-permute-start | bytes 393224 | tf_op jit(solution)/shard_map/ppermute | solution.py:218
  46.3 0.0 collective-permute-done.4.refs_2_
  46.3 0.7 %shard_map.53 = bf16[512,128]{1,0:T(8,128)(2,1)S(1)} custom-call(bf16[512,640]{1,0:T(8,128)(2,1)S(1)} %get-tuple-element.30.refs_0_.refs_1_, bf16[512,512]{1,0:T(8,128)(2,1)S(1)} %get-tuple-element.21.refs_2_.refs_5_.refs_1_.refs_3_.w_b, bf16[512,128]{1,0:T(8,128)(2,1)S(1)} %collective-permute-done.4.refs_2_), custom_call_target="tpu_custom_call" | custom-call | flops 134217728 | tf_op jit(solution)/shard_map/pallas_call | solution.py:33
  47.1 1.3 %collective-permute-start.5 = (bf16[512,128]{1,0:T(8,128)(2,1)S(1)}, bf16[512,128]{1,0:T(8,128)(2,1)S(1)}, u32[]{:S(2)}, u32[]{:S(2)}) collective-permute-start(bf16[512,128]{1,0:T(8,128)(2,1)S(1)} %shard_map.53), channel_id=1, source_target_pairs={{1,2},{3,4},{5,6},{7,8},{9,10},{11,12},{13,14},{15,16},{17,18},{19... | collective-permute-start | bytes 393224 | tf_op jit(solution)/shard_map/ppermute | solution.py:218
  48.4 0.0 collective-permute-done.10.refs_2_
  48.4 1.3 %collective-permute-start.11 = (bf16[512,128]{1,0:T(8,128)(2,1)S(1)}, bf16[512,128]{1,0:T(8,128)(2,1)S(1)}, u32[]{:S(2)}, u32[]{:S(2)}) collective-permute-start(bf16[512,128]{1,0:T(8,128)(2,1)S(1)} %shard_map.56), channel_id=1, source_target_pairs={{0,1},{2,3},{4,5},{6,7},{8,9},{10,11},{12,13},{14,15},{16,17},{18,... | collective-permute-start | bytes 393224 | tf_op jit(solution)/shard_map/ppermute | solution.py:218
  49.7 0.0 collective-permute-done.9.refs_7_.refs_1_
  49.8 1.3 %collective-permute-start.12 = (bf16[512,128]{1,0:T(8,128)(2,1)S(1)}, bf16[512,128]{1,0:T(8,128)(2,1)S(1)}, u32[]{:S(2)}, u32[]{:S(2)}) collective-permute-start(bf16[512,128]{1,0:T(8,128)(2,1)S(1)} %shard_map.57), channel_id=1, source_target_pairs={{2,1},{4,3},{6,5},{8,7},{10,9},{12,11},{14,13},{16,15},{18,17},{20... | collective-permute-start | bytes 393224 | tf_op jit(solution)/shard_map/ppermute | solution.py:218
  51.1 0.0 collective-permute-done.5.refs_6_
  51.1 1.3 %collective-permute-start.14 = (bf16[512,128]{1,0:T(8,128)(2,1)S(1)}, bf16[512,128]{1,0:T(8,128)(2,1)S(1)}, u32[]{:S(2)}, u32[]{:S(2)}) collective-permute-start(bf16[512,128]{1,0:T(8,128)(2,1)S(1)} %shard_map.55.x_even), channel_id=1, source_target_pairs={{2,1},{4,3},{6,5},{8,7},{10,9},{12,11},{14,13},{16,15},{18,17},{20... | collective-permute-start | bytes 393224 | tf_op jit(solution)/shard_map/ppermute | solution.py:218
  52.4 0.6 collective-permute-done.11.refs_6_
  53.0 7.6 %collective-permute-done.12.refs_7_ = bf16[512,128]{1,0:T(8,128)(2,1)S(1)} collective-permute-done((bf16[512,128]{1,0:T(8,128)(2,1)S(1)}, bf16[512,128]{1,0:T(8,128)(2,1)S(1)}, u32[]{:S(2)}, u32[]{:S(2)}) %collective-permute-start.12) | collective-permute-done | bytes 131104 | tf_op jit(solution)/shard_map/ppermute | solution.py:218
  60.6 1.8 %shard_map.58.x_odd = bf16[512,128]{1,0:T(8,128)(2,1)S(1)} custom-call(bf16[512,256]{1,0:T(8,128)(2,1)S(1)} %get-tuple-element.35.refs_0_, bf16[512,640]{1,0:T(8,128)(2,1)S(1)} %get-tuple-element.30.refs_0_.refs_1_, bf16[512,512]{1,0:T(8,128)(2,1)S(1)} %get-tuple-element.33.refs_1_.refs_2_, ...), custom_call_target="tpu_custom_call" | custom-call | flops 469762048 | tf_op jit(solution)/shard_map/pallas_call | solution.py:33
  62.4 1.3 %collective-permute-start.13 = (bf16[512,128]{1,0:T(8,128)(2,1)S(1)}, bf16[512,128]{1,0:T(8,128)(2,1)S(1)}, u32[]{:S(2)}, u32[]{:S(2)}) collective-permute-start(bf16[512,128]{1,0:T(8,128)(2,1)S(1)} %shard_map.58.x_odd), channel_id=1, source_target_pairs={{1,0},{3,2},{5,4},{7,6},{9,8},{11,10},{13,12},{15,14},{17,16},{19,... | collective-permute-start | bytes 393224 | tf_op jit(solution)/shard_map/ppermute | solution.py:218
  63.7 0.0 collective-permute-done.14.x_next_even
  63.7 0.9 %collective-permute-done.13.x_next_odd = bf16[512,128]{1,0:T(8,128)(2,1)S(1)} collective-permute-done((bf16[512,128]{1,0:T(8,128)(2,1)S(1)}, bf16[512,128]{1,0:T(8,128)(2,1)S(1)}, u32[]{:S(2)}, u32[]{:S(2)}) %collective-permute-start.13) | collective-permute-done | bytes 131104 | tf_op jit(solution)/shard_map/ppermute | solution.py:218
  64.7 1.2 %shard_map.59 = bf16[2,512,128]{2,1,0:T(8,128)(2,1)} custom-call(bf16[512,640]{1,0:T(8,128)(2,1)S(1)} %shard_map.47.vg_b, bf16[512,512]{1,0:T(8,128)(2,1)S(1)} %get-tuple-element.21.refs_2_.refs_5_.refs_1_.refs_3_.w_b, bf16[512,128]{1,0:T(8,128)(2,1)S(1)} %shard_map.55.x_even, bf16[512,128]{1,0:T(8,128)(2,1)S(1)} %shard_map.58.x_odd, ...), custom_call_target="tpu_custom_call" | custom-call | flops 134217728 | tf_op jit(solution)/shard_map/pallas_call | solution.py:33
  (6 shorter events, 0.1 us)
Async XLA Ops:
  0.0 1.2 %copy-start = (bf16[2,512,512]{2,1,0:T(8,128)(2,1)S(1)}, bf16[2,512,512]{2,1,0:T(8,128)(2,1)}, u32[]{:S(2)}) copy-start(bf16[2,512,512]{2,1,0:T(8,128)(2,1)} %diag.3) | copy-start | bytes 3145732
  1.2 1.2 %copy-start.1 = (bf16[2,512,512]{2,1,0:T(8,128)(2,1)S(1)}, bf16[2,512,512]{2,1,0:T(8,128)(2,1)}, u32[]{:S(2)}) copy-start(bf16[2,512,512]{2,1,0:T(8,128)(2,1)} %upper.3) | copy-start | bytes 3145732
  2.5 0.9 %copy-start.2 = (bf16[2,512,128]{2,1,0:T(8,128)(2,1)S(1)}, bf16[2,512,128]{2,1,0:T(8,128)(2,1)}, u32[]{:S(2)}) copy-start(bf16[2,512,128]{2,1,0:T(8,128)(2,1)} %right.3) | copy-start | bytes 786436
  4.7 5.5 %copy-start.3 = (bf16[2,512,512]{2,1,0:T(8,128)(2,1)S(1)}, bf16[2,512,512]{2,1,0:T(8,128)(2,1)}, u32[]{:S(2)}) copy-start(bf16[2,512,512]{2,1,0:T(8,128)(2,1)} %lower.1) | copy-start | bytes 3145732
  4.9 8.0 %collective-permute-start.1 = (bf16[512,640]{1,0:T(8,128)(2,1)S(1)}, bf16[512,640]{1,0:T(8,128)(2,1)S(1)}, u32[]{:S(2)}, u32[]{:S(2)}) collective-permute-start(bf16[512,640]{1,0:T(8,128)(2,1)S(1)} %shard_map.47.vg_b), channel_id=1, source_target_pairs={{0,1},{2,3},{4,5},{6,7},{8,9},{10,11},{12,13},{14,15},{16,17},{18,... | collective-permute-start | bytes 1966088 | tf_op jit(solution)/shard_map/ppermute | solution.py:218
  6.4 11.3 %collective-permute-start = (bf16[512,640]{1,0:T(8,128)(2,1)S(1)}, bf16[512,640]{1,0:T(8,128)(2,1)S(1)}, u32[]{:S(2)}, u32[]{:S(2)}) collective-permute-start(bf16[512,640]{1,0:T(8,128)(2,1)S(1)} %shard_map.46.made), channel_id=1, source_target_pairs={{1,2},{3,4},{5,6},{7,8},{9,10},{11,12},{13,14},{15,16},{17,18},{19... | collective-permute-start | bytes 1966088 | tf_op jit(solution)/shard_map/ppermute | solution.py:218
  14.7 10.0 %collective-permute-start.2 = (bf16[512,640]{1,0:T(8,128)(2,1)S(1)}, bf16[512,640]{1,0:T(8,128)(2,1)S(1)}, u32[]{:S(2)}, u32[]{:S(2)}) collective-permute-start(bf16[512,640]{1,0:T(8,128)(2,1)S(1)} %get-tuple-element.29), channel_id=1, source_target_pairs={{1,2},{3,4},{5,6},{7,8},{9,10},{11,12},{13,14},{15,16},{17,18},{19... | collective-permute-start | bytes 1966088 | tf_op jit(solution)/shard_map/ppermute | solution.py:218
  16.0 8.7 %collective-permute-start.3 = (bf16[512,640]{1,0:T(8,128)(2,1)S(1)}, bf16[512,640]{1,0:T(8,128)(2,1)S(1)}, u32[]{:S(2)}, u32[]{:S(2)}) collective-permute-start(bf16[512,640]{1,0:T(8,128)(2,1)S(1)} %get-tuple-element.30.refs_0_.refs_1_), channel_id=1, source_target_pairs={{1,0},{3,2},{5,4},{7,6},{9,8},{11,10},{13,12},{15,14},{17,16},{19,... | collective-permute-start | bytes 1966088 | tf_op jit(solution)/shard_map/ppermute | solution.py:218
  17.7 8.3 %collective-permute-start.6 = (bf16[512,640]{1,0:T(8,128)(2,1)S(1)}, bf16[512,640]{1,0:T(8,128)(2,1)S(1)}, u32[]{:S(2)}, u32[]{:S(2)}) collective-permute-start(bf16[512,640]{1,0:T(8,128)(2,1)S(1)} %get-tuple-element.34), channel_id=1, source_target_pairs={{0,1},{2,3},{4,5},{6,7},{8,9},{10,11},{12,13},{14,15},{16,17},{18,... | collective-permute-start | bytes 1966088 | tf_op jit(solution)/shard_map/ppermute | solution.py:218
  19.0 17.6 %collective-permute-start.7 = (bf16[512,640]{1,0:T(8,128)(2,1)S(1)}, bf16[512,640]{1,0:T(8,128)(2,1)S(1)}, u32[]{:S(2)}, u32[]{:S(2)}) collective-permute-start(bf16[512,640]{1,0:T(8,128)(2,1)S(1)} %get-tuple-element.25.refs_3_.refs_0_.refs_1_), channel_id=1, source_target_pairs={{2,1},{4,3},{6,5},{8,7},{10,9},{12,11},{14,13},{16,15},{18,17},{20... | collective-permute-start | bytes 1966088 | tf_op jit(solution)/shard_map/ppermute | solution.py:218
  24.7 13.3 %collective-permute-start.8 = (bf16[512,128]{1,0:T(8,128)(2,1)S(1)}, bf16[512,128]{1,0:T(8,128)(2,1)S(1)}, u32[]{:S(2)}, u32[]{:S(2)}) collective-permute-start(bf16[512,128]{1,0:T(8,128)(2,1)S(1)} %get-tuple-element.31.refs_0_), channel_id=1, source_target_pairs={{2,1},{4,3},{6,5},{8,7},{10,9},{12,11},{14,13},{16,15},{18,17},{20... | collective-permute-start | bytes 393224 | tf_op jit(solution)/shard_map/ppermute | solution.py:218
  40.2 9.6 %collective-permute-start.9 = (bf16[512,256]{1,0:T(8,128)(2,1)S(1)}, bf16[512,256]{1,0:T(8,128)(2,1)S(1)}, u32[]{:S(2)}, u32[]{:S(2)}) collective-permute-start(bf16[512,256]{1,0:T(8,128)(2,1)S(1)} %get-tuple-element.35.refs_0_), channel_id=1, source_target_pairs={{1,0},{3,2},{5,4},{7,6},{9,8},{11,10},{13,12},{15,14},{17,16},{19,... | collective-permute-start | bytes 786440 | tf_op jit(solution)/shard_map/ppermute | solution.py:218
  41.5 4.9 %collective-permute-start.4 = (bf16[512,128]{1,0:T(8,128)(2,1)S(1)}, bf16[512,128]{1,0:T(8,128)(2,1)S(1)}, u32[]{:S(2)}, u32[]{:S(2)}) collective-permute-start(bf16[512,128]{1,0:T(8,128)(2,1)S(1)} %get-tuple-element.32), channel_id=1, source_target_pairs={{0,1},{2,3},{4,5},{6,7},{8,9},{10,11},{12,13},{14,15},{16,17},{18,... | collective-permute-start | bytes 393224 | tf_op jit(solution)/shard_map/ppermute | solution.py:218
  42.8 5.6 %collective-permute-start.10 = (bf16[512,128]{1,0:T(8,128)(2,1)S(1)}, bf16[512,128]{1,0:T(8,128)(2,1)S(1)}, u32[]{:S(2)}, u32[]{:S(2)}) collective-permute-start(bf16[512,128]{1,0:T(8,128)(2,1)S(1)} %get-tuple-element.36), channel_id=1, source_target_pairs={{1,2},{3,4},{5,6},{7,8},{9,10},{11,12},{13,14},{15,16},{17,18},{19... | collective-permute-start | bytes 393224 | tf_op jit(solution)/shard_map/ppermute | solution.py:218
  47.1 4.0 %collective-permute-start.5 = (bf16[512,128]{1,0:T(8,128)(2,1)S(1)}, bf16[512,128]{1,0:T(8,128)(2,1)S(1)}, u32[]{:S(2)}, u32[]{:S(2)}) collective-permute-start(bf16[512,128]{1,0:T(8,128)(2,1)S(1)} %shard_map.53), channel_id=1, source_target_pairs={{1,2},{3,4},{5,6},{7,8},{9,10},{11,12},{13,14},{15,16},{17,18},{19... | collective-permute-start | bytes 393224 | tf_op jit(solution)/shard_map/ppermute | solution.py:218
  48.4 4.6 %collective-permute-start.11 = (bf16[512,128]{1,0:T(8,128)(2,1)S(1)}, bf16[512,128]{1,0:T(8,128)(2,1)S(1)}, u32[]{:S(2)}, u32[]{:S(2)}) collective-permute-start(bf16[512,128]{1,0:T(8,128)(2,1)S(1)} %shard_map.56), channel_id=1, source_target_pairs={{0,1},{2,3},{4,5},{6,7},{8,9},{10,11},{12,13},{14,15},{16,17},{18,... | collective-permute-start | bytes 393224 | tf_op jit(solution)/shard_map/ppermute | solution.py:218
  49.8 10.8 %collective-permute-start.12 = (bf16[512,128]{1,0:T(8,128)(2,1)S(1)}, bf16[512,128]{1,0:T(8,128)(2,1)S(1)}, u32[]{:S(2)}, u32[]{:S(2)}) collective-permute-start(bf16[512,128]{1,0:T(8,128)(2,1)S(1)} %shard_map.57), channel_id=1, source_target_pairs={{2,1},{4,3},{6,5},{8,7},{10,9},{12,11},{14,13},{16,15},{18,17},{20... | collective-permute-start | bytes 393224 | tf_op jit(solution)/shard_map/ppermute | solution.py:218
  51.1 12.6 %collective-permute-start.14 = (bf16[512,128]{1,0:T(8,128)(2,1)S(1)}, bf16[512,128]{1,0:T(8,128)(2,1)S(1)}, u32[]{:S(2)}, u32[]{:S(2)}) collective-permute-start(bf16[512,128]{1,0:T(8,128)(2,1)S(1)} %shard_map.55.x_even), channel_id=1, source_target_pairs={{2,1},{4,3},{6,5},{8,7},{10,9},{12,11},{14,13},{16,15},{18,17},{20... | collective-permute-start | bytes 393224 | tf_op jit(solution)/shard_map/ppermute | solution.py:218
  62.4 2.3 %collective-permute-start.13 = (bf16[512,128]{1,0:T(8,128)(2,1)S(1)}, bf16[512,128]{1,0:T(8,128)(2,1)S(1)}, u32[]{:S(2)}, u32[]{:S(2)}) collective-permute-start(bf16[512,128]{1,0:T(8,128)(2,1)S(1)} %shard_map.58.x_odd), channel_id=1, source_target_pairs={{1,0},{3,2},{5,4},{7,6},{9,8},{11,10},{13,12},{15,14},{17,16},{19,... | collective-permute-start | bytes 393224 | tf_op jit(solution)/shard_map/ppermute | solution.py:218

commit v2 on v0

v2 whole, which is shorter than its diff:
```python
import functools

import jax
import jax.numpy as jnp
from jax import lax
from jax.experimental import pallas as pl
from jax.experimental.pallas import tpu as pltpu
from jax.sharding import PartitionSpec as P


AXES = ("grp", "dev")
BF16 = jnp.bfloat16
F32 = jnp.float32
VMEM_BYTES = 16 * 1024 * 1024


def is_odd():
    return lax.rem(lax.axis_index(AXES), 2) == 1


def if_left(value):
    return jnp.where(lax.axis_index(AXES) > 0, value, jnp.zeros_like(value))


def if_right(value):
    last = lax.axis_size(AXES) - 1
    return jnp.where(lax.axis_index(AXES) < last, value, jnp.zeros_like(value))


def dot(a, b):
    return jnp.dot(a, b, preferred_element_type=F32)


def by_parity(even, odd):
    odd_here = is_odd()
    if odd is not None:
        pl.when(odd_here)(odd)
    if even is not None:
        pl.when(jnp.logical_not(odd_here))(even)


def identity(order):
    rows = lax.broadcasted_iota(jnp.int32, (order, order), 0)
    return (rows == lax.broadcasted_iota(jnp.int32, (order, order), 1)).astype(F32)


def local_call(kernel, outs, ins, flops, in_hbm=0, scratch=(), aliases=None):
    vmem = pl.BlockSpec(memory_space=pltpu.VMEM)
    hbm = pl.BlockSpec(memory_space=pl.ANY)
    many = len(outs) > 1
    ins = [pltpu.with_memory_space_constraint(x, pltpu.HBM) for x in ins[:in_hbm]] + ins[in_hbm:]
    return pl.pallas_call(
        kernel,
        out_shape=outs if many else outs[0],
        in_specs=[hbm] * in_hbm + [vmem] * (len(ins) - in_hbm),
        out_specs=[vmem] * len(outs) if many else vmem,
        scratch_shapes=list(scratch),
        input_output_aliases=aliases or {},
        compiler_params=pltpu.CompilerParams(vmem_limit_bytes=VMEM_BYTES),
        cost_estimate=pl.CostEstimate(flops=flops // 1000, bytes_accessed=0, transcendentals=0),
    )(*ins)


def bf16_array(rows, columns):
    return jax.ShapeDtypeStruct((rows, columns), BF16)


def f32_array(rows, columns):
    return jax.ShapeDtypeStruct((rows, columns), F32)


def fetch(source, target, sem):
    copy = pltpu.make_async_copy(source, target, sem)
    copy.start()
    return copy


def load_row(order, diag, upper, right, vg, diag_b, upper_b, right_b, sems):
    d_b = fetch(diag.at[1], diag_b, sems.at[0])
    u_b = fetch(upper.at[1], upper_b, sems.at[1])
    r_b = fetch(right.at[1], right_b, sems.at[2])
    d_b.wait()
    u_b.wait()
    vg[:, :order] = dot(diag_b[...], upper_b[...]).astype(BF16)
    r_b.wait()
    vg[:, order:] = dot(diag_b[...], right_b[...]).astype(BF16)


def second_row_odd(order, *refs):
    by_parity(None, lambda: load_row(order, *refs))


def second_row(order, diag, upper, right, vg_odd, vg_b, *rest):
    *pieces, diag_b, upper_b, right_b, sems = rest

    def odd():
        vg_b[...] = vg_odd[...]

    def even():
        load_row(order, diag, upper, right, vg_b, diag_b, upper_b, right_b, sems)
        first = 0
        for piece in pieces:
            piece[...] = vg_b[:, first : first + piece.shape[1]]
            first += piece.shape[1]

    by_parity(even, odd)


def own_products(
    order, diag, lower, upper, right, vg_b, w_a, w_b, m, n, r,
    diag_a, lower_a, upper_a, right_a, diag_b, lower_b, sems,
):
    d_a = fetch(diag.at[0], diag_a, sems.at[0])
    u_a = fetch(upper.at[0], upper_a, sems.at[1])
    d_b = fetch(diag.at[1], diag_b, sems.at[2])
    l_b = fetch(lower.at[1], lower_b, sems.at[3])
    l_a = fetch(lower.at[0], lower_a, sems.at[4])
    r_a = fetch(right.at[0], right_a, sems.at[5])
    d_a.wait()
    u_a.wait()
    v_a = dot(diag_a[...], upper_a[...]).astype(BF16)
    d_b.wait()
    l_b.wait()
    w_b[...] = dot(diag_b[...], lower_b[...]).astype(BF16)
    l_a.wait()
    w_a[...] = dot(diag_a[...], lower_a[...]).astype(BF16)
    r_a.wait()
    g_a = dot(diag_a[...], right_a[...]).astype(BF16)
    n[...] = dot(v_a, vg_b[:, :order]).astype(BF16)
    r[...] = g_a.astype(F32) - dot(v_a, vg_b[:, order:])
    m[...] = dot(v_a, w_b[...])


def scale_one(order, w_a, m, r, v_left, g_left, scale, tg):
    first = 0
    eye = identity(order)
    for piece in v_left:
        at = slice(first, first + piece.shape[1])
        coupling = if_left(dot(w_a[...], piece[...])) + m[:, at]
        scale[:, at] = (eye[:, at] + coupling).astype(BF16)
        first = at.stop
    rest = (r[...] - if_left(dot(w_a[...], g_left[...]))).astype(BF16)
    tg[:, :order] = dot(scale[...], w_a[...]).astype(BF16)
    tg[:, order:] = dot(scale[...], rest).astype(BF16)


def spikes_one(scale, n, w_b, g_one, v_one, w_v, w_g):
    v_one[...] = (-dot(scale[...], n[...])).astype(BF16)
    columns = v_one.shape[1] // len(w_v)
    for i, piece in enumerate(w_v):
        piece[...] = dot(w_b[...], v_one[:, i * columns : (i + 1) * columns]).astype(BF16)
    w_g[...] = dot(w_b[...], g_one[...]).astype(BF16)


def level_one_odd(order, w_a, m, r, v0, vg1, n, w_b, tg, v_one, w_vg, scale):
    columns = order - v0.shape[1]

    def odd():
        v_left, g_left = [v0, vg1.at[:, :columns]], vg1.at[:, columns:]
        scale_one(order, w_a, m, r, v_left, g_left, scale, tg)
        spikes_one(
            scale, n, w_b, tg.at[:, order:], v_one, [w_vg.at[:, :order]], w_vg.at[:, order:]
        )

    by_parity(None, odd)


def scale_one_even(order, w_a, m, r, vg, tg_odd, tg, scale):
    v_left, g_left = [vg.at[:, :order]], vg.at[:, order:]
    by_parity(lambda: scale_one(order, w_a, m, r, v_left, g_left, scale, tg), None)


def spikes_one_even(order, scale, n, w_b, tg, v_odd, v_one, to_pair0, to_pair1, to_pair2):
    def odd():
        to_pair0[...] = tg[:, : order // 2]
        to_pair1[...] = tg[:, order // 2 : order]
        to_pair2[...] = tg[:, order:]

    by_parity(
        lambda: spikes_one(
            scale, n, w_b, tg.at[:, order:], v_one, [to_pair0, to_pair1], to_pair2
        ),
        odd,
    )


def same(value):
    return value


def left_part(order, tg, w_v_left, w_g_left, left_on, left, h):
    t = tg[:, :order]
    columns = left.shape[1] // len(w_v_left)
    for i, piece in enumerate(w_v_left):
        left[:, i * columns : (i + 1) * columns] = left_on(dot(t, piece[...])).astype(BF16)
    h[...] = tg[:, order:].astype(F32) + left_on(dot(t, w_g_left[...]))


def left_part_all(order, tg, w_vg_gap, pair0, pair1, pair2, left, h):
    by_parity(
        lambda: left_part(
            order, tg, [w_vg_gap.at[:, :order]], w_vg_gap.at[:, order:], if_left, left, h
        ),
        lambda: left_part(order, tg, [pair0, pair1], pair2, same, left, h),
    )


def times(pieces, block):
    depth = block.shape[0] // len(pieces)
    return sum(dot(piece[...], block[i * depth : (i + 1) * depth]) for i, piece in enumerate(pieces))


def level_two(v_one, w_b, left, h_left, t_right, g_right, right_on, g, w_g):
    h = h_left[...] - right_on(dot(v_one[...], g_right[...]))
    h16 = h.astype(BF16)
    own = dot(w_b[...], h16).astype(BF16)
    from_right = right_on(dot(v_one[...], times(t_right, own).astype(BF16)))
    g[...] = (h - dot(left[...], h16) - from_right).astype(BF16)
    w_g[...] = dot(w_b[...], g[...]).astype(BF16)


def level_two_all(order, v_one, w_b, left, h_left, tg_gap, pair0, pair1, pair2, y_pair, y_gap):
    own = v_one, w_b, left, h_left
    t_gap, g_gap = [tg_gap.at[:, :order]], tg_gap.at[:, order:]
    by_parity(
        lambda: level_two(*own, [pair0, pair1], pair2, same, y_gap, y_pair),
        lambda: level_two(*own, t_gap, g_gap, if_right, y_pair, y_gap),
    )


def spikes_two(order, tg, v_one, w_b, left, t_right, right_on, s_t, s_v, scale):
    right = times(t_right, w_b[...]).astype(BF16)
    coupling = left[...].astype(F32) + right_on(dot(v_one[...], right))
    scale[...] = (identity(order) - coupling).astype(BF16)
    s_t[...] = if_left(dot(scale[...], tg[:, :order])).astype(BF16)
    s_v[...] = if_right(dot(scale[...], v_one[...])).astype(BF16)


def spikes_two_all(
    order, tg, v_one, w_b, left, tg_gap, pair0, pair1, after, s_t, s_v, scale
):
    own = order, tg, v_one, w_b, left
    by_parity(
        lambda: spikes_two(*own, [pair0, pair1], same, s_t, s_v, scale),
        lambda: spikes_two(*own, [tg_gap.at[:, :order]], if_right, s_t, s_v, scale),
    )


def passed_right(tg, w_b, from_left, out):
    own = if_left(-dot(tg[:, : tg.shape[0]], from_left[...])).astype(BF16)
    out[...] = dot(w_b[...], own).astype(BF16)


def passed_left(v_one, from_right, out):
    out[...] = if_right(dot(v_one[...], from_right[...])).astype(BF16)


def pass_on_pair(tg, v_one, w_b, got, out):
    by_parity(
        lambda: passed_left(v_one, got, out), lambda: passed_right(tg, w_b, got, out)
    )


def pass_on_gap(tg, v_one, w_b, from_left, from_right, after, out):
    by_parity(
        lambda: passed_right(tg, w_b, from_left, out), lambda: passed_left(v_one, from_right, out)
    )


def top_values(y_pair, y_gap, s_t, s_v, from_pair, from_left, from_right, x):
    def top(g, p, q):
        x[...] = (g[...].astype(F32) + dot(s_v[...], q[...]) - dot(s_t[...], p[...])).astype(BF16)

    by_parity(lambda: top(y_gap, from_left, from_pair), lambda: top(y_pair, from_pair, from_right))


def start_second(order, vg_b, w_b, x, rest):
    rest[...] = vg_b[:, order:].astype(F32) - dot(w_b[...], x[...])


def finish(order, vg_b, x, rest, x_pair, x_gap, out):
    def rows(x_next):
        out[0] = x[...]
        out[1] = (rest[...] - if_right(dot(vg_b[:, :order], x_next[...]))).astype(BF16)

    by_parity(lambda: rows(x_pair), lambda: rows(x_gap))


def exchanges(slab, count):
    pairs = [(i, i ^ 1) for i in range(count)]
    after = [(i + 1) % count for i in range(count)]
    after[2], after[slab + 2], after[count - 1] = 0, 3, count - 5
    for first in range(slab + 3, count - 5, 4):
        after[first + 3] = first
    to_right = list(enumerate(after))
    to_left = [(count - 1 - i, count - 1 - j) for i, j in to_right]
    return pairs, to_right, to_left


def body(diag, lower, upper, right):
    order, rhs = diag.shape[1], right.shape[2]
    count = lax.axis_size(AXES)
    pairs, to_right, to_left = exchanges(lax.axis_size("dev"), count)

    def sent(block, route):
        return lax.ppermute(block, AXES, route)

    part = functools.partial
    square = 2 * order**3
    thin = 2 * order * order * rhs
    block = pltpu.VMEM((order, order), BF16)
    side = pltpu.VMEM((order, rhs), BF16)
    wide = bf16_array(order, order + rhs)
    full = bf16_array(order, order)
    slim = bf16_array(order, rhs)

    row_scratch = (block, block, side, pltpu.SemaphoreType.DMA((3,)))
    vg_odd = local_call(
        part(second_row_odd, order), [wide], [diag, upper, right], square + thin, 3, row_scratch
    )
    vg_gap = sent(vg_odd, to_right)
    cut = 3 * order // 4
    vg_b, *to_pair = local_call(
        part(second_row, order),
        [wide, bf16_array(order, cut), bf16_array(order, order - cut + rhs)],
        [diag, upper, right, vg_odd], square + thin, 3, row_scratch,
    )
    vg_pair = [sent(piece, pairs) for piece in to_pair]
    w_a, w_b, m, n, r = local_call(
        part(own_products, order),
        [full, full, f32_array(order, order), full, f32_array(order, rhs)],
        [diag, lower, upper, right, vg_b], 5 * square + 2 * thin, 4,
        (block, block, block, side, block, block, pltpu.SemaphoreType.DMA((6,))),
    )

    tg_odd, v_odd, w_vg_odd = local_call(
        part(level_one_odd, order),
        [wide, full, wide], [w_a, m, r, *vg_pair, n, w_b], 4 * square + 3 * thin, 0, (block,),
    )
    w_vg_gap = sent(w_vg_odd, to_right)
    tg, scale = local_call(
        part(scale_one_even, order),
        [wide, full], [w_a, m, r, vg_gap, tg_odd], 2 * square + 2 * thin, aliases={4: 0},
    )
    tg_gap = sent(tg, to_left)
    half = bf16_array(order, order // 2)
    v_one, *to_pair = local_call(
        part(spikes_one_even, order),
        [full, half, half, slim], [scale, n, w_b, tg, v_odd], 2 * square + thin, aliases={4: 0},
    )
    pair = [sent(piece, pairs) for piece in to_pair]

    left, h_left = local_call(
        part(left_part_all, order),
        [full, f32_array(order, rhs)], [tg, w_vg_gap, *pair], square + thin,
    )
    y_pair, y_gap = local_call(
        part(level_two_all, order),
        [slim, slim], [v_one, w_b, left, h_left, tg_gap, *pair], 6 * thin,
    )
    got_pair = sent(y_pair, pairs)
    got_gap = [sent(y_gap, to_right), sent(y_gap, to_left)]
    on_gap = local_call(
        pass_on_pair, [slim], [tg, v_one, w_b, got_pair], 2 * thin
    )
    from_gap = [sent(on_gap, to_right), sent(on_gap, to_left)]
    s_t, s_v = local_call(
        part(spikes_two_all, order),
        [full, full], [tg, v_one, w_b, left, tg_gap, *pair[:2], on_gap], 4 * square, 0, (block,),
    )
    on_pair = local_call(
        pass_on_gap, [slim], [tg, v_one, w_b, *got_gap, s_t], 2 * thin
    )
    from_pair = sent(on_pair, pairs)
    x = local_call(
        top_values, [slim], [y_pair, y_gap, s_t, s_v, from_pair, *from_gap], 2 * thin
    )
    x_pair, x_gap = sent(x, pairs), sent(x, to_left)
    rest = local_call(part(start_second, order), [f32_array(order, rhs)], [vg_b, w_b, x], thin)
    return local_call(
        part(finish, order),
        [jax.ShapeDtypeStruct((2, order, rhs), BF16)], [vg_b, x, rest, x_pair, x_gap], thin,
    )


def solution(mesh):
    split = P(AXES, None, None)
    return jax.shard_map(
        body, mesh=mesh, in_specs=(split,) * 4, out_specs=split, check_vma=False
    )
```

time: 92.1 us -> 53.7 us (0.58)
  starting transfers between devices: 34.5 us -> 19.1 us
  Pallas kernels: 0 us -> 14.5 us
  waiting for transfers between devices: 31.4 us -> 19.7 us
  local copies, waits for them, and re-layouts: 11.2 us -> 0 us
  matrix products: 10.7 us -> 0 us
  other arithmetic: 3.64 us -> 0 us
    ppermute x6 -> x16, starting transfers between devices: 34.5 us -> 19.1 us  [sent(): return lax.ppermute(block, AXES, route)]
    pallas_call x0 -> x14, Pallas kernels: none -> 14.5 us  [local_call(): pl.pallas_call(kernel, out_shape=outs if many else outs[0], in_specs=[hbm...]
    ppermute x6 -> x16, waiting for transfers between devices: 31.4 us -> 19.7 us  [sent(): return lax.ppermute(block, AXES, route)]
    dot_general x12 -> x0, matrix products: 10.7 us -> none  [the longest x2 3.23 us: reduce_panel(): jnp.dot(scaling, combined, preferred_element_type=jnp.float32)]
    unnamed x8 -> x0, local copies, waits for them, and re-layouts: 4.51 us -> none
    squeeze x2 -> x0, local copies, waits for them, and re-layouts: 2.73 us -> none  [the longest x1 1.74 us: make_panels(): upper_block[row]]
    convert_element_type x2 -> x0, other arithmetic: 1.81 us -> none  [reduce_panel(): remaining = (own_rhs.astype(jnp.float32) - from_left[:, 2 * order:] - fro...]
    neg x4 -> x0, other arithmetic: 1.8 us -> none  [reduce_panel(): combined = jnp.concatenate([-outer_left, -outer_right, remaining], axis=1)]
  transfers between devices with their start and end apart: 6 -> 16, of which waited for: 6 -> 6; matrix products, arithmetic and copies ran while one was open for 7% -> 0% of each run, Pallas kernels for 0% -> 17%
where the time goes in v2:
time: 53.7 us; the launch traced here: 53.5 us
  waiting for transfers between devices  19.7 us (37%)
  starting transfers between devices  19.1 us (36%)
  Pallas kernels  14.5 us (27%)
    ppermute x16, waiting for transfers between devices, sent(): return lax.ppermute(block, AXES, route)  19.7 us
    ppermute x16, starting transfers between devices, sent(): return lax.ppermute(block, AXES, route)  19.1 us
    pallas_call x14, Pallas kernels, local_call(): pl.pallas_call(kernel, out_shape=outs if many else outs[0], in_specs=[hbm...  14.5 us
  transfers between devices with their start and end apart: 16, of which 6 were waited for; matrix products, arithmetic and copies ran while one was open for 0% of the time, Pallas kernels for 17%

profile of v2, /device:TPU:29, one launch (start us, length us, event | category | flops | bytes accessed | tf_op | source)
XLA Modules:
  0.0 53.5 jit_solution(11204236601056548075)
XLA Ops:
  0.0 2.2 %shard_map.46.vg_odd = bf16[512,640]{1,0:T(8,128)(2,1)S(1)} custom-call(bf16[2,512,512]{2,1,0:T(8,128)(2,1)} %diag.3, bf16[2,512,512]{2,1,0:T(8,128)(2,1)} %upper.3, bf16[2,512,128]{2,1,0:T(8,128)(2,1)} %right.3), custom_call_target="tpu_custom_call" | custom-call | flops 335544 | tf_op jit(solution)/shard_map/pallas_call | solution.py:52
  2.2 0.1 collective-permute-start
  2.3 0.1 shard_map.47
  2.4 2.8 %collective-permute-start.1 = (bf16[512,384]{1,0:T(8,128)(2,1)S(1)}, bf16[512,384]{1,0:T(8,128)(2,1)S(1)}, u32[]{:S(2)}, u32[]{:S(2)}) collective-permute-start(bf16[512,384]{1,0:T(8,128)(2,1)S(1)} %get-tuple-element.32), channel_id=1, source_target_pairs={{0,1},{1,0},{2,3},{3,2},{4,5},{5,4},{6,7},{7,6},{8,9},{9,8},{10,11... | collective-permute-start | bytes 1179656 | tf_op jit(solution)/shard_map/ppermute | solution.py:306
  5.2 0.1 collective-permute-start.2
  5.3 3.6 %shard_map.48 = (bf16[512,512]{1,0:T(8,128)(2,1)S(1)}, bf16[512,512]{1,0:T(8,128)(2,1)S(1)}, f32[512,512]{1,0:T(8,128)S(1)}, bf16[512,512]{1,0:T(8,128)(2,1)S(1)}, f32[512,128]{1,0:T(8,128)S(1)}) custom-call(bf16[2,512,512]{2,1,0:T(8,128)(2,1)} %diag.3, bf16[2,512,512]{2,1,0:T(8,128)(2,1)} %lower.1, bf16[2,512,512]{2,1,0:T(8,128)(2,1)} %upper.3, ...), custom_call_target="tpu_custom_call" | custom-call | flops 1476395 | tf_op jit(solution)/shard_map/pallas_call | solution.py:52
  8.8 0.0 collective-permute-done.2.vg1
  8.8 0.0 collective-permute-done.1.v0
  8.8 1.9 %shard_map.49 = (bf16[512,640]{1,0:T(8,128)(2,1)S(1)}, bf16[512,512]{1,0:T(8,128)(2,1)S(1)}, bf16[512,640]{1,0:T(8,128)(2,1)S(1)}) custom-call(bf16[512,512]{1,0:T(8,128)(2,1)S(1)} %get-tuple-element.29.w_a, f32[512,512]{1,0:T(8,128)S(1)} %get-tuple-element.30.m, f32[512,128]{1,0:T(8,128)S(1)} %get-tuple-element.31.r, ...), custom_call_target="tpu_custom_call" | custom-call | flops 1275068 | tf_op jit(solution)/shard_map/pallas_call | solution.py:52
  10.7 0.1 collective-permute-start.3
  10.8 0.0 collective-permute-done.vg
  10.8 1.5 %collective-permute-start.7 = (bf16[512,640]{1,0:T(8,128)(2,1)S(1)}, bf16[512,640]{1,0:T(8,128)(2,1)S(1)}, u32[]{:S(2)}, u32[]{:S(2)}) collective-permute-start(bf16[512,640]{1,0:T(8,128)(2,1)S(1)} %get-tuple-element.38.tg), channel_id=1, source_target_pairs={{31,30},{30,29},{29,31},{28,27},{27,26},{26,25},{25,24},{24,23},{2... | collective-permute-start | bytes 1966088 | tf_op jit(solution)/shard_map/ppermute | solution.py:306
  12.4 0.1 shard_map.51
  12.4 0.9 %collective-permute-start.4 = (bf16[512,256]{1,0:T(8,128)(2,1)S(1)}, bf16[512,256]{1,0:T(8,128)(2,1)S(1)}, u32[]{:S(2)}, u32[]{:S(2)}) collective-permute-start(bf16[512,256]{1,0:T(8,128)(2,1)S(1)} %get-tuple-element.42), channel_id=1, source_target_pairs={{0,1},{1,0},{2,3},{3,2},{4,5},{5,4},{6,7},{7,6},{8,9},{9,8},{10,11... | collective-permute-start | bytes 786440 | tf_op jit(solution)/shard_map/ppermute | solution.py:306
  13.4 0.1 collective-permute-start.5
  13.5 0.4 collective-permute-start.6
  13.9 1.2 %collective-permute-done.6.pair2 = bf16[512,128]{1,0:T(8,128)(2,1)S(1)} collective-permute-done((bf16[512,128]{1,0:T(8,128)(2,1)S(1)}, bf16[512,128]{1,0:T(8,128)(2,1)S(1)}, u32[]{:S(2)}, u32[]{:S(2)}) %collective-permute-start.6) | collective-permute-done | bytes 131104 | tf_op jit(solution)/shard_map/ppermute | solution.py:306
  15.1 0.0 collective-permute-done.4.pair0
  15.1 0.0 collective-permute-done.5.pair1
  15.1 3.2 %collective-permute-done.3.w_vg_gap = bf16[512,640]{1,0:T(8,128)(2,1)S(1)} collective-permute-done((bf16[512,640]{1,0:T(8,128)(2,1)S(1)}, bf16[512,640]{1,0:T(8,128)(2,1)S(1)}, u32[]{:S(2)}, u32[]{:S(2)}) %collective-permute-start.3) | collective-permute-done | bytes 655392 | tf_op jit(solution)/shard_map/ppermute | solution.py:306
  18.3 0.6 %shard_map.52 = (bf16[512,512]{1,0:T(8,128)(2,1)S(1)}, f32[512,128]{1,0:T(8,128)S(1)}) custom-call(bf16[512,640]{1,0:T(8,128)(2,1)S(1)} %get-tuple-element.38.tg, bf16[512,640]{1,0:T(8,128)(2,1)S(1)} %collective-permute-done.3.w_vg_gap, bf16[512,256]{1,0:T(8,128)(2,1)S(1)} %collective-permute-done.4.pair0, ...), custom_call_target="tpu_custom_call" | custom-call | flops 335544 | tf_op jit(solution)/shard_map/pallas_call | solution.py:52
  18.9 6.5 %collective-permute-done.7.tg_gap = bf16[512,640]{1,0:T(8,128)(2,1)S(1)} collective-permute-done((bf16[512,640]{1,0:T(8,128)(2,1)S(1)}, bf16[512,640]{1,0:T(8,128)(2,1)S(1)}, u32[]{:S(2)}, u32[]{:S(2)}) %collective-permute-start.7) | collective-permute-done | bytes 655392 | tf_op jit(solution)/shard_map/ppermute | solution.py:306
  25.4 1.7 %shard_map.53 = (bf16[512,128]{1,0:T(8,128)(2,1)S(1)}, bf16[512,128]{1,0:T(8,128)(2,1)S(1)}) custom-call(bf16[512,512]{1,0:T(8,128)(2,1)S(1)} %get-tuple-element.40.v_one, bf16[512,512]{1,0:T(8,128)(2,1)S(1)} %get-tuple-element.35.w_b, bf16[512,512]{1,0:T(8,128)(2,1)S(1)} %get-tuple-element.45.left, f32[512,128]{1,0:T(8,128)S(1)} %get-tuple-element.46.h_left, ...), custom_call_target="tpu_custom_call" | custom-call | flops 402653 | tf_op jit(solution)/shard_map/pallas_call | solution.py:52
  27.1 2.1 %collective-permute-start.8 = (bf16[512,128]{1,0:T(8,128)(2,1)S(1)}, bf16[512,128]{1,0:T(8,128)(2,1)S(1)}, u32[]{:S(2)}, u32[]{:S(2)}) collective-permute-start(bf16[512,128]{1,0:T(8,128)(2,1)S(1)} %get-tuple-element.47.y_pair), channel_id=1, source_target_pairs={{0,1},{1,0},{2,3},{3,2},{4,5},{5,4},{6,7},{7,6},{8,9},{9,8},{10,11... | collective-permute-start | bytes 393224 | tf_op jit(solution)/shard_map/ppermute | solution.py:306
  29.2 0.1 collective-permute-start.10
  29.2 5.3 %collective-permute-start.9 = (bf16[512,128]{1,0:T(8,128)(2,1)S(1)}, bf16[512,128]{1,0:T(8,128)(2,1)S(1)}, u32[]{:S(2)}, u32[]{:S(2)}) collective-permute-start(bf16[512,128]{1,0:T(8,128)(2,1)S(1)} %get-tuple-element.48.y_gap), channel_id=1, source_target_pairs={{0,1},{1,2},{2,0},{3,4},{4,5},{5,6},{6,7},{7,8},{8,9},{9,10},{10,1... | collective-permute-start | bytes 393224 | tf_op jit(solution)/shard_map/ppermute | solution.py:306
  34.5 0.0 collective-permute-done.8.got
  34.5 0.7 %shard_map.54.after = bf16[512,128]{1,0:T(8,128)(2,1)S(1)} custom-call(bf16[512,640]{1,0:T(8,128)(2,1)S(1)} %get-tuple-element.38.tg, bf16[512,512]{1,0:T(8,128)(2,1)S(1)} %get-tuple-element.40.v_one, bf16[512,512]{1,0:T(8,128)(2,1)S(1)} %get-tuple-element.35.w_b, bf16[512,128]{1,0:T(8,128)(2,1)S(1)} %collective-permute-done.8.got), custom_call_target="tpu_custom_call" | custom-call | flops 134217 | tf_op jit(solution)/shard_map/pallas_call | solution.py:52
  35.3 0.1 collective-permute-start.13
  35.3 5.3 %collective-permute-start.12 = (bf16[512,128]{1,0:T(8,128)(2,1)S(1)}, bf16[512,128]{1,0:T(8,128)(2,1)S(1)}, u32[]{:S(2)}, u32[]{:S(2)}) collective-permute-start(bf16[512,128]{1,0:T(8,128)(2,1)S(1)} %shard_map.54.after), channel_id=1, source_target_pairs={{0,1},{1,2},{2,0},{3,4},{4,5},{5,6},{6,7},{7,8},{8,9},{9,10},{10,1... | collective-permute-start | bytes 393224 | tf_op jit(solution)/shard_map/ppermute | solution.py:306
  40.7 1.6 %shard_map.55 = (bf16[512,512]{1,0:T(8,128)(2,1)S(1)}, bf16[512,512]{1,0:T(8,128)(2,1)S(1)}) custom-call(bf16[512,640]{1,0:T(8,128)(2,1)S(1)} %get-tuple-element.38.tg, bf16[512,512]{1,0:T(8,128)(2,1)S(1)} %get-tuple-element.40.v_one, bf16[512,512]{1,0:T(8,128)(2,1)S(1)} %get-tuple-element.35.w_b, bf16[512,512]{1,0:T(8,128)(2,1)S(1)} %get-tuple-element.45.left, ...), custom_call_target="tpu_custom_call" | custom-call | flops 1073741 | tf_op jit(solution)/shard_map/pallas_call | solution.py:52
  42.2 0.0 collective-permute-done.10.from_right
  42.3 0.0 collective-permute-done.9.from_left
  42.3 0.3 shard_map.56
  42.6 0.1 collective-permute-start.11
  42.7 0.7 %collective-permute-done.13.from_right = bf16[512,128]{1,0:T(8,128)(2,1)S(1)} collective-permute-done((bf16[512,128]{1,0:T(8,128)(2,1)S(1)}, bf16[512,128]{1,0:T(8,128)(2,1)S(1)}, u32[]{:S(2)}, u32[]{:S(2)}) %collective-permute-start.13) | collective-permute-done | bytes 131104 | tf_op jit(solution)/shard_map/ppermute | solution.py:306
  43.3 0.0 collective-permute-done.12.from_left
  43.3 0.7 %collective-permute-done.11.from_pair = bf16[512,128]{1,0:T(8,128)(2,1)S(1)} collective-permute-done((bf16[512,128]{1,0:T(8,128)(2,1)S(1)}, bf16[512,128]{1,0:T(8,128)(2,1)S(1)}, u32[]{:S(2)}, u32[]{:S(2)}) %collective-permute-start.11) | collective-permute-done | bytes 131104 | tf_op jit(solution)/shard_map/ppermute | solution.py:306
  44.0 0.4 shard_map.57.x
  44.4 0.2 collective-permute-start.15
  44.6 0.1 collective-permute-start.14
  44.7 0.3 shard_map.58.rest
  45.0 7.5 %collective-permute-done.15.x_gap = bf16[512,128]{1,0:T(8,128)(2,1)S(1)} collective-permute-done((bf16[512,128]{1,0:T(8,128)(2,1)S(1)}, bf16[512,128]{1,0:T(8,128)(2,1)S(1)}, u32[]{:S(2)}, u32[]{:S(2)}) %collective-permute-start.15) | collective-permute-done | bytes 131104 | tf_op jit(solution)/shard_map/ppermute | solution.py:306
  52.5 0.0 collective-permute-done.14.x_pair
  52.5 1.0 %shard_map.59 = bf16[2,512,128]{2,1,0:T(8,128)(2,1)} custom-call(bf16[512,640]{1,0:T(8,128)(2,1)S(1)} %get-tuple-element.28.vg_b, bf16[512,128]{1,0:T(8,128)(2,1)S(1)} %shard_map.57.x, f32[512,128]{1,0:T(8,128)S(1)} %shard_map.58.rest, bf16[512,128]{1,0:T(8,128)(2,1)S(1)} %collective-permute-done.14.x_pair, bf16[512,128]{1,0:T(8,128)(2,1)S(1)} %collective-permute-done.15.x_gap), custom_call_target="tpu_custom_call" | custom-call | flops 67108 | tf_op jit(solution)/shard_map/pallas_call | solution.py:52
  (1 shorter events, 0.0 us)
Async XLA Ops:
  2.2 8.6 %collective-permute-start = (bf16[512,640]{1,0:T(8,128)(2,1)S(1)}, bf16[512,640]{1,0:T(8,128)(2,1)S(1)}, u32[]{:S(2)}, u32[]{:S(2)}) collective-permute-start(bf16[512,640]{1,0:T(8,128)(2,1)S(1)} %shard_map.46.vg_odd), channel_id=1, source_target_pairs={{0,1},{1,2},{2,0},{3,4},{4,5},{5,6},{6,7},{7,8},{8,9},{9,10},{10,1... | collective-permute-start | bytes 1966088 | tf_op jit(solution)/shard_map/ppermute | solution.py:306
  2.4 6.4 %collective-permute-start.1 = (bf16[512,384]{1,0:T(8,128)(2,1)S(1)}, bf16[512,384]{1,0:T(8,128)(2,1)S(1)}, u32[]{:S(2)}, u32[]{:S(2)}) collective-permute-start(bf16[512,384]{1,0:T(8,128)(2,1)S(1)} %get-tuple-element.32), channel_id=1, source_target_pairs={{0,1},{1,0},{2,3},{3,2},{4,5},{5,4},{6,7},{7,6},{8,9},{9,8},{10,11... | collective-permute-start | bytes 1179656 | tf_op jit(solution)/shard_map/ppermute | solution.py:306
  5.2 3.6 %collective-permute-start.2 = (bf16[512,256]{1,0:T(8,128)(2,1)S(1)}, bf16[512,256]{1,0:T(8,128)(2,1)S(1)}, u32[]{:S(2)}, u32[]{:S(2)}) collective-permute-start(bf16[512,256]{1,0:T(8,128)(2,1)S(1)} %get-tuple-element.33), channel_id=1, source_target_pairs={{0,1},{1,0},{2,3},{3,2},{4,5},{5,4},{6,7},{7,6},{8,9},{9,8},{10,11... | collective-permute-start | bytes 786440 | tf_op jit(solution)/shard_map/ppermute | solution.py:306
  10.7 7.6 %collective-permute-start.3 = (bf16[512,640]{1,0:T(8,128)(2,1)S(1)}, bf16[512,640]{1,0:T(8,128)(2,1)S(1)}, u32[]{:S(2)}, u32[]{:S(2)}) collective-permute-start(bf16[512,640]{1,0:T(8,128)(2,1)S(1)} %get-tuple-element.41), channel_id=1, source_target_pairs={{0,1},{1,2},{2,0},{3,4},{4,5},{5,6},{6,7},{7,8},{8,9},{9,10},{10,1... | collective-permute-start | bytes 1966088 | tf_op jit(solution)/shard_map/ppermute | solution.py:306
  10.8 14.5 %collective-permute-start.7 = (bf16[512,640]{1,0:T(8,128)(2,1)S(1)}, bf16[512,640]{1,0:T(8,128)(2,1)S(1)}, u32[]{:S(2)}, u32[]{:S(2)}) collective-permute-start(bf16[512,640]{1,0:T(8,128)(2,1)S(1)} %get-tuple-element.38.tg), channel_id=1, source_target_pairs={{31,30},{30,29},{29,31},{28,27},{27,26},{26,25},{25,24},{24,23},{2... | collective-permute-start | bytes 1966088 | tf_op jit(solution)/shard_map/ppermute | solution.py:306
  12.4 2.7 %collective-permute-start.4 = (bf16[512,256]{1,0:T(8,128)(2,1)S(1)}, bf16[512,256]{1,0:T(8,128)(2,1)S(1)}, u32[]{:S(2)}, u32[]{:S(2)}) collective-permute-start(bf16[512,256]{1,0:T(8,128)(2,1)S(1)} %get-tuple-element.42), channel_id=1, source_target_pairs={{0,1},{1,0},{2,3},{3,2},{4,5},{5,4},{6,7},{7,6},{8,9},{9,8},{10,11... | collective-permute-start | bytes 786440 | tf_op jit(solution)/shard_map/ppermute | solution.py:306
  13.4 1.7 %collective-permute-start.5 = (bf16[512,256]{1,0:T(8,128)(2,1)S(1)}, bf16[512,256]{1,0:T(8,128)(2,1)S(1)}, u32[]{:S(2)}, u32[]{:S(2)}) collective-permute-start(bf16[512,256]{1,0:T(8,128)(2,1)S(1)} %get-tuple-element.43), channel_id=1, source_target_pairs={{0,1},{1,0},{2,3},{3,2},{4,5},{5,4},{6,7},{7,6},{8,9},{9,8},{10,11... | collective-permute-start | bytes 786440 | tf_op jit(solution)/shard_map/ppermute | solution.py:306
  13.5 1.6 %collective-permute-start.6 = (bf16[512,128]{1,0:T(8,128)(2,1)S(1)}, bf16[512,128]{1,0:T(8,128)(2,1)S(1)}, u32[]{:S(2)}, u32[]{:S(2)}) collective-permute-start(bf16[512,128]{1,0:T(8,128)(2,1)S(1)} %get-tuple-element.44), channel_id=1, source_target_pairs={{0,1},{1,0},{2,3},{3,2},{4,5},{5,4},{6,7},{7,6},{8,9},{9,8},{10,11... | collective-permute-start | bytes 393224 | tf_op jit(solution)/shard_map/ppermute | solution.py:306
  27.1 7.4 %collective-permute-start.8 = (bf16[512,128]{1,0:T(8,128)(2,1)S(1)}, bf16[512,128]{1,0:T(8,128)(2,1)S(1)}, u32[]{:S(2)}, u32[]{:S(2)}) collective-permute-start(bf16[512,128]{1,0:T(8,128)(2,1)S(1)} %get-tuple-element.47.y_pair), channel_id=1, source_target_pairs={{0,1},{1,0},{2,3},{3,2},{4,5},{5,4},{6,7},{7,6},{8,9},{9,8},{10,11... | collective-permute-start | bytes 393224 | tf_op jit(solution)/shard_map/ppermute | solution.py:306
  29.2 13.1 %collective-permute-start.10 = (bf16[512,128]{1,0:T(8,128)(2,1)S(1)}, bf16[512,128]{1,0:T(8,128)(2,1)S(1)}, u32[]{:S(2)}, u32[]{:S(2)}) collective-permute-start(bf16[512,128]{1,0:T(8,128)(2,1)S(1)} %get-tuple-element.48.y_gap), channel_id=1, source_target_pairs={{31,30},{30,29},{29,31},{28,27},{27,26},{26,25},{25,24},{24,23},{2... | collective-permute-start | bytes 393224 | tf_op jit(solution)/shard_map/ppermute | solution.py:306
  29.2 13.0 %collective-permute-start.9 = (bf16[512,128]{1,0:T(8,128)(2,1)S(1)}, bf16[512,128]{1,0:T(8,128)(2,1)S(1)}, u32[]{:S(2)}, u32[]{:S(2)}) collective-permute-start(bf16[512,128]{1,0:T(8,128)(2,1)S(1)} %get-tuple-element.48.y_gap), channel_id=1, source_target_pairs={{0,1},{1,2},{2,0},{3,4},{4,5},{5,6},{6,7},{7,8},{8,9},{9,10},{10,1... | collective-permute-start | bytes 393224 | tf_op jit(solution)/shard_map/ppermute | solution.py:306
  35.3 8.0 %collective-permute-start.13 = (bf16[512,128]{1,0:T(8,128)(2,1)S(1)}, bf16[512,128]{1,0:T(8,128)(2,1)S(1)}, u32[]{:S(2)}, u32[]{:S(2)}) collective-permute-start(bf16[512,128]{1,0:T(8,128)(2,1)S(1)} %shard_map.54.after), channel_id=1, source_target_pairs={{31,30},{30,29},{29,31},{28,27},{27,26},{26,25},{25,24},{24,23},{2... | collective-permute-start | bytes 393224 | tf_op jit(solution)/shard_map/ppermute | solution.py:306
  35.3 8.0 %collective-permute-start.12 = (bf16[512,128]{1,0:T(8,128)(2,1)S(1)}, bf16[512,128]{1,0:T(8,128)(2,1)S(1)}, u32[]{:S(2)}, u32[]{:S(2)}) collective-permute-start(bf16[512,128]{1,0:T(8,128)(2,1)S(1)} %shard_map.54.after), channel_id=1, source_target_pairs={{0,1},{1,2},{2,0},{3,4},{4,5},{5,6},{6,7},{7,8},{8,9},{9,10},{10,1... | collective-permute-start | bytes 393224 | tf_op jit(solution)/shard_map/ppermute | solution.py:306
  42.6 1.4 %collective-permute-start.11 = (bf16[512,128]{1,0:T(8,128)(2,1)S(1)}, bf16[512,128]{1,0:T(8,128)(2,1)S(1)}, u32[]{:S(2)}, u32[]{:S(2)}) collective-permute-start(bf16[512,128]{1,0:T(8,128)(2,1)S(1)} %shard_map.56), channel_id=1, source_target_pairs={{0,1},{1,0},{2,3},{3,2},{4,5},{5,4},{6,7},{7,6},{8,9},{9,8},{10,11... | collective-permute-start | bytes 393224 | tf_op jit(solution)/shard_map/ppermute | solution.py:306
  44.4 8.0 %collective-permute-start.15 = (bf16[512,128]{1,0:T(8,128)(2,1)S(1)}, bf16[512,128]{1,0:T(8,128)(2,1)S(1)}, u32[]{:S(2)}, u32[]{:S(2)}) collective-permute-start(bf16[512,128]{1,0:T(8,128)(2,1)S(1)} %shard_map.57.x), channel_id=1, source_target_pairs={{31,30},{30,29},{29,31},{28,27},{27,26},{26,25},{25,24},{24,23},{2... | collective-permute-start | bytes 393224 | tf_op jit(solution)/shard_map/ppermute | solution.py:306
  44.6 7.8 %collective-permute-start.14 = (bf16[512,128]{1,0:T(8,128)(2,1)S(1)}, bf16[512,128]{1,0:T(8,128)(2,1)S(1)}, u32[]{:S(2)}, u32[]{:S(2)}) collective-permute-start(bf16[512,128]{1,0:T(8,128)(2,1)S(1)} %shard_map.57.x), channel_id=1, source_target_pairs={{0,1},{1,0},{2,3},{3,2},{4,5},{5,4},{6,7},{7,6},{8,9},{9,8},{10,11... | collective-permute-start | bytes 393224 | tf_op jit(solution)/shard_map/ppermute | solution.py:306

commit v3 on v2

v3 whole, which is shorter than its diff:
```python
import functools

import jax
import jax.numpy as jnp
from jax import lax
from jax.experimental import pallas as pl
from jax.experimental.pallas import tpu as pltpu
from jax.sharding import PartitionSpec as P


AXES = ("grp", "dev")
BF16 = jnp.bfloat16
F32 = jnp.float32
VMEM_BYTES = 12 * 1024 * 1024


def is_odd():
    return lax.rem(lax.axis_index(AXES), 2) == 1


def if_left(value):
    return jnp.where(lax.axis_index(AXES) > 0, value, jnp.zeros_like(value))


def if_right(value):
    last = lax.axis_size(AXES) - 1
    return jnp.where(lax.axis_index(AXES) < last, value, jnp.zeros_like(value))


def dot(a, b):
    return jnp.dot(a, b, preferred_element_type=F32)


def by_parity(even, odd):
    odd_here = is_odd()
    if odd is not None:
        pl.when(odd_here)(odd)
    if even is not None:
        pl.when(jnp.logical_not(odd_here))(even)


def identity(order):
    rows = lax.broadcasted_iota(jnp.int32, (order, order), 0)
    return (rows == lax.broadcasted_iota(jnp.int32, (order, order), 1)).astype(F32)


def local_call(kernel, outs, ins, flops, in_hbm=0, scratch=(), aliases=None, weight=0.001):
    vmem = pl.BlockSpec(memory_space=pltpu.VMEM)
    hbm = pl.BlockSpec(memory_space=pl.ANY)
    many = len(outs) > 1
    ins = [pltpu.with_memory_space_constraint(x, pltpu.HBM) for x in ins[:in_hbm]] + ins[in_hbm:]
    return pl.pallas_call(
        kernel,
        out_shape=outs if many else outs[0],
        in_specs=[hbm] * in_hbm + [vmem] * (len(ins) - in_hbm),
        out_specs=[vmem] * len(outs) if many else vmem,
        scratch_shapes=list(scratch),
        input_output_aliases=aliases or {},
        compiler_params=pltpu.CompilerParams(vmem_limit_bytes=VMEM_BYTES),
        cost_estimate=pl.CostEstimate(flops=int(flops * weight), bytes_accessed=0, transcendentals=0),
    )(*ins)


def bf16_array(rows, columns):
    return jax.ShapeDtypeStruct((rows, columns), BF16)


def f32_array(rows, columns):
    return jax.ShapeDtypeStruct((rows, columns), F32)


def fetch(source, target, sem):
    copy = pltpu.make_async_copy(source, target, sem)
    copy.start()
    return copy


def load_row(order, diag, upper, right, vg, diag_b, upper_b, right_b, sems):
    d_b = fetch(diag.at[1], diag_b, sems.at[0])
    u_b = fetch(upper.at[1], upper_b, sems.at[1])
    r_b = fetch(right.at[1], right_b, sems.at[2])
    d_b.wait()
    u_b.wait()
    vg[:, :order] = dot(diag_b[...], upper_b[...]).astype(BF16)
    r_b.wait()
    vg[:, order:] = dot(diag_b[...], right_b[...]).astype(BF16)


def second_row_odd(order, *refs):
    by_parity(None, lambda: load_row(order, *refs))


def second_row(order, diag, upper, right, vg_odd, vg_b, *rest):
    *pieces, diag_b, upper_b, right_b, sems = rest

    def odd():
        vg_b[...] = vg_odd[...]

    def even():
        load_row(order, diag, upper, right, vg_b, diag_b, upper_b, right_b, sems)
        first = 0
        for piece in pieces:
            piece[...] = vg_b[:, first : first + piece.shape[1]]
            first += piece.shape[1]

    by_parity(even, odd)


def own_products(
    order, diag, lower, upper, right, vg_b, w_a, w_b, m, n, r,
    diag_a, lower_a, upper_a, right_a, diag_b, lower_b, sems,
):
    d_a = fetch(diag.at[0], diag_a, sems.at[0])
    u_a = fetch(upper.at[0], upper_a, sems.at[1])
    d_b = fetch(diag.at[1], diag_b, sems.at[2])
    l_b = fetch(lower.at[1], lower_b, sems.at[3])
    l_a = fetch(lower.at[0], lower_a, sems.at[4])
    r_a = fetch(right.at[0], right_a, sems.at[5])
    d_a.wait()
    u_a.wait()
    v_a = dot(diag_a[...], upper_a[...]).astype(BF16)
    d_b.wait()
    l_b.wait()
    w_b[...] = dot(diag_b[...], lower_b[...]).astype(BF16)
    l_a.wait()
    w_a[...] = dot(diag_a[...], lower_a[...]).astype(BF16)
    r_a.wait()
    g_a = dot(diag_a[...], right_a[...]).astype(BF16)
    n[...] = dot(v_a, vg_b[:, :order]).astype(BF16)
    r[...] = g_a.astype(F32) - dot(v_a, vg_b[:, order:])
    m[...] = dot(v_a, w_b[...])


def scale_one(order, w_a, m, r, v_left, g_left, scale, tg):
    first = 0
    eye = identity(order)
    for piece in v_left:
        at = slice(first, first + piece.shape[1])
        coupling = if_left(dot(w_a[...], piece[...])) + m[:, at]
        scale[:, at] = (eye[:, at] + coupling).astype(BF16)
        first = at.stop
    rest = (r[...] - if_left(dot(w_a[...], g_left[...]))).astype(BF16)
    tg[:, :order] = dot(scale[...], w_a[...]).astype(BF16)
    tg[:, order:] = dot(scale[...], rest).astype(BF16)


def spikes_one(order, scale, n, w_b, tg, v_one, w_t, w_v, w_g):
    v_one[...] = (-dot(scale[...], n[...])).astype(BF16)
    w_v[...] = dot(w_b[...], v_one[...]).astype(BF16)
    w_g[...] = dot(w_b[...], tg[:, order:]).astype(BF16)
    w_t[...] = dot(w_b[...], tg[:, :order]).astype(BF16)


def pack(side):
    columns = side.shape[1]
    return jnp.concatenate(
        [side[i : i + columns] for i in range(0, side.shape[0], columns)], axis=1
    )


def unpack(rows, columns):
    return jnp.concatenate(
        [rows[:, i : i + columns] for i in range(0, rows.shape[1], columns)], axis=0
    )


def hand_to_pair(order, blocks, side, to_pair):
    rows, first = pack(side), 0
    for block, piece in zip(blocks, to_pair):
        last = first + piece.shape[0] - order
        piece[:order, :] = block
        piece[order:, :] = rows[first:last]
        first = last


def side_of_pair(order, got, columns):
    return unpack(jnp.concatenate([piece[order:, :] for piece in got], axis=0), columns)


def level_one_odd(order, w_a, m, r, v0, vg1, n, w_b, tg, v_one, w_vg, *rest):
    *to_pair, scale, w_t = rest
    columns = order - v0.shape[1]

    def odd():
        v_left, g_left = [v0, vg1.at[:, :columns]], vg1.at[:, columns:]
        scale_one(order, w_a, m, r, v_left, g_left, scale, tg)
        w_v, w_g = w_vg.at[:, :order], w_vg.at[:, order:]
        spikes_one(order, scale, n, w_b, tg, v_one, w_t, w_v, w_g)
        hand_to_pair(order, [tg[:, :order], w_t[...], v_one[...]], tg[:, order:], to_pair)

    by_parity(None, odd)


def scale_one_even(order, w_a, m, r, vg, tg_odd, tg, scale):
    v_left, g_left = [vg.at[:, :order]], vg.at[:, order:]
    by_parity(lambda: scale_one(order, w_a, m, r, v_left, g_left, scale, tg), None)


def spikes_one_even(order, scale, n, w_b, tg, v_odd, pair0, pair1, pair2, v_one, *rest):
    *to_pair, w_t, w_v, w_g = rest

    def even():
        spikes_one(order, scale, n, w_b, tg, v_one, w_t, w_v, w_g)
        hand_to_pair(order, [w_v[...], w_t[...], v_one[...]], w_g[...], to_pair)

    by_parity(even, None)


def pair_part(
    order, tg, v_one, w_b, to_pair1, w_vg, pair0, pair1, pair2,
    near, far, w_far, p_far, p_v, n_h, w_h, w_n_h, p_n_h,
):
    got, w_t, w_t_pair, v_pair = (x[:order, :] for x in (pair0, to_pair1, pair1, pair2))
    got_g = side_of_pair(order, [pair0, pair1, pair2], n_h.shape[1])
    t, eye = tg[:, :order], identity(order)

    def even():
        right = dot(got, w_b[...]).astype(BF16)
        near[...] = (eye - dot(v_one[...], right)).astype(BF16)
        far[...] = dot(w_b[...], near[...]).astype(BF16)
        p_far[...] = dot(w_t_pair, far[...]).astype(BF16)
        p_v[...] = dot(w_t_pair, w_t).astype(BF16)
        n_h[...] = tg[:, order:].astype(F32) - dot(v_one[...], got_g)

    def odd():
        near[...] = (eye - dot(t, got)).astype(BF16)
        far[...] = dot(near[...], v_one[...]).astype(BF16)
        w_far[...] = dot(w_b[...], far[...]).astype(BF16)
        p_far[...] = dot(v_pair, far[...]).astype(BF16)
        p_v[...] = dot(v_pair, v_one[...]).astype(BF16)
        own = (tg[:, order:].astype(F32) + dot(t, got_g)).astype(BF16)
        scaled = dot(near[...], own)
        n_h[...] = scaled
        w_h[...] = dot(w_b[...], own)
        w_n_h[...] = dot(w_b[...], scaled.astype(BF16))
        p_n_h[...] = dot(v_pair, scaled.astype(BF16))

    by_parity(even, odd)


def level_two(
    order, tg, v_one, w_vg, near, far, w_far, p_far, p_v, n_h, w_h, w_n_h, p_n_h, w_vg_gap, tg_gap,
    g, a0, a1, b,
):
    rows = order // 2
    left_of_two = lax.rem(lax.axis_index(AXES), 4) < 2

    def hand_out(right, left):
        first, second = jnp.where(left_of_two, right, left), jnp.where(left_of_two, left, right)
        a0[...] = first[:rows]
        a1[...] = first[rows:]
        b[...] = second

    def even():
        t = tg[:, :order]
        whole = (n_h[...] + if_left(dot(t, w_vg_gap[:, order:]))).astype(BF16)
        from_left = if_left(dot(w_vg_gap[:, :order], whole)).astype(BF16)
        value = (dot(near[...], whole) - dot(t, from_left)).astype(BF16)
        onward = (dot(p_v[...], from_left) - dot(p_far[...], whole)).astype(BF16)
        g[...] = value
        hand_out(onward, value)

    def odd():
        g_right, w_v = tg_gap[:, order:], w_vg[:, :order]
        own = w_h[...] - if_right(dot(w_v, g_right))
        from_right = if_right(dot(tg_gap[:, :order], own.astype(BF16))).astype(BF16)

        def whole(start, gap, further):
            return (start[...] - if_right(dot(gap[...], g_right)) - dot(further, from_right)).astype(BF16)

        g[...] = whole(n_h, far, v_one[...])
        hand_out(whole(w_n_h, w_far, w_v), whole(p_n_h, p_far, p_v[...]))

    by_parity(even, odd)


def spikes_two(
    order, tg, v_one, w_b, pair1, pair2, near, w_vg_gap, tg_gap, after, from_left, from_right, scale
):
    t = tg[:, :order]
    index, count = lax.axis_index(AXES), lax.axis_size(AXES)

    def put(left, right):
        from_left[...] = jnp.where(index > 1, left, jnp.zeros_like(left)).astype(BF16)
        from_right[...] = jnp.where(index < count - 2, right, jnp.zeros_like(right)).astype(BF16)

    def even():
        gap = if_left(dot(t, w_vg_gap[:, :order]))
        scale[...] = (near[...].astype(F32) - gap).astype(BF16)
        s_v = dot(scale[...], v_one[...]).astype(BF16)
        put(-dot(scale[...], t), dot(s_v, pair2[:order, :]))

    def odd():
        right = dot(tg_gap[:, :order], w_b[...]).astype(BF16)
        gap = if_right(dot(v_one[...], right))
        scale[...] = (near[...].astype(F32) - gap).astype(BF16)
        s_t = dot(scale[...], t).astype(BF16)
        put(dot(s_t, pair1[:order, :]), dot(scale[...], v_one[...]))

    by_parity(even, odd)


def top_values(g, from_left, from_right, a0, a1, b, x, *halves):
    def top(left, right):
        change = dot(from_left[...], left) + dot(from_right[...], right)
        x[...] = (g[...].astype(F32) + change).astype(BF16)

    first = jnp.concatenate([a0[...], a1[...]], axis=0)
    left_of_two = lax.rem(lax.axis_index(AXES), 4) < 2
    pl.when(left_of_two)(lambda: top(b[...], first))
    pl.when(jnp.logical_not(left_of_two))(lambda: top(first, b[...]))
    rows = halves[0].shape[0]
    for i, half in enumerate(halves):
        half[...] = x[i * rows : (i + 1) * rows, :]


def second_values(order, vg_b, w_b, x, x_pair0, x_pair1, rest):
    rest[...] = vg_b[:, order:].astype(F32) - dot(w_b[...], x[...])

    def even():
        x_next = jnp.concatenate([x_pair0[...], x_pair1[...]], axis=0)
        rest[...] -= dot(vg_b[:, :order], x_next)

    by_parity(even, None)


def finish(order, vg_b, x, rest, x_gap, out):
    out[0] = x[...]

    def even():
        out[1] = rest[...].astype(BF16)

    def odd():
        out[1] = (rest[...] - if_right(dot(vg_b[:, :order], x_gap[...]))).astype(BF16)

    by_parity(even, odd)


def exchanges(slab, count):
    pairs = [(i, i ^ 1) for i in range(count)]
    twos = [(i, i ^ 2) for i in range(count)]
    inner = range(2, count - 2)
    other_twos = [(i, ((i - 2) ^ 2) + 2 if i in inner else i ^ 1) for i in range(count)]
    after = [(i + 1) % count for i in range(count)]
    after[2], after[slab + 2], after[count - 1] = 0, 3, count - 5
    for first in range(slab + 3, count - 5, 4):
        after[first + 3] = first
    to_right = list(enumerate(after))
    to_left = [(count - 1 - i, count - 1 - j) for i, j in to_right]
    return pairs, twos, other_twos, to_right, to_left


def body(diag, lower, upper, right):
    order, rhs = diag.shape[1], right.shape[2]
    count = lax.axis_size(AXES)
    pairs, twos, other_twos, to_right, to_left = exchanges(lax.axis_size("dev"), count)

    def sent(block, route):
        return lax.ppermute(block, AXES, route)

    part = functools.partial
    square = 2 * order**3
    thin = 2 * order * order * rhs
    block = pltpu.VMEM((order, order), BF16)
    side = pltpu.VMEM((order, rhs), BF16)
    wide = bf16_array(order, order + rhs)
    full = bf16_array(order, order)
    slim = bf16_array(order, rhs)

    row_scratch = (block, block, side, pltpu.SemaphoreType.DMA((3,)))
    vg_odd = local_call(
        part(second_row_odd, order), [wide], [diag, upper, right], square + thin, 3, row_scratch
    )
    vg_gap = sent(vg_odd, to_right)
    cut = 3 * order // 4
    vg_b, *to_pair = local_call(
        part(second_row, order),
        [wide, bf16_array(order, cut), bf16_array(order, order - cut + rhs)],
        [diag, upper, right, vg_odd], square + thin, 3, row_scratch,
    )
    vg_pair = [sent(piece, pairs) for piece in to_pair]
    w_a, w_b, m, n, r = local_call(
        part(own_products, order),
        [full, full, f32_array(order, order), full, f32_array(order, rhs)],
        [diag, lower, upper, right, vg_b], 5 * square + 2 * thin, 4,
        (block, block, block, side, block, block, pltpu.SemaphoreType.DMA((6,))),
    )

    extra = rhs // 16 * 6
    shares = [bf16_array(order + rows, order) for rows in (extra, extra, rhs - 2 * extra)]
    tg_odd, v_odd, w_vg_odd, *to_pair = local_call(
        part(level_one_odd, order),
        [wide, full, wide, *shares], [w_a, m, r, *vg_pair, n, w_b], 5 * square, 0, (block, block),
    )
    w_vg_gap = sent(w_vg_odd, to_right)
    tg, scale = local_call(
        part(scale_one_even, order),
        [wide, full], [w_a, m, r, vg_gap, tg_odd], 2 * square + 2 * thin, aliases={4: 0},
    )
    tg_gap = sent(tg, to_left)
    v_one, *to_pair = local_call(
        part(spikes_one_even, order),
        [full, *shares], [scale, n, w_b, tg, v_odd, *to_pair], 3 * square + thin,
        0, (block, block, side), {4: 0, 5: 1, 6: 2, 7: 3},
    )
    pair = [sent(piece, pairs) for piece in to_pair]

    tall, flat = f32_array(order, rhs), bf16_array(order // 2, rhs)
    known = local_call(
        part(pair_part, order),
        [full] * 5 + [tall] * 4,
        [tg, v_one, w_b, to_pair[1], w_vg_odd, *pair], 6 * square,
    )
    g_two, *to_two = local_call(
        part(level_two, order),
        [slim, flat, flat, slim], [tg, v_one, w_vg_odd, *known, w_vg_gap, tg_gap], 8 * thin,
    )
    by_two = [sent(to_two[0], twos), sent(to_two[1], twos), sent(to_two[2], other_twos)]
    from_left, from_right = local_call(
        part(spikes_two, order),
        [full, full],
        [tg, v_one, w_b, *pair[1:], known[0], w_vg_gap, tg_gap, g_two], 5 * square,
        0, (block,),
    )
    x, *x_own = local_call(
        top_values, [slim, flat, flat], [g_two, from_left, from_right, *by_two], 2 * thin
    )
    x_gap = sent(x, to_left)
    x_pair = [sent(piece, pairs) for piece in x_own]
    rest = local_call(part(second_values, order), [tall], [vg_b, w_b, x, *x_pair], 2 * thin, weight=1)
    return local_call(
        part(finish, order),
        [jax.ShapeDtypeStruct((2, order, rhs), BF16)], [vg_b, x, rest, x_gap], thin,
    )


def solution(mesh):
    split = P(AXES, None, None)
    return jax.shard_map(
        body, mesh=mesh, in_specs=(split,) * 4, out_specs=split, check_vma=False
    )
```

time: 53.7 us -> 47.8 us (0.89)
  starting transfers between devices: 19.1 us -> 12.6 us
  Pallas kernels: 14.5 us -> 15.9 us
  waiting for transfers between devices: 19.7 us -> 19 us
    ppermute x16 -> x14, starting transfers between devices: 19.1 us -> 12.6 us  [sent(): return lax.ppermute(block, AXES, route)]
    pallas_call x14 -> x12, Pallas kernels: 14.5 us -> 15.9 us  [local_call(): pl.pallas_call(kernel, out_shape=outs if many else outs[0], in_specs=[hbm...]
    ppermute x16 -> x14, waiting for transfers between devices: 19.7 us -> 19 us  [sent(): return lax.ppermute(block, AXES, route)]
  transfers between devices with their start and end apart: 16 -> 14, of which waited for: 6 -> 7; matrix products, arithmetic and copies ran while one was open for 0% -> 0% of each run, Pallas kernels for 17% -> 22%
where the time goes in v3:
time: 47.8 us; the launch traced here: 47.7 us
  waiting for transfers between devices  19 us (40%)
  Pallas kernels  15.9 us (33%)
  starting transfers between devices  12.6 us (26%)
    ppermute x14, waiting for transfers between devices, sent(): return lax.ppermute(block, AXES, route)  19 us
    pallas_call x12, Pallas kernels, local_call(): pl.pallas_call(kernel, out_shape=outs if many else outs[0], in_specs=[hbm...  15.9 us
    ppermute x14, starting transfers between devices, sent(): return lax.ppermute(block, AXES, route)  12.6 us
  transfers between devices with their start and end apart: 14, of which 7 were waited for; matrix products, arithmetic and copies ran while one was open for 0% of the time, Pallas kernels for 22%

profile of v3, /device:TPU:29, one launch (start us, length us, event | category | flops | bytes accessed | tf_op | source)
XLA Modules:
  0.0 47.7 jit_solution(2164232001432873307)
XLA Ops:
  0.0 2.2 %shard_map.46.vg_odd = bf16[512,640]{1,0:T(8,128)(2,1)S(1)} custom-call(bf16[2,512,512]{2,1,0:T(8,128)(2,1)} %diag.3, bf16[2,512,512]{2,1,0:T(8,128)(2,1)} %upper.3, bf16[2,512,128]{2,1,0:T(8,128)(2,1)} %right.3), custom_call_target="tpu_custom_call" | custom-call | flops 335544 | tf_op jit(solution)/shard_map/pallas_call | solution.py:52
  2.2 0.1 collective-permute-start
  2.3 0.1 shard_map.47
  2.4 2.8 %collective-permute-start.1 = (bf16[512,384]{1,0:T(8,128)(2,1)S(1)}, bf16[512,384]{1,0:T(8,128)(2,1)S(1)}, u32[]{:S(2)}, u32[]{:S(2)}) collective-permute-start(bf16[512,384]{1,0:T(8,128)(2,1)S(1)} %get-tuple-element.47), channel_id=1, source_target_pairs={{0,1},{1,0},{2,3},{3,2},{4,5},{5,4},{6,7},{7,6},{8,9},{9,8},{10,11... | collective-permute-start | bytes 1179656 | tf_op jit(solution)/shard_map/ppermute | solution.py:359
  5.2 0.1 collective-permute-start.2
  5.3 3.6 %shard_map.48 = (bf16[512,512]{1,0:T(8,128)(2,1)S(1)}, bf16[512,512]{1,0:T(8,128)(2,1)S(1)}, f32[512,512]{1,0:T(8,128)S(1)}, bf16[512,512]{1,0:T(8,128)(2,1)S(1)}, f32[512,128]{1,0:T(8,128)S(1)}) custom-call(bf16[2,512,512]{2,1,0:T(8,128)(2,1)} %diag.3, bf16[2,512,512]{2,1,0:T(8,128)(2,1)} %lower.1, bf16[2,512,512]{2,1,0:T(8,128)(2,1)} %upper.3, ...), custom_call_target="tpu_custom_call" | custom-call | flops 1476395 | tf_op jit(solution)/shard_map/pallas_call | solution.py:52
  8.8 0.0 collective-permute-done.2.vg1
  8.8 0.0 collective-permute-done.1.v0
  8.8 2.2 %shard_map.49 = (bf16[512,640]{1,0:T(8,128)(2,1)S(1)}, bf16[512,512]{1,0:T(8,128)(2,1)S(1)}, bf16[512,640]{1,0:T(8,128)(2,1)S(1)}, bf16[560,512]{1,0:T(8,128)(2,...) custom-call(bf16[512,512]{1,0:T(8,128)(2,1)S(1)} %get-tuple-element.44.w_a, ...), custom_call_target="tpu_custom_call" | custom-call | flops 1342177 | tf_op jit(solution)/shard_map/pallas_call | solution.py:52
  11.0 0.1 collective-permute-start.6
  11.1 0.0 collective-permute-done.vg
  11.1 1.5 %collective-permute-start.7 = (bf16[512,640]{1,0:T(8,128)(2,1)S(1)}, bf16[512,640]{1,0:T(8,128)(2,1)S(1)}, u32[]{:S(2)}, u32[]{:S(2)}) collective-permute-start(bf16[512,640]{1,0:T(8,128)(2,1)S(1)} %get-tuple-element.52.tg), channel_id=1, source_target_pairs={{31,30},{30,29},{29,31},{28,27},{27,26},{26,25},{25,24},{24,23},{2... | collective-permute-start | bytes 1966088 | tf_op jit(solution)/shard_map/ppermute | solution.py:359
  12.7 1.3 %collective-permute-start.3 = (bf16[560,512]{1,0:T(8,128)(2,1)S(1)}, bf16[560,512]{1,0:T(8,128)(2,1)S(1)}, u32[]{:S(2)}, u32[]{:S(2)}) collective-permute-start(bf16[560,512]{1,0:T(8,128)(2,1)S(1)} %get-tuple-element.61), channel_id=1, source_target_pairs={{0,1},{1,0},{2,3},{3,2},{4,5},{5,4},{6,7},{7,6},{8,9},{9,8},{10,11... | collective-permute-start | bytes 1720328 | tf_op jit(solution)/shard_map/ppermute | solution.py:359
  14.0 0.1 collective-permute-start.4
  14.1 0.4 collective-permute-start.5
  14.5 2.7 %collective-permute-done.5.pair2 = bf16[544,512]{1,0:T(8,128)(2,1)S(1)} collective-permute-done((bf16[544,512]{1,0:T(8,128)(2,1)S(1)}, bf16[544,512]{1,0:T(8,128)(2,1)S(1)}, u32[]{:S(2)}, u32[]{:S(2)}) %collective-permute-start.5) | collective-permute-done | bytes 557088 | tf_op jit(solution)/shard_map/ppermute | solution.py:359
  17.2 0.0 collective-permute-done.3.pair0
  17.2 0.0 collective-permute-done.4.pair1
  17.2 2.6 %shard_map.52 = (bf16[512,512]{1,0:T(8,128)(2,1)S(1)}, bf16[512,512]{1,0:T(8,128)(2,1)S(1)}, bf16[512,512]{1,0:T(8,128)(2,1)S(1)}, bf16[512,512]{1,0:T(8,128)(2,...) custom-call(bf16[512,640]{1,0:T(8,128)(2,1)S(1)} %get-tuple-element., ...), custom_call_target="tpu_custom_call" | custom-call | flops 1610612 | tf_op jit(solution)/shard_map/pallas_call | solution.py:52
  19.8 0.0 collective-permute-done.6.w_vg_gap
  19.8 5.5 %collective-permute-done.7.tg_gap = bf16[512,640]{1,0:T(8,128)(2,1)S(1)} collective-permute-done((bf16[512,640]{1,0:T(8,128)(2,1)S(1)}, bf16[512,640]{1,0:T(8,128)(2,1)S(1)}, u32[]{:S(2)}, u32[]{:S(2)}) %collective-permute-start.7) | collective-permute-done | bytes 655392 | tf_op jit(solution)/shard_map/ppermute | solution.py:359
  25.4 1.8 %shard_map.53 = (bf16[512,128]{1,0:T(8,128)(2,1)S(1)}, bf16[256,128]{1,0:T(8,128)(2,1)S(1)}, bf16[256,128]{1,0:T(8,128)(2,1)S(1)}, bf16[512,128]{1,0:T(8,128)(2,1)S(1)}) custom-call(bf16[512,640]{1,0:T(8,128)(2,1)S(1)} %get-tuple-element.52.tg, bf16[512,512]{1,0:T(8,128)(2,1)S(1)} %get-tuple-element.58.v_one, bf16[512,640]{1,0:T(8,128)(2,1)S(1)} %get-tuple-element.59.w_vg, ...), custom_call_target="tpu_custom_call" | custom-call | flops 536870 | tf_op jit(solution)/shard_map/pallas_call | solution.py:52
  27.2 4.2 %collective-permute-start.10 = (bf16[512,128]{1,0:T(8,128)(2,1)S(1)}, bf16[512,128]{1,0:T(8,128)(2,1)S(1)}, u32[]{:S(2)}, u32[]{:S(2)}) collective-permute-start(bf16[512,128]{1,0:T(8,128)(2,1)S(1)} %get-tuple-element.77), channel_id=1, source_target_pairs={{0,1},{1,0},{2,4},{3,5},{4,2},{5,3},{6,8},{7,9},{8,6},{9,7},{10,12... | collective-permute-start | bytes 393224 | tf_op jit(solution)/shard_map/ppermute | solution.py:359
  31.4 0.0 collective-permute-start.8
  31.4 1.5 %collective-permute-start.9 = (bf16[256,128]{1,0:T(8,128)(2,1)S(1)}, bf16[256,128]{1,0:T(8,128)(2,1)S(1)}, u32[]{:S(2)}, u32[]{:S(2)}) collective-permute-start(bf16[256,128]{1,0:T(8,128)(2,1)S(1)} %get-tuple-element.76), channel_id=1, source_target_pairs={{0,2},{1,3},{2,0},{3,1},{4,6},{5,7},{6,4},{7,5},{8,10},{9,11},{10,... | collective-permute-start | bytes 196616 | tf_op jit(solution)/shard_map/ppermute | solution.py:359
  32.8 1.6 %shard_map.54 = (bf16[512,512]{1,0:T(8,128)(2,1)S(1)}, bf16[512,512]{1,0:T(8,128)(2,1)S(1)}) custom-call(bf16[512,640]{1,0:T(8,128)(2,1)S(1)} %get-tuple-element.52.tg, bf16[512,512]{1,0:T(8,128)(2,1)S(1)} %get-tuple-element.58.v_one, bf16[512,512]{1,0:T(8,128)(2,1)S(1)} %get-tuple-element.50.w_b, bf16[560,512]{1,0:T(8,128)(2,1)S(1)} %collective-permute-done.4.pair1, ...), custom_call_target="tpu_custom_call" | custom-call | flops 1342177 | tf_op jit(solution)/shard_map/pallas_call | solution.py:52
  34.5 3.1 %collective-permute-done.8.a0 = bf16[256,128]{1,0:T(8,128)(2,1)S(1)} collective-permute-done((bf16[256,128]{1,0:T(8,128)(2,1)S(1)}, bf16[256,128]{1,0:T(8,128)(2,1)S(1)}, u32[]{:S(2)}, u32[]{:S(2)}) %collective-permute-start.8) | collective-permute-done | bytes 65568 | tf_op jit(solution)/shard_map/ppermute | solution.py:359
  37.6 0.5 %collective-permute-done.9.a1 = bf16[256,128]{1,0:T(8,128)(2,1)S(1)} collective-permute-done((bf16[256,128]{1,0:T(8,128)(2,1)S(1)}, bf16[256,128]{1,0:T(8,128)(2,1)S(1)}, u32[]{:S(2)}, u32[]{:S(2)}) %collective-permute-start.9) | collective-permute-done | bytes 65568 | tf_op jit(solution)/shard_map/ppermute | solution.py:359
  38.1 0.0 collective-permute-done.10.b
  38.1 0.5 shard_map.55
  38.6 0.1 collective-permute-start.13
  38.7 0.1 collective-permute-start.11
  38.8 0.5 %collective-permute-start.12 = (bf16[256,128]{1,0:T(8,128)(2,1)S(1)}, bf16[256,128]{1,0:T(8,128)(2,1)S(1)}, u32[]{:S(2)}, u32[]{:S(2)}) collective-permute-start(bf16[256,128]{1,0:T(8,128)(2,1)S(1)} %get-tuple-element.80), channel_id=1, source_target_pairs={{0,1},{1,0},{2,3},{3,2},{4,5},{5,4},{6,7},{7,6},{8,9},{9,8},{10,11... | collective-permute-start | bytes 196616 | tf_op jit(solution)/shard_map/ppermute | solution.py:359
  39.3 0.7 %collective-permute-done.11.x_pair0 = bf16[256,128]{1,0:T(8,128)(2,1)S(1)} collective-permute-done((bf16[256,128]{1,0:T(8,128)(2,1)S(1)}, bf16[256,128]{1,0:T(8,128)(2,1)S(1)}, u32[]{:S(2)}, u32[]{:S(2)}) %collective-permute-start.11) | collective-permute-done | bytes 65568 | tf_op jit(solution)/shard_map/ppermute | solution.py:359
  40.0 0.2 collective-permute-done.12.x_pair1
  40.2 0.3 shard_map.56.rest
  40.5 6.2 %collective-permute-done.13.x_gap = bf16[512,128]{1,0:T(8,128)(2,1)S(1)} collective-permute-done((bf16[512,128]{1,0:T(8,128)(2,1)S(1)}, bf16[512,128]{1,0:T(8,128)(2,1)S(1)}, u32[]{:S(2)}, u32[]{:S(2)}) %collective-permute-start.13) | collective-permute-done | bytes 131104 | tf_op jit(solution)/shard_map/ppermute | solution.py:359
  46.7 1.0 %shard_map.57 = bf16[2,512,128]{2,1,0:T(8,128)(2,1)} custom-call(bf16[512,640]{1,0:T(8,128)(2,1)S(1)} %get-tuple-element.43.vg_b, bf16[512,128]{1,0:T(8,128)(2,1)S(1)} %get-tuple-element.78.x, f32[512,128]{1,0:T(8,128)S(1)} %shard_map.56.rest, bf16[512,128]{1,0:T(8,128)(2,1)S(1)} %collective-permute-done.13.x_gap), custom_call_target="tpu_custom_call" | custom-call | flops 67108 | tf_op jit(solution)/shard_map/pallas_call | solution.py:52
  (2 shorter events, 0.0 us)
Async XLA Ops:
  2.2 8.9 %collective-permute-start = (bf16[512,640]{1,0:T(8,128)(2,1)S(1)}, bf16[512,640]{1,0:T(8,128)(2,1)S(1)}, u32[]{:S(2)}, u32[]{:S(2)}) collective-permute-start(bf16[512,640]{1,0:T(8,128)(2,1)S(1)} %shard_map.46.vg_odd), channel_id=1, source_target_pairs={{0,1},{1,2},{2,0},{3,4},{4,5},{5,6},{6,7},{7,8},{8,9},{9,10},{10,1... | collective-permute-start | bytes 1966088 | tf_op jit(solution)/shard_map/ppermute | solution.py:359
  2.4 6.4 %collective-permute-start.1 = (bf16[512,384]{1,0:T(8,128)(2,1)S(1)}, bf16[512,384]{1,0:T(8,128)(2,1)S(1)}, u32[]{:S(2)}, u32[]{:S(2)}) collective-permute-start(bf16[512,384]{1,0:T(8,128)(2,1)S(1)} %get-tuple-element.47), channel_id=1, source_target_pairs={{0,1},{1,0},{2,3},{3,2},{4,5},{5,4},{6,7},{7,6},{8,9},{9,8},{10,11... | collective-permute-start | bytes 1179656 | tf_op jit(solution)/shard_map/ppermute | solution.py:359
  5.2 3.6 %collective-permute-start.2 = (bf16[512,256]{1,0:T(8,128)(2,1)S(1)}, bf16[512,256]{1,0:T(8,128)(2,1)S(1)}, u32[]{:S(2)}, u32[]{:S(2)}) collective-permute-start(bf16[512,256]{1,0:T(8,128)(2,1)S(1)} %get-tuple-element.48), channel_id=1, source_target_pairs={{0,1},{1,0},{2,3},{3,2},{4,5},{5,4},{6,7},{7,6},{8,9},{9,8},{10,11... | collective-permute-start | bytes 786440 | tf_op jit(solution)/shard_map/ppermute | solution.py:359
  11.0 8.8 %collective-permute-start.6 = (bf16[512,640]{1,0:T(8,128)(2,1)S(1)}, bf16[512,640]{1,0:T(8,128)(2,1)S(1)}, u32[]{:S(2)}, u32[]{:S(2)}) collective-permute-start(bf16[512,640]{1,0:T(8,128)(2,1)S(1)} %get-tuple-element.59.w_vg), channel_id=1, source_target_pairs={{0,1},{1,2},{2,0},{3,4},{4,5},{5,6},{6,7},{7,8},{8,9},{9,10},{10,1... | collective-permute-start | bytes 1966088 | tf_op jit(solution)/shard_map/ppermute | solution.py:359
  11.1 14.2 %collective-permute-start.7 = (bf16[512,640]{1,0:T(8,128)(2,1)S(1)}, bf16[512,640]{1,0:T(8,128)(2,1)S(1)}, u32[]{:S(2)}, u32[]{:S(2)}) collective-permute-start(bf16[512,640]{1,0:T(8,128)(2,1)S(1)} %get-tuple-element.52.tg), channel_id=1, source_target_pairs={{31,30},{30,29},{29,31},{28,27},{27,26},{26,25},{25,24},{24,23},{2... | collective-permute-start | bytes 1966088 | tf_op jit(solution)/shard_map/ppermute | solution.py:359
  12.7 4.5 %collective-permute-start.3 = (bf16[560,512]{1,0:T(8,128)(2,1)S(1)}, bf16[560,512]{1,0:T(8,128)(2,1)S(1)}, u32[]{:S(2)}, u32[]{:S(2)}) collective-permute-start(bf16[560,512]{1,0:T(8,128)(2,1)S(1)} %get-tuple-element.61), channel_id=1, source_target_pairs={{0,1},{1,0},{2,3},{3,2},{4,5},{5,4},{6,7},{7,6},{8,9},{9,8},{10,11... | collective-permute-start | bytes 1720328 | tf_op jit(solution)/shard_map/ppermute | solution.py:359
  14.0 3.2 %collective-permute-start.4 = (bf16[560,512]{1,0:T(8,128)(2,1)S(1)}, bf16[560,512]{1,0:T(8,128)(2,1)S(1)}, u32[]{:S(2)}, u32[]{:S(2)}) collective-permute-start(bf16[560,512]{1,0:T(8,128)(2,1)S(1)} %get-tuple-element.60.to_pair1), channel_id=1, source_target_pairs={{0,1},{1,0},{2,3},{3,2},{4,5},{5,4},{6,7},{7,6},{8,9},{9,8},{10,11... | collective-permute-start | bytes 1720328 | tf_op jit(solution)/shard_map/ppermute | solution.py:359
  14.1 3.1 %collective-permute-start.5 = (bf16[544,512]{1,0:T(8,128)(2,1)S(1)}, bf16[544,512]{1,0:T(8,128)(2,1)S(1)}, u32[]{:S(2)}, u32[]{:S(2)}) collective-permute-start(bf16[544,512]{1,0:T(8,128)(2,1)S(1)} %get-tuple-element.62), channel_id=1, source_target_pairs={{0,1},{1,0},{2,3},{3,2},{4,5},{5,4},{6,7},{7,6},{8,9},{9,8},{10,11... | collective-permute-start | bytes 1671176 | tf_op jit(solution)/shard_map/ppermute | solution.py:359
  27.2 11.0 %collective-permute-start.10 = (bf16[512,128]{1,0:T(8,128)(2,1)S(1)}, bf16[512,128]{1,0:T(8,128)(2,1)S(1)}, u32[]{:S(2)}, u32[]{:S(2)}) collective-permute-start(bf16[512,128]{1,0:T(8,128)(2,1)S(1)} %get-tuple-element.77), channel_id=1, source_target_pairs={{0,1},{1,0},{2,4},{3,5},{4,2},{5,3},{6,8},{7,9},{8,6},{9,7},{10,12... | collective-permute-start | bytes 393224 | tf_op jit(solution)/shard_map/ppermute | solution.py:359
  31.4 6.2 %collective-permute-start.8 = (bf16[256,128]{1,0:T(8,128)(2,1)S(1)}, bf16[256,128]{1,0:T(8,128)(2,1)S(1)}, u32[]{:S(2)}, u32[]{:S(2)}) collective-permute-start(bf16[256,128]{1,0:T(8,128)(2,1)S(1)} %get-tuple-element.75), channel_id=1, source_target_pairs={{0,2},{1,3},{2,0},{3,1},{4,6},{5,7},{6,4},{7,5},{8,10},{9,11},{10,... | collective-permute-start | bytes 196616 | tf_op jit(solution)/shard_map/ppermute | solution.py:359
  31.4 6.8 %collective-permute-start.9 = (bf16[256,128]{1,0:T(8,128)(2,1)S(1)}, bf16[256,128]{1,0:T(8,128)(2,1)S(1)}, u32[]{:S(2)}, u32[]{:S(2)}) collective-permute-start(bf16[256,128]{1,0:T(8,128)(2,1)S(1)} %get-tuple-element.76), channel_id=1, source_target_pairs={{0,2},{1,3},{2,0},{3,1},{4,6},{5,7},{6,4},{7,5},{8,10},{9,11},{10,... | collective-permute-start | bytes 196616 | tf_op jit(solution)/shard_map/ppermute | solution.py:359
  38.6 8.0 %collective-permute-start.13 = (bf16[512,128]{1,0:T(8,128)(2,1)S(1)}, bf16[512,128]{1,0:T(8,128)(2,1)S(1)}, u32[]{:S(2)}, u32[]{:S(2)}) collective-permute-start(bf16[512,128]{1,0:T(8,128)(2,1)S(1)} %get-tuple-element.78.x), channel_id=1, source_target_pairs={{31,30},{30,29},{29,31},{28,27},{27,26},{26,25},{25,24},{24,23},{2... | collective-permute-start | bytes 393224 | tf_op jit(solution)/shard_map/ppermute | solution.py:359
  38.7 1.3 %collective-permute-start.11 = (bf16[256,128]{1,0:T(8,128)(2,1)S(1)}, bf16[256,128]{1,0:T(8,128)(2,1)S(1)}, u32[]{:S(2)}, u32[]{:S(2)}) collective-permute-start(bf16[256,128]{1,0:T(8,128)(2,1)S(1)} %get-tuple-element.79), channel_id=1, source_target_pairs={{0,1},{1,0},{2,3},{3,2},{4,5},{5,4},{6,7},{7,6},{8,9},{9,8},{10,11... | collective-permute-start | bytes 196616 | tf_op jit(solution)/shard_map/ppermute | solution.py:359
  38.8 1.4 %collective-permute-start.12 = (bf16[256,128]{1,0:T(8,128)(2,1)S(1)}, bf16[256,128]{1,0:T(8,128)(2,1)S(1)}, u32[]{:S(2)}, u32[]{:S(2)}) collective-permute-start(bf16[256,128]{1,0:T(8,128)(2,1)S(1)} %get-tuple-element.80), channel_id=1, source_target_pairs={{0,1},{1,0},{2,3},{3,2},{4,5},{5,4},{6,7},{7,6},{8,9},{9,8},{10,11... | collective-permute-start | bytes 196616 | tf_op jit(solution)/shard_map/ppermute | solution.py:359

commit v4 on v3

--- a/solution.py
+++ b/solution.py
@@ -238,19 +238,13 @@
     by_parity(even, odd)
 
 
-def level_two(
-    order, tg, v_one, w_vg, near, far, w_far, p_far, p_v, n_h, w_h, w_n_h, p_n_h, w_vg_gap, tg_gap,
-    g, a0, a1, b,
-):
-    rows = order // 2
+def hand_out(right, left, a, b):
     left_of_two = lax.rem(lax.axis_index(AXES), 4) < 2
-
-    def hand_out(right, left):
-        first, second = jnp.where(left_of_two, right, left), jnp.where(left_of_two, left, right)
-        a0[...] = first[:rows]
-        a1[...] = first[rows:]
-        b[...] = second
-
+    a[...] = jnp.where(left_of_two, right, left)
+    b[...] = jnp.where(left_of_two, left, right)
+
+
+def level_two_even(order, tg, near, far, p_far, p_v, n_h, w_vg_gap, g, a, b):
     def even():
         t = tg[:, :order]
         whole = (n_h[...] + if_left(dot(t, w_vg_gap[:, order:]))).astype(BF16)
@@ -258,79 +252,105 @@
         value = (dot(near[...], whole) - dot(t, from_left)).astype(BF16)
         onward = (dot(p_v[...], from_left) - dot(p_far[...], whole)).astype(BF16)
         g[...] = value
-        hand_out(onward, value)
-
+        hand_out(onward, value, a, b)
+
+    by_parity(even, None)
+
+
+def level_two_odd(
+    order, v_one, w_vg, far, w_far, p_far, p_v, n_h, w_h, w_n_h, p_n_h, tg_gap, after, g, a, b
+):
     def odd():
         g_right, w_v = tg_gap[:, order:], w_vg[:, :order]
         own = w_h[...] - if_right(dot(w_v, g_right))
         from_right = if_right(dot(tg_gap[:, :order], own.astype(BF16))).astype(BF16)
 
         def whole(start, gap, further):
-            return (start[...] - if_right(dot(gap[...], g_right)) - dot(further, from_right)).astype(BF16)
+            gap_part = if_right(dot(gap[...], g_right)) + dot(further, from_right)
+            return (start[...] - gap_part).astype(BF16)
 
         g[...] = whole(n_h, far, v_one[...])
-        hand_out(whole(w_n_h, w_far, w_v), whole(p_n_h, p_far, p_v[...]))
-
-    by_parity(even, odd)
-
-
-def spikes_two(
-    order, tg, v_one, w_b, pair1, pair2, near, w_vg_gap, tg_gap, after, from_left, from_right, scale
-):
-    t = tg[:, :order]
-    index, count = lax.axis_index(AXES), lax.axis_size(AXES)
-
-    def put(left, right):
-        from_left[...] = jnp.where(index > 1, left, jnp.zeros_like(left)).astype(BF16)
-        from_right[...] = jnp.where(index < count - 2, right, jnp.zeros_like(right)).astype(BF16)
-
-    def even():
+        hand_out(whole(w_n_h, w_far, w_v), whole(p_n_h, p_far, p_v[...]), a, b)
+
+    by_parity(None, odd)
+
+
+def if_two_left(value):
+    return jnp.where(lax.axis_index(AXES) > 1, value, jnp.zeros_like(value))
+
+
+def if_two_right(value):
+    last = lax.axis_size(AXES) - 2
+    return jnp.where(lax.axis_index(AXES) < last, value, jnp.zeros_like(value))
+
+
+def spikes_two_even(order, tg, v_one, near, pair2, w_vg_gap, after, from_left, from_right, scale):
+    def even():
+        t = tg[:, :order]
         gap = if_left(dot(t, w_vg_gap[:, :order]))
         scale[...] = (near[...].astype(F32) - gap).astype(BF16)
         s_v = dot(scale[...], v_one[...]).astype(BF16)
-        put(-dot(scale[...], t), dot(s_v, pair2[:order, :]))
-
+        from_left[...] = if_two_left(-dot(scale[...], t)).astype(BF16)
+        from_right[...] = if_two_right(dot(s_v, pair2[:order, :])).astype(BF16)
+
+    by_parity(even, None)
+
+
+def spikes_two_odd(order, tg, v_one, w_b, near, pair1, tg_gap, after, from_left, from_right, scale):
     def odd():
         right = dot(tg_gap[:, :order], w_b[...]).astype(BF16)
         gap = if_right(dot(v_one[...], right))
         scale[...] = (near[...].astype(F32) - gap).astype(BF16)
-        s_t = dot(scale[...], t).astype(BF16)
-        put(dot(s_t, pair1[:order, :]), dot(scale[...], v_one[...]))
+        s_t = dot(scale[...], tg[:, :order]).astype(BF16)
+        from_left[...] = if_two_left(dot(s_t, pair1[:order, :])).astype(BF16)
+        from_right[...] = if_two_right(dot(scale[...], v_one[...])).astype(BF16)
+
+    by_parity(None, odd)
+
+
+def top_value(g, from_left, from_right, a, b, x):
+    def top(left, right):
+        change = dot(from_left[...], left[...]) + dot(from_right[...], right[...])
+        x[...] = (g[...].astype(F32) + change).astype(BF16)
+
+    left_of_two = lax.rem(lax.axis_index(AXES), 4) < 2
+    pl.when(left_of_two)(lambda: top(b, a))
+    pl.when(jnp.logical_not(left_of_two))(lambda: top(a, b))
+
+
+def top_even(g, from_left, from_right, a, b, after, x):
+    by_parity(lambda: top_value(g, from_left, from_right, a, b, x), None)
+
+
+def top_odd(g, from_left, from_right, a, b, x, *halves):
+    def odd():
+        top_value(g, from_left, from_right, a, b, x)
+        rows = halves[0].shape[0]
+        for i, half in enumerate(halves):
+            half[...] = x[i * rows : (i + 1) * rows, :]
+
+    by_parity(None, odd)
+
+
+def second_values(order, vg_b, w_b, x_even, x_odd, x_pair0, x_pair1, rest):
+    def even():
+        x_next = jnp.concatenate([x_pair0[...], x_pair1[...]], axis=0)
+        own = vg_b[:, order:].astype(F32) - dot(w_b[...], x_even[...])
+        rest[...] = own - dot(vg_b[:, :order], x_next)
+
+    def odd():
+        rest[...] = vg_b[:, order:].astype(F32) - dot(w_b[...], x_odd[...])
 
     by_parity(even, odd)
 
 
-def top_values(g, from_left, from_right, a0, a1, b, x, *halves):
-    def top(left, right):
-        change = dot(from_left[...], left) + dot(from_right[...], right)
-        x[...] = (g[...].astype(F32) + change).astype(BF16)
-
-    first = jnp.concatenate([a0[...], a1[...]], axis=0)
-    left_of_two = lax.rem(lax.axis_index(AXES), 4) < 2
-    pl.when(left_of_two)(lambda: top(b[...], first))
-    pl.when(jnp.logical_not(left_of_two))(lambda: top(first, b[...]))
-    rows = halves[0].shape[0]
-    for i, half in enumerate(halves):
-        half[...] = x[i * rows : (i + 1) * rows, :]
-
-
-def second_values(order, vg_b, w_b, x, x_pair0, x_pair1, rest):
-    rest[...] = vg_b[:, order:].astype(F32) - dot(w_b[...], x[...])
-
-    def even():
-        x_next = jnp.concatenate([x_pair0[...], x_pair1[...]], axis=0)
-        rest[...] -= dot(vg_b[:, :order], x_next)
-
-    by_parity(even, None)
-
-
-def finish(order, vg_b, x, rest, x_gap, out):
-    out[0] = x[...]
-
-    def even():
+def finish(order, vg_b, x_even, x_odd, rest, x_gap, out):
+    def even():
+        out[0] = x_even[...]
         out[1] = rest[...].astype(BF16)
 
     def odd():
+        out[0] = x_odd[...]
         out[1] = (rest[...] - if_right(dot(vg_b[:, :order], x_gap[...]))).astype(BF16)
 
     by_parity(even, odd)
@@ -338,9 +358,14 @@
 
 def exchanges(slab, count):
     pairs = [(i, i ^ 1) for i in range(count)]
-    twos = [(i, i ^ 2) for i in range(count)]
-    inner = range(2, count - 2)
-    other_twos = [(i, ((i - 2) ^ 2) + 2 if i in inner else i ^ 1) for i in range(count)]
+    twos, other_twos = [], []
+    for parity in (0, 1):
+        over = [i ^ slab for i in range(count)]
+        twos.append([(i, i ^ 2 if i % 2 == parity else over[i]) for i in range(count)])
+        to = [((i - 2) ^ 2) + 2 if i % 2 == parity else over[i] for i in range(count)]
+        for end in (parity, count - 2 + parity):
+            to[end], to[end ^ 1], to[over[end ^ 1]] = end ^ 1, over[end ^ 1], end
+        other_twos.append(list(enumerate(to)))
     after = [(i + 1) % count for i in range(count)]
     after[2], after[slab + 2], after[count - 1] = 0, 3, count - 5
     for first in range(slab + 3, count - 5, 4):
@@ -411,26 +436,41 @@
         [full] * 5 + [tall] * 4,
         [tg, v_one, w_b, to_pair[1], w_vg_odd, *pair], 6 * square,
     )
-    g_two, *to_two = local_call(
-        part(level_two, order),
-        [slim, flat, flat, slim], [tg, v_one, w_vg_odd, *known, w_vg_gap, tg_gap], 8 * thin,
-    )
-    by_two = [sent(to_two[0], twos), sent(to_two[1], twos), sent(to_two[2], other_twos)]
-    from_left, from_right = local_call(
-        part(spikes_two, order),
-        [full, full],
-        [tg, v_one, w_b, *pair[1:], known[0], w_vg_gap, tg_gap, g_two], 5 * square,
-        0, (block,),
-    )
-    x, *x_own = local_call(
-        top_values, [slim, flat, flat], [g_two, from_left, from_right, *by_two], 2 * thin
-    )
-    x_gap = sent(x, to_left)
+    near, far, w_far, p_far, p_v, n_h, w_h, w_n_h, p_n_h = known
+    g_even, a_even, b_even = local_call(
+        part(level_two_even, order),
+        [slim] * 3, [tg, near, far, p_far, p_v, n_h, w_vg_gap], 6 * thin,
+    )
+    even_a, even_b = sent(a_even, twos[0]), sent(b_even, other_twos[0])
+    left_even, right_even = local_call(
+        part(spikes_two_even, order),
+        [full, full], [tg, v_one, near, pair[2], w_vg_gap, a_even], 4 * square, 0, (block,),
+    )
+    g_odd, a_odd, b_odd = local_call(
+        part(level_two_odd, order),
+        [slim] * 3,
+        [v_one, w_vg_odd, far, w_far, p_far, p_v, n_h, w_h, w_n_h, p_n_h, tg_gap, left_even], 8 * thin,
+    )
+    odd_a, odd_b = sent(a_odd, twos[1]), sent(b_odd, other_twos[1])
+    left_odd, right_odd = local_call(
+        part(spikes_two_odd, order),
+        [full, full], [tg, v_one, w_b, near, pair[1], tg_gap, a_odd], 5 * square, 0, (block,),
+    )
+    x_even = local_call(
+        top_even, [slim], [g_even, left_even, right_even, even_a, even_b, left_odd], 2 * thin
+    )
+    x_gap = sent(x_even, to_left)
+    x_odd, *x_own = local_call(
+        top_odd,
+        [slim, flat, flat], [g_odd, left_odd, right_odd, odd_a, odd_b], 2 * thin,
+    )
     x_pair = [sent(piece, pairs) for piece in x_own]
-    rest = local_call(part(second_values, order), [tall], [vg_b, w_b, x, *x_pair], 2 * thin, weight=1)
+    rest = local_call(
+        part(second_values, order), [tall], [vg_b, w_b, x_even, x_odd, *x_pair], 2 * thin
+    )
     return local_call(
         part(finish, order),
-        [jax.ShapeDtypeStruct((2, order, rhs), BF16)], [vg_b, x, rest, x_gap], thin,
+        [jax.ShapeDtypeStruct((2, order, rhs), BF16)], [vg_b, x_even, x_odd, rest, x_gap], thin,
     )
 
 

time: 47.8 us -> 44.5 us (0.931)
  waiting for transfers between devices: 19 us -> 7.14 us
  starting transfers between devices: 12.6 us -> 21.3 us
    ppermute x14 -> x15, waiting for transfers between devices: 19 us -> 7.14 us  [sent(): return lax.ppermute(block, AXES, route)]
    ppermute x14 -> x15, starting transfers between devices: 12.6 us -> 21.3 us  [sent(): return lax.ppermute(block, AXES, route)]
    pallas_call x12 -> x15, Pallas kernels: 15.9 us -> 15.7 us  [local_call(): pl.pallas_call(kernel, out_shape=outs if many else outs[0], in_specs=[hbm...]
  transfers between devices with their start and end apart: 14 -> 15, of which waited for: 7 -> 5; matrix products, arithmetic and copies ran while one was open for 0% -> 0% of each run, Pallas kernels for 22% -> 28%
where the time goes in v4:
time: 44.5 us; the launch traced here: 44.3 us
  starting transfers between devices  21.3 us (48%)
  Pallas kernels  15.7 us (35%)
  waiting for transfers between devices  7.14 us (16%)
    ppermute x15, starting transfers between devices, sent(): return lax.ppermute(block, AXES, route)  21.3 us
    pallas_call x15, Pallas kernels, local_call(): pl.pallas_call(kernel, out_shape=outs if many else outs[0], in_specs=[hbm...  15.7 us
    ppermute x15, waiting for transfers between devices, sent(): return lax.ppermute(block, AXES, route)  7.14 us
  transfers between devices with their start and end apart: 15, of which 5 were waited for; matrix products, arithmetic and copies ran while one was open for 0% of the time, Pallas kernels for 28%

profile of v4, /device:TPU:29, one launch (start us, length us, event | category | flops | bytes accessed | tf_op | source)
XLA Modules:
  0.0 44.3 jit_solution(8097232058451865882)
XLA Ops:
  0.0 2.2 %shard_map.46.vg_odd = bf16[512,640]{1,0:T(8,128)(2,1)S(1)} custom-call(bf16[2,512,512]{2,1,0:T(8,128)(2,1)} %diag.3, bf16[2,512,512]{2,1,0:T(8,128)(2,1)} %upper.3, bf16[2,512,128]{2,1,0:T(8,128)(2,1)} %right.3), custom_call_target="tpu_custom_call" | custom-call | flops 335544 | tf_op jit(solution)/shard_map/pallas_call | solution.py:52
  2.2 0.1 collective-permute-start
  2.3 0.1 shard_map.47
  2.4 2.8 %collective-permute-start.1 = (bf16[512,384]{1,0:T(8,128)(2,1)S(1)}, bf16[512,384]{1,0:T(8,128)(2,1)S(1)}, u32[]{:S(2)}, u32[]{:S(2)}) collective-permute-start(bf16[512,384]{1,0:T(8,128)(2,1)S(1)} %get-tuple-element.51), channel_id=1, source_target_pairs={{0,1},{1,0},{2,3},{3,2},{4,5},{5,4},{6,7},{7,6},{8,9},{9,8},{10,11... | collective-permute-start | bytes 1179656 | tf_op jit(solution)/shard_map/ppermute | solution.py:384
  5.2 0.1 collective-permute-start.2
  5.3 3.6 %shard_map.48 = (bf16[512,512]{1,0:T(8,128)(2,1)S(1)}, bf16[512,512]{1,0:T(8,128)(2,1)S(1)}, f32[512,512]{1,0:T(8,128)S(1)}, bf16[512,512]{1,0:T(8,128)(2,1)S(1)}, f32[512,128]{1,0:T(8,128)S(1)}) custom-call(bf16[2,512,512]{2,1,0:T(8,128)(2,1)} %diag.3, bf16[2,512,512]{2,1,0:T(8,128)(2,1)} %lower.1, bf16[2,512,512]{2,1,0:T(8,128)(2,1)} %upper.3, ...), custom_call_target="tpu_custom_call" | custom-call | flops 1476395 | tf_op jit(solution)/shard_map/pallas_call | solution.py:52
  8.8 0.0 collective-permute-done.2.vg1
  8.8 0.0 collective-permute-done.1.v0
  8.8 2.2 %shard_map.49 = (bf16[512,640]{1,0:T(8,128)(2,1)S(1)}, bf16[512,512]{1,0:T(8,128)(2,1)S(1)}, bf16[512,640]{1,0:T(8,128)(2,1)S(1)}, bf16[560,512]{1,0:T(8,128)(2,...) custom-call(bf16[512,512]{1,0:T(8,128)(2,1)S(1)} %get-tuple-element.48.w_a, ...), custom_call_target="tpu_custom_call" | custom-call | flops 1342177 | tf_op jit(solution)/shard_map/pallas_call | solution.py:52
  11.0 0.1 collective-permute-start.6
  11.1 0.0 collective-permute-done.vg
  11.1 1.5 %collective-permute-start.9 = (bf16[512,640]{1,0:T(8,128)(2,1)S(1)}, bf16[512,640]{1,0:T(8,128)(2,1)S(1)}, u32[]{:S(2)}, u32[]{:S(2)}) collective-permute-start(bf16[512,640]{1,0:T(8,128)(2,1)S(1)} %get-tuple-element.56.tg), channel_id=1, source_target_pairs={{31,30},{30,29},{29,31},{28,27},{27,26},{26,25},{25,24},{24,23},{2... | collective-permute-start | bytes 1966088 | tf_op jit(solution)/shard_map/ppermute | solution.py:384
  12.7 1.3 %collective-permute-start.3 = (bf16[560,512]{1,0:T(8,128)(2,1)S(1)}, bf16[560,512]{1,0:T(8,128)(2,1)S(1)}, u32[]{:S(2)}, u32[]{:S(2)}) collective-permute-start(bf16[560,512]{1,0:T(8,128)(2,1)S(1)} %get-tuple-element.65), channel_id=1, source_target_pairs={{0,1},{1,0},{2,3},{3,2},{4,5},{5,4},{6,7},{7,6},{8,9},{9,8},{10,11... | collective-permute-start | bytes 1720328 | tf_op jit(solution)/shard_map/ppermute | solution.py:384
  14.0 0.1 collective-permute-start.4
  14.1 0.4 collective-permute-start.5
  14.5 2.7 %collective-permute-done.5.pair2 = bf16[544,512]{1,0:T(8,128)(2,1)S(1)} collective-permute-done((bf16[544,512]{1,0:T(8,128)(2,1)S(1)}, bf16[544,512]{1,0:T(8,128)(2,1)S(1)}, u32[]{:S(2)}, u32[]{:S(2)}) %collective-permute-start.5) | collective-permute-done | bytes 557088 | tf_op jit(solution)/shard_map/ppermute | solution.py:384
  17.2 0.0 collective-permute-done.3.pair0
  17.2 0.0 collective-permute-done.4.pair1
  17.2 2.6 %shard_map.52 = (bf16[512,512]{1,0:T(8,128)(2,1)S(1)}, bf16[512,512]{1,0:T(8,128)(2,1)S(1)}, bf16[512,512]{1,0:T(8,128)(2,1)S(1)}, bf16[512,512]{1,0:T(8,128)(2,...) custom-call(bf16[512,640]{1,0:T(8,128)(2,1)S(1)} %get-tuple-element., ...), custom_call_target="tpu_custom_call" | custom-call | flops 1610612 | tf_op jit(solution)/shard_map/pallas_call | solution.py:52
  19.8 0.0 collective-permute-done.6.w_vg_gap
  19.9 1.3 %collective-permute-start.7 = (bf16[512,128]{1,0:T(8,128)(2,1)S(1)}, bf16[512,128]{1,0:T(8,128)(2,1)S(1)}, u32[]{:S(2)}, u32[]{:S(2)}) collective-permute-start(bf16[512,128]{1,0:T(8,128)(2,1)S(1)} %get-tuple-element.73.after), channel_id=1, source_target_pairs={{0,2},{1,17},{2,0},{3,19},{4,6},{5,21},{6,4},{7,23},{8,10},{9,25},... | collective-permute-start | bytes 393224 | tf_op jit(solution)/shard_map/ppermute | solution.py:384
  21.1 2.9 %collective-permute-start.8 = (bf16[512,128]{1,0:T(8,128)(2,1)S(1)}, bf16[512,128]{1,0:T(8,128)(2,1)S(1)}, u32[]{:S(2)}, u32[]{:S(2)}) collective-permute-start(bf16[512,128]{1,0:T(8,128)(2,1)S(1)} %get-tuple-element.76), channel_id=1, source_target_pairs={{0,1},{1,17},{2,4},{3,19},{4,2},{5,21},{6,8},{7,23},{8,6},{9,25},{... | collective-permute-start | bytes 393224 | tf_op jit(solution)/shard_map/ppermute | solution.py:384
  24.1 1.3 %collective-permute-done.9.tg_gap = bf16[512,640]{1,0:T(8,128)(2,1)S(1)} collective-permute-done((bf16[512,640]{1,0:T(8,128)(2,1)S(1)}, bf16[512,640]{1,0:T(8,128)(2,1)S(1)}, u32[]{:S(2)}, u32[]{:S(2)}) %collective-permute-start.9) | collective-permute-done | bytes 655392 | tf_op jit(solution)/shard_map/ppermute | solution.py:384
  25.4 1.6 %shard_map.55 = (bf16[512,128]{1,0:T(8,128)(2,1)S(1)}, bf16[512,128]{1,0:T(8,128)(2,1)S(1)}, bf16[512,128]{1,0:T(8,128)(2,1)S(1)}) custom-call(bf16[512,512]{1,0:T(8,128)(2,1)S(1)} %get-tuple-element.62.v_one, bf16[512,640]{1,0:T(8,128)(2,1)S(1)} %get-tuple-element.64.w_vg, bf16[512,512]{1,0:T(8,128)(2,1)S(1)} %get-tuple-element.68.far, ...), custom_call_target="tpu_custom_call" | custom-call | flops 536870 | tf_op jit(solution)/shard_map/pallas_call | solution.py:52
  27.0 2.1 %collective-permute-start.10 = (bf16[512,128]{1,0:T(8,128)(2,1)S(1)}, bf16[512,128]{1,0:T(8,128)(2,1)S(1)}, u32[]{:S(2)}, u32[]{:S(2)}) collective-permute-start(bf16[512,128]{1,0:T(8,128)(2,1)S(1)} %get-tuple-element.81.after), channel_id=1, source_target_pairs={{0,16},{1,3},{2,18},{3,1},{4,20},{5,7},{6,22},{7,5},{8,24},{9,11},... | collective-permute-start | bytes 393224 | tf_op jit(solution)/shard_map/ppermute | solution.py:384
  29.1 2.7 %collective-permute-start.11 = (bf16[512,128]{1,0:T(8,128)(2,1)S(1)}, bf16[512,128]{1,0:T(8,128)(2,1)S(1)}, u32[]{:S(2)}, u32[]{:S(2)}) collective-permute-start(bf16[512,128]{1,0:T(8,128)(2,1)S(1)} %get-tuple-element.85), channel_id=1, source_target_pairs={{0,16},{1,0},{2,18},{3,5},{4,20},{5,3},{6,22},{7,9},{8,24},{9,7},{... | collective-permute-start | bytes 393224 | tf_op jit(solution)/shard_map/ppermute | solution.py:384
  31.8 1.6 %shard_map.56 = (bf16[512,512]{1,0:T(8,128)(2,1)S(1)}, bf16[512,512]{1,0:T(8,128)(2,1)S(1)}) custom-call(bf16[512,640]{1,0:T(8,128)(2,1)S(1)} %get-tuple-element.56.tg, bf16[512,512]{1,0:T(8,128)(2,1)S(1)} %get-tuple-element.62.v_one, bf16[512,512]{1,0:T(8,128)(2,1)S(1)} %get-tuple-element.54.w_b, bf16[512,512]{1,0:T(8,128)(2,1)S(1)} %get-tuple-element.67.near, ...), custom_call_target="tpu_custom_call" | custom-call | flops 1342177 | tf_op jit(solution)/shard_map/pallas_call | solution.py:52
  33.4 0.0 collective-permute-done.7.a
  33.4 0.0 collective-permute-done.8.b
  33.5 5.4 %collective-permute-start.14 = (bf16[512,128]{1,0:T(8,128)(2,1)S(1)}, bf16[512,128]{1,0:T(8,128)(2,1)S(1)}, u32[]{:S(2)}, u32[]{:S(2)}) collective-permute-start(bf16[512,128]{1,0:T(8,128)(2,1)S(1)} %shard_map.57.x_even), channel_id=1, source_target_pairs={{31,30},{30,29},{29,31},{28,27},{27,26},{26,25},{25,24},{24,23},{2... | collective-permute-start | bytes 393224 | tf_op jit(solution)/shard_map/ppermute | solution.py:384
  38.9 0.0 collective-permute-done.10.a
  38.9 0.0 collective-permute-done.11.b
  38.9 0.4 %shard_map.58 = (bf16[512,128]{1,0:T(8,128)(2,1)S(1)}, bf16[256,128]{1,0:T(8,128)(2,1)S(1)}, bf16[256,128]{1,0:T(8,128)(2,1)S(1)}) custom-call(bf16[512,128]{1,0:T(8,128)(2,1)S(1)} %get-tuple-element.83.g, bf16[512,512]{1,0:T(8,128)(2,1)S(1)} %get-tuple-element.82.after.from_left, bf16[512,512]{1,0:T(8,128)(2,1)S(1)} %get-tuple-element.84.from_right, ...), custom_call_target="tpu_custom_call" | custom-call | flops 134217 | tf_op jit(solution)/shard_map/pallas_call | solution.py:52
  39.3 0.1 collective-permute-start.12
  39.4 0.5 %collective-permute-start.13 = (bf16[256,128]{1,0:T(8,128)(2,1)S(1)}, bf16[256,128]{1,0:T(8,128)(2,1)S(1)}, u32[]{:S(2)}, u32[]{:S(2)}) collective-permute-start(bf16[256,128]{1,0:T(8,128)(2,1)S(1)} %get-tuple-element.88), channel_id=1, source_target_pairs={{0,1},{1,0},{2,3},{3,2},{4,5},{5,4},{6,7},{7,6},{8,9},{9,8},{10,11... | collective-permute-start | bytes 196616 | tf_op jit(solution)/shard_map/ppermute | solution.py:384
  39.9 0.7 %collective-permute-done.12.x_pair0 = bf16[256,128]{1,0:T(8,128)(2,1)S(1)} collective-permute-done((bf16[256,128]{1,0:T(8,128)(2,1)S(1)}, bf16[256,128]{1,0:T(8,128)(2,1)S(1)}, u32[]{:S(2)}, u32[]{:S(2)}) %collective-permute-start.12) | collective-permute-done | bytes 65568 | tf_op jit(solution)/shard_map/ppermute | solution.py:384
  40.7 0.2 collective-permute-done.13.x_pair1
  40.8 0.3 shard_map.59.rest
  41.1 2.2 %collective-permute-done.14.x_gap = bf16[512,128]{1,0:T(8,128)(2,1)S(1)} collective-permute-done((bf16[512,128]{1,0:T(8,128)(2,1)S(1)}, bf16[512,128]{1,0:T(8,128)(2,1)S(1)}, u32[]{:S(2)}, u32[]{:S(2)}) %collective-permute-start.14) | collective-permute-done | bytes 131104 | tf_op jit(solution)/shard_map/ppermute | solution.py:384
  43.3 1.0 %shard_map.60 = bf16[2,512,128]{2,1,0:T(8,128)(2,1)} custom-call(bf16[512,640]{1,0:T(8,128)(2,1)S(1)} %get-tuple-element.47.vg_b, bf16[512,128]{1,0:T(8,128)(2,1)S(1)} %shard_map.57.x_even, bf16[512,128]{1,0:T(8,128)(2,1)S(1)} %get-tuple-element.86.x_odd, f32[512,128]{1,0:T(8,128)S(1)} %shard_map.59.rest, bf16[512,128]{1,0:T(8,128)(2,1)S(1)} %collective-permute-done.14.x_gap), custom_call_target="tpu_custom_call" | custom-call | flops 67108 | tf_op jit(solution)/shard_map/pallas_call | solution.py:52
  (5 shorter events, 0.1 us)
Async XLA Ops:
  2.2 8.9 %collective-permute-start = (bf16[512,640]{1,0:T(8,128)(2,1)S(1)}, bf16[512,640]{1,0:T(8,128)(2,1)S(1)}, u32[]{:S(2)}, u32[]{:S(2)}) collective-permute-start(bf16[512,640]{1,0:T(8,128)(2,1)S(1)} %shard_map.46.vg_odd), channel_id=1, source_target_pairs={{0,1},{1,2},{2,0},{3,4},{4,5},{5,6},{6,7},{7,8},{8,9},{9,10},{10,1... | collective-permute-start | bytes 1966088 | tf_op jit(solution)/shard_map/ppermute | solution.py:384
  2.4 6.4 %collective-permute-start.1 = (bf16[512,384]{1,0:T(8,128)(2,1)S(1)}, bf16[512,384]{1,0:T(8,128)(2,1)S(1)}, u32[]{:S(2)}, u32[]{:S(2)}) collective-permute-start(bf16[512,384]{1,0:T(8,128)(2,1)S(1)} %get-tuple-element.51), channel_id=1, source_target_pairs={{0,1},{1,0},{2,3},{3,2},{4,5},{5,4},{6,7},{7,6},{8,9},{9,8},{10,11... | collective-permute-start | bytes 1179656 | tf_op jit(solution)/shard_map/ppermute | solution.py:384
  5.2 3.6 %collective-permute-start.2 = (bf16[512,256]{1,0:T(8,128)(2,1)S(1)}, bf16[512,256]{1,0:T(8,128)(2,1)S(1)}, u32[]{:S(2)}, u32[]{:S(2)}) collective-permute-start(bf16[512,256]{1,0:T(8,128)(2,1)S(1)} %get-tuple-element.52), channel_id=1, source_target_pairs={{0,1},{1,0},{2,3},{3,2},{4,5},{5,4},{6,7},{7,6},{8,9},{9,8},{10,11... | collective-permute-start | bytes 786440 | tf_op jit(solution)/shard_map/ppermute | solution.py:384
  11.0 8.8 %collective-permute-start.6 = (bf16[512,640]{1,0:T(8,128)(2,1)S(1)}, bf16[512,640]{1,0:T(8,128)(2,1)S(1)}, u32[]{:S(2)}, u32[]{:S(2)}) collective-permute-start(bf16[512,640]{1,0:T(8,128)(2,1)S(1)} %get-tuple-element.64.w_vg), channel_id=1, source_target_pairs={{0,1},{1,2},{2,0},{3,4},{4,5},{5,6},{6,7},{7,8},{8,9},{9,10},{10,1... | collective-permute-start | bytes 1966088 | tf_op jit(solution)/shard_map/ppermute | solution.py:384
  11.1 14.2 %collective-permute-start.9 = (bf16[512,640]{1,0:T(8,128)(2,1)S(1)}, bf16[512,640]{1,0:T(8,128)(2,1)S(1)}, u32[]{:S(2)}, u32[]{:S(2)}) collective-permute-start(bf16[512,640]{1,0:T(8,128)(2,1)S(1)} %get-tuple-element.56.tg), channel_id=1, source_target_pairs={{31,30},{30,29},{29,31},{28,27},{27,26},{26,25},{25,24},{24,23},{2... | collective-permute-start | bytes 1966088 | tf_op jit(solution)/shard_map/ppermute | solution.py:384
  12.7 4.5 %collective-permute-start.3 = (bf16[560,512]{1,0:T(8,128)(2,1)S(1)}, bf16[560,512]{1,0:T(8,128)(2,1)S(1)}, u32[]{:S(2)}, u32[]{:S(2)}) collective-permute-start(bf16[560,512]{1,0:T(8,128)(2,1)S(1)} %get-tuple-element.65), channel_id=1, source_target_pairs={{0,1},{1,0},{2,3},{3,2},{4,5},{5,4},{6,7},{7,6},{8,9},{9,8},{10,11... | collective-permute-start | bytes 1720328 | tf_op jit(solution)/shard_map/ppermute | solution.py:384
  14.0 3.2 %collective-permute-start.4 = (bf16[560,512]{1,0:T(8,128)(2,1)S(1)}, bf16[560,512]{1,0:T(8,128)(2,1)S(1)}, u32[]{:S(2)}, u32[]{:S(2)}) collective-permute-start(bf16[560,512]{1,0:T(8,128)(2,1)S(1)} %get-tuple-element.63.to_pair1), channel_id=1, source_target_pairs={{0,1},{1,0},{2,3},{3,2},{4,5},{5,4},{6,7},{7,6},{8,9},{9,8},{10,11... | collective-permute-start | bytes 1720328 | tf_op jit(solution)/shard_map/ppermute | solution.py:384
  14.1 3.1 %collective-permute-start.5 = (bf16[544,512]{1,0:T(8,128)(2,1)S(1)}, bf16[544,512]{1,0:T(8,128)(2,1)S(1)}, u32[]{:S(2)}, u32[]{:S(2)}) collective-permute-start(bf16[544,512]{1,0:T(8,128)(2,1)S(1)} %get-tuple-element.66), channel_id=1, source_target_pairs={{0,1},{1,0},{2,3},{3,2},{4,5},{5,4},{6,7},{7,6},{8,9},{9,8},{10,11... | collective-permute-start | bytes 1671176 | tf_op jit(solution)/shard_map/ppermute | solution.py:384
  19.9 13.6 %collective-permute-start.7 = (bf16[512,128]{1,0:T(8,128)(2,1)S(1)}, bf16[512,128]{1,0:T(8,128)(2,1)S(1)}, u32[]{:S(2)}, u32[]{:S(2)}) collective-permute-start(bf16[512,128]{1,0:T(8,128)(2,1)S(1)} %get-tuple-element.73.after), channel_id=1, source_target_pairs={{0,2},{1,17},{2,0},{3,19},{4,6},{5,21},{6,4},{7,23},{8,10},{9,25},... | collective-permute-start | bytes 393224 | tf_op jit(solution)/shard_map/ppermute | solution.py:384
  21.1 12.3 %collective-permute-start.8 = (bf16[512,128]{1,0:T(8,128)(2,1)S(1)}, bf16[512,128]{1,0:T(8,128)(2,1)S(1)}, u32[]{:S(2)}, u32[]{:S(2)}) collective-permute-start(bf16[512,128]{1,0:T(8,128)(2,1)S(1)} %get-tuple-element.76), channel_id=1, source_target_pairs={{0,1},{1,17},{2,4},{3,19},{4,2},{5,21},{6,8},{7,23},{8,6},{9,25},{... | collective-permute-start | bytes 393224 | tf_op jit(solution)/shard_map/ppermute | solution.py:384
  27.0 11.9 %collective-permute-start.10 = (bf16[512,128]{1,0:T(8,128)(2,1)S(1)}, bf16[512,128]{1,0:T(8,128)(2,1)S(1)}, u32[]{:S(2)}, u32[]{:S(2)}) collective-permute-start(bf16[512,128]{1,0:T(8,128)(2,1)S(1)} %get-tuple-element.81.after), channel_id=1, source_target_pairs={{0,16},{1,3},{2,18},{3,1},{4,20},{5,7},{6,22},{7,5},{8,24},{9,11},... | collective-permute-start | bytes 393224 | tf_op jit(solution)/shard_map/ppermute | solution.py:384
  29.1 9.8 %collective-permute-start.11 = (bf16[512,128]{1,0:T(8,128)(2,1)S(1)}, bf16[512,128]{1,0:T(8,128)(2,1)S(1)}, u32[]{:S(2)}, u32[]{:S(2)}) collective-permute-start(bf16[512,128]{1,0:T(8,128)(2,1)S(1)} %get-tuple-element.85), channel_id=1, source_target_pairs={{0,16},{1,0},{2,18},{3,5},{4,20},{5,3},{6,22},{7,9},{8,24},{9,7},{... | collective-permute-start | bytes 393224 | tf_op jit(solution)/shard_map/ppermute | solution.py:384
  33.5 9.8 %collective-permute-start.14 = (bf16[512,128]{1,0:T(8,128)(2,1)S(1)}, bf16[512,128]{1,0:T(8,128)(2,1)S(1)}, u32[]{:S(2)}, u32[]{:S(2)}) collective-permute-start(bf16[512,128]{1,0:T(8,128)(2,1)S(1)} %shard_map.57.x_even), channel_id=1, source_target_pairs={{31,30},{30,29},{29,31},{28,27},{27,26},{26,25},{25,24},{24,23},{2... | collective-permute-start | bytes 393224 | tf_op jit(solution)/shard_map/ppermute | solution.py:384
  39.3 1.3 %collective-permute-start.12 = (bf16[256,128]{1,0:T(8,128)(2,1)S(1)}, bf16[256,128]{1,0:T(8,128)(2,1)S(1)}, u32[]{:S(2)}, u32[]{:S(2)}) collective-permute-start(bf16[256,128]{1,0:T(8,128)(2,1)S(1)} %get-tuple-element.87), channel_id=1, source_target_pairs={{0,1},{1,0},{2,3},{3,2},{4,5},{5,4},{6,7},{7,6},{8,9},{9,8},{10,11... | collective-permute-start | bytes 196616 | tf_op jit(solution)/shard_map/ppermute | solution.py:384
  39.4 1.4 %collective-permute-start.13 = (bf16[256,128]{1,0:T(8,128)(2,1)S(1)}, bf16[256,128]{1,0:T(8,128)(2,1)S(1)}, u32[]{:S(2)}, u32[]{:S(2)}) collective-permute-start(bf16[256,128]{1,0:T(8,128)(2,1)S(1)} %get-tuple-element.88), channel_id=1, source_target_pairs={{0,1},{1,0},{2,3},{3,2},{4,5},{5,4},{6,7},{7,6},{8,9},{9,8},{10,11... | collective-permute-start | bytes 196616 | tf_op jit(solution)/shard_map/ppermute | solution.py:384

commit v5 on v4

--- a/solution.py
+++ b/solution.py
@@ -90,7 +90,7 @@
     by_parity(None, lambda: load_row(order, *refs))
 
 
-def second_row(order, diag, upper, right, vg_odd, vg_b, *rest):
+def second_row(order, diag, upper, right, vg_odd, after, vg_b, *rest):
     *pieces, diag_b, upper_b, right_b, sems = rest
 
     def odd():
@@ -106,29 +106,63 @@
     by_parity(even, odd)
 
 
-def own_products(
-    order, diag, lower, upper, right, vg_b, w_a, w_b, m, n, r,
-    diag_a, lower_a, upper_a, right_a, diag_b, lower_b, sems,
+def own_products_odd(
+    order, diag, lower, upper, right, vg_odd, w_a, w_b, m, n, r, v_a, diag_a, lower_a, diag_b, lower_b,
+    upper_a, right_a, sems,
 ):
-    d_a = fetch(diag.at[0], diag_a, sems.at[0])
-    u_a = fetch(upper.at[0], upper_a, sems.at[1])
-    d_b = fetch(diag.at[1], diag_b, sems.at[2])
-    l_b = fetch(lower.at[1], lower_b, sems.at[3])
-    l_a = fetch(lower.at[0], lower_a, sems.at[4])
-    r_a = fetch(right.at[0], right_a, sems.at[5])
-    d_a.wait()
-    u_a.wait()
-    v_a = dot(diag_a[...], upper_a[...]).astype(BF16)
-    d_b.wait()
-    l_b.wait()
+    def odd():
+        held = diag_a, lower_a, diag_b, lower_b, upper_a, right_a
+        first_right_side(order, own_copies(diag, lower, upper, right, *held, sems), vg_odd, held, v_a, r)
+        spikes_own(order, vg_odd, diag_a, lower_a, diag_b, lower_b, v_a, w_a, w_b, m, n)
+
+    by_parity(None, odd)
+
+
+def own_products_even(order, diag, lower, upper, right, vg_b, *rest):
+    r, v_a, diag_a, lower_a, diag_b, lower_b, upper_a, right_a, sems = rest[6:]
+
+    def even():
+        held = diag_a, lower_a, diag_b, lower_b, upper_a, right_a
+        first_right_side(order, own_copies(diag, lower, upper, right, *held, sems), vg_b, held, v_a, r)
+
+    by_parity(even, None)
+
+
+def spikes_own_even(order, vg_b, diag_a, lower_a, diag_b, lower_b, v_a, after, *rest):
+    w_a, w_b, m, n = rest[4:]
+
+    def even():
+        spikes_own(order, vg_b, diag_a, lower_a, diag_b, lower_b, v_a, w_a, w_b, m, n)
+
+    by_parity(even, None)
+
+
+def own_copies(diag, lower, upper, right, diag_a, lower_a, diag_b, lower_b, upper_a, right_a, sems):
+    pairs = (
+        (diag.at[0], diag_a), (upper.at[0], upper_a), (right.at[0], right_a),
+        (diag.at[1], diag_b), (lower.at[1], lower_b), (lower.at[0], lower_a),
+    )
+    return [pltpu.make_async_copy(x, y, sems.at[i]) for i, (x, y) in enumerate(pairs)]
+
+
+def first_right_side(order, copies, vg_b, held, v_a, r):
+    diag_a, lower_a, diag_b, lower_b, upper_a, right_a = held
+    for copy in copies:
+        copy.start()
+    for copy in copies[:3]:
+        copy.wait()
+    v_a[...] = dot(diag_a[...], upper_a[...]).astype(BF16)
+    g_a = dot(diag_a[...], right_a[...]).astype(BF16)
+    r[...] = g_a.astype(F32) - dot(v_a[...], vg_b[:, order:])
+    for copy in copies[3:]:
+        copy.wait()
+
+
+def spikes_own(order, vg_b, diag_a, lower_a, diag_b, lower_b, v_a, w_a, w_b, m, n):
     w_b[...] = dot(diag_b[...], lower_b[...]).astype(BF16)
-    l_a.wait()
     w_a[...] = dot(diag_a[...], lower_a[...]).astype(BF16)
-    r_a.wait()
-    g_a = dot(diag_a[...], right_a[...]).astype(BF16)
-    n[...] = dot(v_a, vg_b[:, :order]).astype(BF16)
-    r[...] = g_a.astype(F32) - dot(v_a, vg_b[:, order:])
-    m[...] = dot(v_a, w_b[...])
+    n[...] = dot(v_a[...], vg_b[:, :order]).astype(BF16)
+    m[...] = dot(v_a[...], w_b[...])
 
 
 def scale_one(order, w_a, m, r, v_left, g_left, scale, tg):
@@ -196,7 +230,7 @@
     by_parity(lambda: scale_one(order, w_a, m, r, v_left, g_left, scale, tg), None)
 
 
-def spikes_one_even(order, scale, n, w_b, tg, v_odd, pair0, pair1, pair2, v_one, *rest):
+def spikes_one_even(order, scale, n, w_b, tg, v_odd, pair0, pair1, pair2, tg_out, v_one, *rest):
     *to_pair, w_t, w_v, w_g = rest
 
     def even():
@@ -397,20 +431,28 @@
         part(second_row_odd, order), [wide], [diag, upper, right], square + thin, 3, row_scratch
     )
     vg_gap = sent(vg_odd, to_right)
+    own_arrays = [f32_array(order, rhs)] + [full] * 5
+    spike_arrays = [full, full, f32_array(order, order), full]
+    own_scratch = (block, side, pltpu.SemaphoreType.DMA((6,)))
+    spikes = local_call(
+        part(own_products_odd, order),
+        spike_arrays + own_arrays, [diag, lower, upper, right, vg_odd], 5 * square + 2 * thin,
+        4, own_scratch,
+    )
+    spikes, own = spikes[:4], spikes[4:]
     cut = 3 * order // 4
     vg_b, *to_pair = local_call(
         part(second_row, order),
         [wide, bf16_array(order, cut), bf16_array(order, order - cut + rhs)],
-        [diag, upper, right, vg_odd], square + thin, 3, row_scratch,
+        [diag, upper, right, vg_odd, own[0]], square + thin, 3, row_scratch,
     )
     vg_pair = [sent(piece, pairs) for piece in to_pair]
-    w_a, w_b, m, n, r = local_call(
-        part(own_products, order),
-        [full, full, f32_array(order, order), full, f32_array(order, rhs)],
-        [diag, lower, upper, right, vg_b], 5 * square + 2 * thin, 4,
-        (block, block, block, side, block, block, pltpu.SemaphoreType.DMA((6,))),
-    )
-
+    r, v_a, *held = local_call(
+        part(own_products_even, order),
+        own_arrays, [diag, lower, upper, right, vg_b, *own], square + 2 * thin,
+        4, own_scratch, {5 + i: i for i in range(6)},
+    )
+    w_a, w_b, m, n = spikes
     extra = rhs // 16 * 6
     shares = [bf16_array(order + rows, order) for rows in (extra, extra, rhs - 2 * extra)]
     tg_odd, v_odd, w_vg_odd, *to_pair = local_call(
@@ -418,16 +460,21 @@
         [wide, full, wide, *shares], [w_a, m, r, *vg_pair, n, w_b], 5 * square, 0, (block, block),
     )
     w_vg_gap = sent(w_vg_odd, to_right)
+    w_a, w_b, m, n = local_call(
+        part(spikes_own_even, order),
+        spike_arrays, [vg_b, *held, v_a, vg_gap, *spikes], 4 * square,
+        aliases={7 + i: i for i in range(4)},
+    )
     tg, scale = local_call(
         part(scale_one_even, order),
         [wide, full], [w_a, m, r, vg_gap, tg_odd], 2 * square + 2 * thin, aliases={4: 0},
     )
+    tg, v_one, *to_pair = local_call(
+        part(spikes_one_even, order),
+        [wide, full, *shares], [scale, n, w_b, tg, v_odd, *to_pair], 3 * square + thin,
+        0, (block, block, side), {3: 0, 4: 1, 5: 2, 6: 3, 7: 4},
+    )
     tg_gap = sent(tg, to_left)
-    v_one, *to_pair = local_call(
-        part(spikes_one_even, order),
-        [full, *shares], [scale, n, w_b, tg, v_odd, *to_pair], 3 * square + thin,
-        0, (block, block, side), {4: 0, 5: 1, 6: 2, 7: 3},
-    )
     pair = [sent(piece, pairs) for piece in to_pair]
 
     tall, flat = f32_array(order, rhs), bf16_array(order // 2, rhs)

time: 44.5 us -> 42.8 us (0.962)
  starting transfers between devices: 21.3 us -> 11.1 us
  waiting for transfers between devices: 7.14 us -> 15.6 us
    ppermute x15, starting transfers between devices: 21.3 us -> 11.1 us  [sent(): return lax.ppermute(block, AXES, route)]
    ppermute x15, waiting for transfers between devices: 7.14 us -> 15.6 us  [sent(): return lax.ppermute(block, AXES, route)]
    pallas_call x15 -> x17, Pallas kernels: 15.7 us -> 15.6 us  [local_call(): pl.pallas_call(kernel, out_shape=outs if many else outs[0], in_specs=[hbm...]
  transfers between devices with their start and end apart: 15 -> 15, of which waited for: 5 -> 7; matrix products, arithmetic and copies ran while one was open for 0% -> 0% of each run, Pallas kernels for 28% -> 29%
where the time goes in v5:
time: 42.8 us; the launch traced here: 42.5 us
  Pallas kernels  15.6 us (36%)
  waiting for transfers between devices  15.6 us (36%)
  starting transfers between devices  11.1 us (26%)
    pallas_call x17, Pallas kernels, local_call(): pl.pallas_call(kernel, out_shape=outs if many else outs[0], in_specs=[hbm...  15.6 us
    ppermute x15, waiting for transfers between devices, sent(): return lax.ppermute(block, AXES, route)  15.6 us
    ppermute x15, starting transfers between devices, sent(): return lax.ppermute(block, AXES, route)  11.1 us
  transfers between devices with their start and end apart: 15, of which 7 were waited for; matrix products, arithmetic and copies ran while one was open for 0% of the time, Pallas kernels for 29%

profile of v5, /device:TPU:29, one launch (start us, length us, event | category | flops | bytes accessed | tf_op | source)
XLA Modules:
  0.0 42.5 jit_solution(8274410985339340879)
XLA Ops:
  0.0 2.2 %shard_map.46.vg_odd = bf16[512,640]{1,0:T(8,128)(2,1)S(1)} custom-call(bf16[2,512,512]{2,1,0:T(8,128)(2,1)} %diag.5, bf16[2,512,512]{2,1,0:T(8,128)(2,1)} %upper.5, bf16[2,512,128]{2,1,0:T(8,128)(2,1)} %right.5), custom_call_target="tpu_custom_call" | custom-call | flops 335544 | tf_op jit(solution)/shard_map/pallas_call | solution.py:52
  2.2 0.1 collective-permute-start
  2.3 3.3 %shard_map.47 = (bf16[512,512]{1,0:T(8,128)(2,1)S(1)}, bf16[512,512]{1,0:T(8,128)(2,1)S(1)}, f32[512,512]{1,0:T(8,128)S(1)}, bf16[512,512]{1,0:T(8,128)(2,1)S(1)...) custom-call(bf16[2,512,512]{2,1,0:T(8,128)(2,1)} %diag.5, ...), custom_call_target="tpu_custom_call" | custom-call | flops 1476395 | tf_op jit(solution)/shard_map/pallas_call | solution.py:52
  5.6 0.1 shard_map.48
  5.7 0.1 collective-permute-start.1
  5.8 0.5 %collective-permute-start.2 = (bf16[512,256]{1,0:T(8,128)(2,1)S(1)}, bf16[512,256]{1,0:T(8,128)(2,1)S(1)}, u32[]{:S(2)}, u32[]{:S(2)}) collective-permute-start(bf16[512,256]{1,0:T(8,128)(2,1)S(1)} %get-tuple-element.83), channel_id=1, source_target_pairs={{0,1},{1,0},{2,3},{3,2},{4,5},{5,4},{6,7},{7,6},{8,9},{9,8},{10,11... | collective-permute-start | bytes 786440 | tf_op jit(solution)/shard_map/ppermute | solution.py:418
  6.3 0.1 shard_map.49
  6.3 1.5 %collective-permute-done.2.vg1 = bf16[512,256]{1,0:T(8,128)(2,1)S(1)} collective-permute-done((bf16[512,256]{1,0:T(8,128)(2,1)S(1)}, bf16[512,256]{1,0:T(8,128)(2,1)S(1)}, u32[]{:S(2)}, u32[]{:S(2)}) %collective-permute-start.2) | collective-permute-done | bytes 262176 | tf_op jit(solution)/shard_map/ppermute | solution.py:418
  7.8 0.0 collective-permute-done.1.v0
  7.8 2.2 %shard_map.51 = (bf16[512,640]{1,0:T(8,128)(2,1)S(1)}, bf16[512,512]{1,0:T(8,128)(2,1)S(1)}, bf16[512,640]{1,0:T(8,128)(2,1)S(1)}, bf16[560,512]{1,0:T(8,128)(2,...) custom-call(bf16[512,512]{1,0:T(8,128)(2,1)S(1)} %get-tuple-element.75.rest_0_.w_a, ...), custom_call_target="tpu_custom_call" | custom-call | flops 1342177 | tf_op jit(solution)/shard_map/pallas_call | solution.py:52
  10.0 0.1 collective-permute-start.6
  10.1 0.0 collective-permute-done.after.vg
  10.2 4.6 %collective-permute-start.9 = (bf16[512,640]{1,0:T(8,128)(2,1)S(1)}, bf16[512,640]{1,0:T(8,128)(2,1)S(1)}, u32[]{:S(2)}, u32[]{:S(2)}) collective-permute-start(bf16[512,640]{1,0:T(8,128)(2,1)S(1)} %get-tuple-element.93.tg), channel_id=1, source_target_pairs={{31,30},{30,29},{29,31},{28,27},{27,26},{26,25},{25,24},{24,23},{2... | collective-permute-start | bytes 1966088 | tf_op jit(solution)/shard_map/ppermute | solution.py:418
  14.8 0.1 collective-permute-start.3
  14.8 0.4 %collective-permute-start.4 = (bf16[560,512]{1,0:T(8,128)(2,1)S(1)}, bf16[560,512]{1,0:T(8,128)(2,1)S(1)}, u32[]{:S(2)}, u32[]{:S(2)}) collective-permute-start(bf16[560,512]{1,0:T(8,128)(2,1)S(1)} %get-tuple-element.95.to_pair1), channel_id=1, source_target_pairs={{0,1},{1,0},{2,3},{3,2},{4,5},{5,4},{6,7},{7,6},{8,9},{9,8},{10,11... | collective-permute-start | bytes 1720328 | tf_op jit(solution)/shard_map/ppermute | solution.py:418
  15.3 0.1 collective-permute-start.5
  15.3 3.6 %collective-permute-done.5.pair2 = bf16[544,512]{1,0:T(8,128)(2,1)S(1)} collective-permute-done((bf16[544,512]{1,0:T(8,128)(2,1)S(1)}, bf16[544,512]{1,0:T(8,128)(2,1)S(1)}, u32[]{:S(2)}, u32[]{:S(2)}) %collective-permute-start.5) | collective-permute-done | bytes 557088 | tf_op jit(solution)/shard_map/ppermute | solution.py:418
  18.9 0.0 collective-permute-done.3.pair0
  18.9 0.0 collective-permute-done.4.pair1
  18.9 2.6 %shard_map.54 = (bf16[512,512]{1,0:T(8,128)(2,1)S(1)}, bf16[512,512]{1,0:T(8,128)(2,1)S(1)}, bf16[512,512]{1,0:T(8,128)(2,1)S(1)}, bf16[512,512]{1,0:T(8,128)(2,...) custom-call(bf16[512,640]{1,0:T(8,128)(2,1)S(1)} %get-tuple-element., ...), custom_call_target="tpu_custom_call" | custom-call | flops 1610612 | tf_op jit(solution)/shard_map/pallas_call | solution.py:52
  21.5 0.0 collective-permute-done.6.w_vg_gap
  21.6 0.2 shard_map.55
  21.8 2.3 %collective-permute-start.8 = (bf16[512,128]{1,0:T(8,128)(2,1)S(1)}, bf16[512,128]{1,0:T(8,128)(2,1)S(1)}, u32[]{:S(2)}, u32[]{:S(2)}) collective-permute-start(bf16[512,128]{1,0:T(8,128)(2,1)S(1)} %get-tuple-element.108), channel_id=1, source_target_pairs={{0,1},{1,17},{2,4},{3,19},{4,2},{5,21},{6,8},{7,23},{8,6},{9,25},{... | collective-permute-start | bytes 393224 | tf_op jit(solution)/shard_map/ppermute | solution.py:418
  24.1 0.0 collective-permute-start.7
  24.1 3.8 %collective-permute-done.9.tg_gap = bf16[512,640]{1,0:T(8,128)(2,1)S(1)} collective-permute-done((bf16[512,640]{1,0:T(8,128)(2,1)S(1)}, bf16[512,640]{1,0:T(8,128)(2,1)S(1)}, u32[]{:S(2)}, u32[]{:S(2)}) %collective-permute-start.9) | collective-permute-done | bytes 655392 | tf_op jit(solution)/shard_map/ppermute | solution.py:418
  27.9 1.6 %shard_map.57 = (bf16[512,128]{1,0:T(8,128)(2,1)S(1)}, bf16[512,128]{1,0:T(8,128)(2,1)S(1)}, bf16[512,128]{1,0:T(8,128)(2,1)S(1)}) custom-call(bf16[512,512]{1,0:T(8,128)(2,1)S(1)} %get-tuple-element.94.v_one, bf16[512,640]{1,0:T(8,128)(2,1)S(1)} %get-tuple-element.96.w_vg, bf16[512,512]{1,0:T(8,128)(2,1)S(1)} %get-tuple-element.100.far, ...), custom_call_target="tpu_custom_call" | custom-call | flops 536870 | tf_op jit(solution)/shard_map/pallas_call | solution.py:52
  29.5 2.3 %collective-permute-start.11 = (bf16[512,128]{1,0:T(8,128)(2,1)S(1)}, bf16[512,128]{1,0:T(8,128)(2,1)S(1)}, u32[]{:S(2)}, u32[]{:S(2)}) collective-permute-start(bf16[512,128]{1,0:T(8,128)(2,1)S(1)} %get-tuple-element.117), channel_id=1, source_target_pairs={{0,16},{1,0},{2,18},{3,5},{4,20},{5,3},{6,22},{7,9},{8,24},{9,7},{... | collective-permute-start | bytes 393224 | tf_op jit(solution)/shard_map/ppermute | solution.py:418
  31.8 0.0 collective-permute-start.10
  31.8 1.6 %shard_map.58 = (bf16[512,512]{1,0:T(8,128)(2,1)S(1)}, bf16[512,512]{1,0:T(8,128)(2,1)S(1)}) custom-call(bf16[512,640]{1,0:T(8,128)(2,1)S(1)} %get-tuple-element.93.tg, bf16[512,512]{1,0:T(8,128)(2,1)S(1)} %get-tuple-element.94.v_one, bf16[512,512]{1,0:T(8,128)(2,1)S(1)} %get-tuple-element.87.w_b, bf16[512,512]{1,0:T(8,128)(2,1)S(1)} %get-tuple-element.99.near, ...), custom_call_target="tpu_custom_call" | custom-call | flops 1342177 | tf_op jit(solution)/shard_map/pallas_call | solution.py:52
  33.4 0.0 collective-permute-done.8.b
  33.4 0.0 collective-permute-done.7.a
  33.5 0.1 collective-permute-start.14
  33.5 3.5 %collective-permute-done.11.b = bf16[512,128]{1,0:T(8,128)(2,1)S(1)} collective-permute-done((bf16[512,128]{1,0:T(8,128)(2,1)S(1)}, bf16[512,128]{1,0:T(8,128)(2,1)S(1)}, u32[]{:S(2)}, u32[]{:S(2)}) %collective-permute-start.11) | collective-permute-done | bytes 131104 | tf_op jit(solution)/shard_map/ppermute | solution.py:418
  37.0 0.0 collective-permute-done.10.a
  37.0 0.4 %shard_map.60 = (bf16[512,128]{1,0:T(8,128)(2,1)S(1)}, bf16[256,128]{1,0:T(8,128)(2,1)S(1)}, bf16[256,128]{1,0:T(8,128)(2,1)S(1)}) custom-call(bf16[512,128]{1,0:T(8,128)(2,1)S(1)} %get-tuple-element.115.g, bf16[512,512]{1,0:T(8,128)(2,1)S(1)} %get-tuple-element.114.after.from_left, bf16[512,512]{1,0:T(8,128)(2,1)S(1)} %get-tuple-element.116.from_right, ...), custom_call_target="tpu_custom_call" | custom-call | flops 134217 | tf_op jit(solution)/shard_map/pallas_call | solution.py:52
  37.5 0.1 collective-permute-start.12
  37.6 0.5 %collective-permute-start.13 = (bf16[256,128]{1,0:T(8,128)(2,1)S(1)}, bf16[256,128]{1,0:T(8,128)(2,1)S(1)}, u32[]{:S(2)}, u32[]{:S(2)}) collective-permute-start(bf16[256,128]{1,0:T(8,128)(2,1)S(1)} %get-tuple-element.120), channel_id=1, source_target_pairs={{0,1},{1,0},{2,3},{3,2},{4,5},{5,4},{6,7},{7,6},{8,9},{9,8},{10,11... | collective-permute-start | bytes 196616 | tf_op jit(solution)/shard_map/ppermute | solution.py:418
  38.1 0.7 %collective-permute-done.12.x_pair0 = bf16[256,128]{1,0:T(8,128)(2,1)S(1)} collective-permute-done((bf16[256,128]{1,0:T(8,128)(2,1)S(1)}, bf16[256,128]{1,0:T(8,128)(2,1)S(1)}, u32[]{:S(2)}, u32[]{:S(2)}) %collective-permute-start.12) | collective-permute-done | bytes 65568 | tf_op jit(solution)/shard_map/ppermute | solution.py:418
  38.8 0.2 collective-permute-done.13.x_pair1
  39.0 0.3 shard_map.61.rest
  39.3 2.2 %collective-permute-done.14.x_gap = bf16[512,128]{1,0:T(8,128)(2,1)S(1)} collective-permute-done((bf16[512,128]{1,0:T(8,128)(2,1)S(1)}, bf16[512,128]{1,0:T(8,128)(2,1)S(1)}, u32[]{:S(2)}, u32[]{:S(2)}) %collective-permute-start.14) | collective-permute-done | bytes 131104 | tf_op jit(solution)/shard_map/ppermute | solution.py:418
  41.5 1.0 %shard_map.62 = bf16[2,512,128]{2,1,0:T(8,128)(2,1)} custom-call(bf16[512,640]{1,0:T(8,128)(2,1)S(1)} %get-tuple-element.64.vg_b, bf16[512,128]{1,0:T(8,128)(2,1)S(1)} %shard_map.59.x_even, bf16[512,128]{1,0:T(8,128)(2,1)S(1)} %get-tuple-element.118.x_odd, f32[512,128]{1,0:T(8,128)S(1)} %shard_map.61.rest, bf16[512,128]{1,0:T(8,128)(2,1)S(1)} %collective-permute-done.14.x_gap), custom_call_target="tpu_custom_call" | custom-call | flops 67108 | tf_op jit(solution)/shard_map/pallas_call | solution.py:52
  (5 shorter events, 0.1 us)
Async XLA Ops:
  2.2 7.8 %collective-permute-start = (bf16[512,640]{1,0:T(8,128)(2,1)S(1)}, bf16[512,640]{1,0:T(8,128)(2,1)S(1)}, u32[]{:S(2)}, u32[]{:S(2)}) collective-permute-start(bf16[512,640]{1,0:T(8,128)(2,1)S(1)} %shard_map.46.vg_odd), channel_id=1, source_target_pairs={{0,1},{1,2},{2,0},{3,4},{4,5},{5,6},{6,7},{7,8},{8,9},{9,10},{10,1... | collective-permute-start | bytes 1966088 | tf_op jit(solution)/shard_map/ppermute | solution.py:418
  5.7 2.2 %collective-permute-start.1 = (bf16[512,384]{1,0:T(8,128)(2,1)S(1)}, bf16[512,384]{1,0:T(8,128)(2,1)S(1)}, u32[]{:S(2)}, u32[]{:S(2)}) collective-permute-start(bf16[512,384]{1,0:T(8,128)(2,1)S(1)} %get-tuple-element.82), channel_id=1, source_target_pairs={{0,1},{1,0},{2,3},{3,2},{4,5},{5,4},{6,7},{7,6},{8,9},{9,8},{10,11... | collective-permute-start | bytes 1179656 | tf_op jit(solution)/shard_map/ppermute | solution.py:418
  5.8 2.1 %collective-permute-start.2 = (bf16[512,256]{1,0:T(8,128)(2,1)S(1)}, bf16[512,256]{1,0:T(8,128)(2,1)S(1)}, u32[]{:S(2)}, u32[]{:S(2)}) collective-permute-start(bf16[512,256]{1,0:T(8,128)(2,1)S(1)} %get-tuple-element.83), channel_id=1, source_target_pairs={{0,1},{1,0},{2,3},{3,2},{4,5},{5,4},{6,7},{7,6},{8,9},{9,8},{10,11... | collective-permute-start | bytes 786440 | tf_op jit(solution)/shard_map/ppermute | solution.py:418
  10.0 11.5 %collective-permute-start.6 = (bf16[512,640]{1,0:T(8,128)(2,1)S(1)}, bf16[512,640]{1,0:T(8,128)(2,1)S(1)}, u32[]{:S(2)}, u32[]{:S(2)}) collective-permute-start(bf16[512,640]{1,0:T(8,128)(2,1)S(1)} %get-tuple-element.96.w_vg), channel_id=1, source_target_pairs={{0,1},{1,2},{2,0},{3,4},{4,5},{5,6},{6,7},{7,8},{8,9},{9,10},{10,1... | collective-permute-start | bytes 1966088 | tf_op jit(solution)/shard_map/ppermute | solution.py:418
  10.2 17.7 %collective-permute-start.9 = (bf16[512,640]{1,0:T(8,128)(2,1)S(1)}, bf16[512,640]{1,0:T(8,128)(2,1)S(1)}, u32[]{:S(2)}, u32[]{:S(2)}) collective-permute-start(bf16[512,640]{1,0:T(8,128)(2,1)S(1)} %get-tuple-element.93.tg), channel_id=1, source_target_pairs={{31,30},{30,29},{29,31},{28,27},{27,26},{26,25},{25,24},{24,23},{2... | collective-permute-start | bytes 1966088 | tf_op jit(solution)/shard_map/ppermute | solution.py:418
  14.8 4.2 %collective-permute-start.3 = (bf16[560,512]{1,0:T(8,128)(2,1)S(1)}, bf16[560,512]{1,0:T(8,128)(2,1)S(1)}, u32[]{:S(2)}, u32[]{:S(2)}) collective-permute-start(bf16[560,512]{1,0:T(8,128)(2,1)S(1)} %get-tuple-element.97), channel_id=1, source_target_pairs={{0,1},{1,0},{2,3},{3,2},{4,5},{5,4},{6,7},{7,6},{8,9},{9,8},{10,11... | collective-permute-start | bytes 1720328 | tf_op jit(solution)/shard_map/ppermute | solution.py:418
  14.8 4.1 %collective-permute-start.4 = (bf16[560,512]{1,0:T(8,128)(2,1)S(1)}, bf16[560,512]{1,0:T(8,128)(2,1)S(1)}, u32[]{:S(2)}, u32[]{:S(2)}) collective-permute-start(bf16[560,512]{1,0:T(8,128)(2,1)S(1)} %get-tuple-element.95.to_pair1), channel_id=1, source_target_pairs={{0,1},{1,0},{2,3},{3,2},{4,5},{5,4},{6,7},{7,6},{8,9},{9,8},{10,11... | collective-permute-start | bytes 1720328 | tf_op jit(solution)/shard_map/ppermute | solution.py:418
  15.3 3.7 %collective-permute-start.5 = (bf16[544,512]{1,0:T(8,128)(2,1)S(1)}, bf16[544,512]{1,0:T(8,128)(2,1)S(1)}, u32[]{:S(2)}, u32[]{:S(2)}) collective-permute-start(bf16[544,512]{1,0:T(8,128)(2,1)S(1)} %get-tuple-element.98), channel_id=1, source_target_pairs={{0,1},{1,0},{2,3},{3,2},{4,5},{5,4},{6,7},{7,6},{8,9},{9,8},{10,11... | collective-permute-start | bytes 1671176 | tf_op jit(solution)/shard_map/ppermute | solution.py:418
  21.8 11.6 %collective-permute-start.8 = (bf16[512,128]{1,0:T(8,128)(2,1)S(1)}, bf16[512,128]{1,0:T(8,128)(2,1)S(1)}, u32[]{:S(2)}, u32[]{:S(2)}) collective-permute-start(bf16[512,128]{1,0:T(8,128)(2,1)S(1)} %get-tuple-element.108), channel_id=1, source_target_pairs={{0,1},{1,17},{2,4},{3,19},{4,2},{5,21},{6,8},{7,23},{8,6},{9,25},{... | collective-permute-start | bytes 393224 | tf_op jit(solution)/shard_map/ppermute | solution.py:418
  24.1 9.4 %collective-permute-start.7 = (bf16[512,128]{1,0:T(8,128)(2,1)S(1)}, bf16[512,128]{1,0:T(8,128)(2,1)S(1)}, u32[]{:S(2)}, u32[]{:S(2)}) collective-permute-start(bf16[512,128]{1,0:T(8,128)(2,1)S(1)} %get-tuple-element.105.after), channel_id=1, source_target_pairs={{0,2},{1,17},{2,0},{3,19},{4,6},{5,21},{6,4},{7,23},{8,10},{9,25},... | collective-permute-start | bytes 393224 | tf_op jit(solution)/shard_map/ppermute | solution.py:418
  29.5 7.6 %collective-permute-start.11 = (bf16[512,128]{1,0:T(8,128)(2,1)S(1)}, bf16[512,128]{1,0:T(8,128)(2,1)S(1)}, u32[]{:S(2)}, u32[]{:S(2)}) collective-permute-start(bf16[512,128]{1,0:T(8,128)(2,1)S(1)} %get-tuple-element.117), channel_id=1, source_target_pairs={{0,16},{1,0},{2,18},{3,5},{4,20},{5,3},{6,22},{7,9},{8,24},{9,7},{... | collective-permute-start | bytes 393224 | tf_op jit(solution)/shard_map/ppermute | solution.py:418
  31.8 5.3 %collective-permute-start.10 = (bf16[512,128]{1,0:T(8,128)(2,1)S(1)}, bf16[512,128]{1,0:T(8,128)(2,1)S(1)}, u32[]{:S(2)}, u32[]{:S(2)}) collective-permute-start(bf16[512,128]{1,0:T(8,128)(2,1)S(1)} %get-tuple-element.113.after), channel_id=1, source_target_pairs={{0,16},{1,3},{2,18},{3,1},{4,20},{5,7},{6,22},{7,5},{8,24},{9,11},... | collective-permute-start | bytes 393224 | tf_op jit(solution)/shard_map/ppermute | solution.py:418
  33.5 8.0 %collective-permute-start.14 = (bf16[512,128]{1,0:T(8,128)(2,1)S(1)}, bf16[512,128]{1,0:T(8,128)(2,1)S(1)}, u32[]{:S(2)}, u32[]{:S(2)}) collective-permute-start(bf16[512,128]{1,0:T(8,128)(2,1)S(1)} %shard_map.59.x_even), channel_id=1, source_target_pairs={{31,30},{30,29},{29,31},{28,27},{27,26},{26,25},{25,24},{24,23},{2... | collective-permute-start | bytes 393224 | tf_op jit(solution)/shard_map/ppermute | solution.py:418
  37.5 1.3 %collective-permute-start.12 = (bf16[256,128]{1,0:T(8,128)(2,1)S(1)}, bf16[256,128]{1,0:T(8,128)(2,1)S(1)}, u32[]{:S(2)}, u32[]{:S(2)}) collective-permute-start(bf16[256,128]{1,0:T(8,128)(2,1)S(1)} %get-tuple-element.119), channel_id=1, source_target_pairs={{0,1},{1,0},{2,3},{3,2},{4,5},{5,4},{6,7},{7,6},{8,9},{9,8},{10,11... | collective-permute-start | bytes 196616 | tf_op jit(solution)/shard_map/ppermute | solution.py:418
  37.6 1.4 %collective-permute-start.13 = (bf16[256,128]{1,0:T(8,128)(2,1)S(1)}, bf16[256,128]{1,0:T(8,128)(2,1)S(1)}, u32[]{:S(2)}, u32[]{:S(2)}) collective-permute-start(bf16[256,128]{1,0:T(8,128)(2,1)S(1)} %get-tuple-element.120), channel_id=1, source_target_pairs={{0,1},{1,0},{2,3},{3,2},{4,5},{5,4},{6,7},{7,6},{8,9},{9,8},{10,11... | collective-permute-start | bytes 196616 | tf_op jit(solution)/shard_map/ppermute | solution.py:418

commit v6 on v5

--- a/solution.py
+++ b/solution.py
@@ -75,29 +75,36 @@
     return copy
 
 
-def load_row(order, diag, upper, right, vg, diag_b, upper_b, right_b, sems):
-    d_b = fetch(diag.at[1], diag_b, sems.at[0])
-    u_b = fetch(upper.at[1], upper_b, sems.at[1])
-    r_b = fetch(right.at[1], right_b, sems.at[2])
-    d_b.wait()
-    u_b.wait()
-    vg[:, :order] = dot(diag_b[...], upper_b[...]).astype(BF16)
-    r_b.wait()
-    vg[:, order:] = dot(diag_b[...], right_b[...]).astype(BF16)
-
-
-def second_row_odd(order, *refs):
-    by_parity(None, lambda: load_row(order, *refs))
+def load_row(order, diag, upper, right, vg, diag_b, sides, sems, later=()):
+    copies = [
+        fetch(diag.at[1], diag_b, sems.at[0]),
+        fetch(upper.at[1], sides.at[:, :order], sems.at[1]),
+        fetch(right.at[1], sides.at[:, order:], sems.at[2]),
+    ]
+    for copy in later:
+        copy.start()
+    for copy in copies:
+        copy.wait()
+    vg[...] = dot(diag_b[...], sides[...]).astype(BF16)
+
+
+def second_row_odd(order, diag, upper, right, lower, vg, diag_b, lower_b, sides, sems):
+    def odd():
+        later = pltpu.make_async_copy(lower.at[1], lower_b, sems.at[3])
+        load_row(order, diag, upper, right, vg, diag_b, sides, sems, [later])
+        later.wait()
+
+    by_parity(None, odd)
 
 
 def second_row(order, diag, upper, right, vg_odd, after, vg_b, *rest):
-    *pieces, diag_b, upper_b, right_b, sems = rest
+    *pieces, diag_b, sides, sems = rest
 
     def odd():
         vg_b[...] = vg_odd[...]
 
     def even():
-        load_row(order, diag, upper, right, vg_b, diag_b, upper_b, right_b, sems)
+        load_row(order, diag, upper, right, vg_b, diag_b, sides, sems)
         first = 0
         for piece in pieces:
             piece[...] = vg_b[:, first : first + piece.shape[1]]
@@ -107,13 +114,16 @@
 
 
 def own_products_odd(
-    order, diag, lower, upper, right, vg_odd, w_a, w_b, m, n, r, v_a, diag_a, lower_a, diag_b, lower_b,
-    upper_a, right_a, sems,
+    order, diag, lower, upper, right, vg_odd, diag_b, lower_b,
+    w_a, w_b, m, n, r, v_a, diag_a, lower_a, upper_a, right_a, sems,
 ):
     def odd():
-        held = diag_a, lower_a, diag_b, lower_b, upper_a, right_a
-        first_right_side(order, own_copies(diag, lower, upper, right, *held, sems), vg_odd, held, v_a, r)
-        spikes_own(order, vg_odd, diag_a, lower_a, diag_b, lower_b, v_a, w_a, w_b, m, n)
+        copies = first_row_copies(diag, lower, upper, right, diag_a, lower_a, upper_a, right_a, sems)
+        for copy in copies:
+            copy.start()
+        w_b[...] = dot(diag_b[...], lower_b[...]).astype(BF16)
+        first_right_side(order, copies, vg_odd, diag_a, upper_a, right_a, v_a, r)
+        first_spikes(order, vg_odd, diag_a, lower_a, v_a, w_a, w_b, m, n)
 
     by_parity(None, odd)
 
@@ -122,8 +132,14 @@
     r, v_a, diag_a, lower_a, diag_b, lower_b, upper_a, right_a, sems = rest[6:]
 
     def even():
-        held = diag_a, lower_a, diag_b, lower_b, upper_a, right_a
-        first_right_side(order, own_copies(diag, lower, upper, right, *held, sems), vg_b, held, v_a, r)
+        copies = first_row_copies(diag, lower, upper, right, diag_a, lower_a, upper_a, right_a, sems)
+        copies += [
+            pltpu.make_async_copy(diag.at[1], diag_b, sems.at[4]),
+            pltpu.make_async_copy(lower.at[1], lower_b, sems.at[5]),
+        ]
+        for copy in copies:
+            copy.start()
+        first_right_side(order, copies, vg_b, diag_a, upper_a, right_a, v_a, r)
 
     by_parity(even, None)
 
@@ -132,23 +148,18 @@
     w_a, w_b, m, n = rest[4:]
 
     def even():
-        spikes_own(order, vg_b, diag_a, lower_a, diag_b, lower_b, v_a, w_a, w_b, m, n)
-
-    by_parity(even, None)
-
-
-def own_copies(diag, lower, upper, right, diag_a, lower_a, diag_b, lower_b, upper_a, right_a, sems):
-    pairs = (
-        (diag.at[0], diag_a), (upper.at[0], upper_a), (right.at[0], right_a),
-        (diag.at[1], diag_b), (lower.at[1], lower_b), (lower.at[0], lower_a),
-    )
-    return [pltpu.make_async_copy(x, y, sems.at[i]) for i, (x, y) in enumerate(pairs)]
-
-
-def first_right_side(order, copies, vg_b, held, v_a, r):
-    diag_a, lower_a, diag_b, lower_b, upper_a, right_a = held
-    for copy in copies:
-        copy.start()
+        w_b[...] = dot(diag_b[...], lower_b[...]).astype(BF16)
+        first_spikes(order, vg_b, diag_a, lower_a, v_a, w_a, w_b, m, n)
+
+    by_parity(even, None)
+
+
+def first_row_copies(diag, lower, upper, right, diag_a, lower_a, upper_a, right_a, sems):
+    pairs = (diag, diag_a), (upper, upper_a), (right, right_a), (lower, lower_a)
+    return [pltpu.make_async_copy(x.at[0], y, sems.at[i]) for i, (x, y) in enumerate(pairs)]
+
+
+def first_right_side(order, copies, vg_b, diag_a, upper_a, right_a, v_a, r):
     for copy in copies[:3]:
         copy.wait()
     v_a[...] = dot(diag_a[...], upper_a[...]).astype(BF16)
@@ -158,8 +169,7 @@
         copy.wait()
 
 
-def spikes_own(order, vg_b, diag_a, lower_a, diag_b, lower_b, v_a, w_a, w_b, m, n):
-    w_b[...] = dot(diag_b[...], lower_b[...]).astype(BF16)
+def first_spikes(order, vg_b, diag_a, lower_a, v_a, w_a, w_b, m, n):
     w_a[...] = dot(diag_a[...], lower_a[...]).astype(BF16)
     n[...] = dot(v_a[...], vg_b[:, :order]).astype(BF16)
     m[...] = dot(v_a[...], w_b[...])
@@ -203,7 +213,8 @@
     for block, piece in zip(blocks, to_pair):
         last = first + piece.shape[0] - order
         piece[:order, :] = block
-        piece[order:, :] = rows[first:last]
+        if last > first:
+            piece[order:, :] = rows[first:last]
         first = last
 
 
@@ -240,51 +251,61 @@
     by_parity(even, None)
 
 
-def pair_part(
-    order, tg, v_one, w_b, to_pair1, w_vg, pair0, pair1, pair2,
-    near, far, w_far, p_far, p_v, n_h, w_h, w_n_h, p_n_h,
+def same(value):
+    return value
+
+
+def pair_part_even(order, tg, v_one, w_b, pair0, pair1, near, n_h):
+    def even():
+        right = dot(pair0[:order, :], w_b[...]).astype(BF16)
+        near[...] = (identity(order) - dot(v_one[...], right)).astype(BF16)
+        side = side_of_pair(order, [pair0, pair1], n_h.shape[1])
+        n_h[...] = tg[:, order:].astype(F32) - dot(v_one[...], side)
+
+    by_parity(even, None)
+
+
+def pair_part_odd(
+    order, tg, v_one, w_b, pair0, pair1, pair2, near, far, w_far, p_far, p_v, n_h, w_h, w_n_h, p_n_h
 ):
-    got, w_t, w_t_pair, v_pair = (x[:order, :] for x in (pair0, to_pair1, pair1, pair2))
-    got_g = side_of_pair(order, [pair0, pair1, pair2], n_h.shape[1])
-    t, eye = tg[:, :order], identity(order)
-
-    def even():
-        right = dot(got, w_b[...]).astype(BF16)
-        near[...] = (eye - dot(v_one[...], right)).astype(BF16)
-        far[...] = dot(w_b[...], near[...]).astype(BF16)
-        p_far[...] = dot(w_t_pair, far[...]).astype(BF16)
-        p_v[...] = dot(w_t_pair, w_t).astype(BF16)
-        n_h[...] = tg[:, order:].astype(F32) - dot(v_one[...], got_g)
-
-    def odd():
-        near[...] = (eye - dot(t, got)).astype(BF16)
+    def odd():
+        t, v_pair = tg[:, :order], pair2[...]
+        near[...] = (identity(order) - dot(t, pair0[:order, :])).astype(BF16)
         far[...] = dot(near[...], v_one[...]).astype(BF16)
         w_far[...] = dot(w_b[...], far[...]).astype(BF16)
         p_far[...] = dot(v_pair, far[...]).astype(BF16)
         p_v[...] = dot(v_pair, v_one[...]).astype(BF16)
-        own = (tg[:, order:].astype(F32) + dot(t, got_g)).astype(BF16)
+        side = side_of_pair(order, [pair0, pair1], n_h.shape[1])
+        own = (tg[:, order:].astype(F32) + dot(t, side)).astype(BF16)
         scaled = dot(near[...], own)
         n_h[...] = scaled
         w_h[...] = dot(w_b[...], own)
         w_n_h[...] = dot(w_b[...], scaled.astype(BF16))
         p_n_h[...] = dot(v_pair, scaled.astype(BF16))
 
-    by_parity(even, odd)
+    by_parity(None, odd)
+
+
+def hand_over(block, out):
+    rows = block.shape[0]
+    out[:rows, :] = block[...]
+    if out.shape[0] > rows:
+        out[rows:, :] = jnp.zeros((out.shape[0] - rows, out.shape[1]), BF16)
 
 
 def hand_out(right, left, a, b):
     left_of_two = lax.rem(lax.axis_index(AXES), 4) < 2
-    a[...] = jnp.where(left_of_two, right, left)
+    hand_over(jnp.where(left_of_two, right, left), a)
     b[...] = jnp.where(left_of_two, left, right)
 
 
-def level_two_even(order, tg, near, far, p_far, p_v, n_h, w_vg_gap, g, a, b):
+def level_two_even(order, tg, w_b, near, n_h, pair1, w_vg_gap, g, a, b):
     def even():
         t = tg[:, :order]
         whole = (n_h[...] + if_left(dot(t, w_vg_gap[:, order:]))).astype(BF16)
         from_left = if_left(dot(w_vg_gap[:, :order], whole)).astype(BF16)
         value = (dot(near[...], whole) - dot(t, from_left)).astype(BF16)
-        onward = (dot(p_v[...], from_left) - dot(p_far[...], whole)).astype(BF16)
+        onward = (-dot(pair1[:order, :], dot(w_b[...], value).astype(BF16))).astype(BF16)
         g[...] = value
         hand_out(onward, value, a, b)
 
@@ -344,7 +365,8 @@
 
 def top_value(g, from_left, from_right, a, b, x):
     def top(left, right):
-        change = dot(from_left[...], left[...]) + dot(from_right[...], right[...])
+        rows = g.shape[0]
+        change = dot(from_left[...], left[:rows, :]) + dot(from_right[...], right[:rows, :])
         x[...] = (g[...].astype(F32) + change).astype(BF16)
 
     left_of_two = lax.rem(lax.axis_index(AXES), 4) < 2
@@ -352,42 +374,31 @@
     pl.when(jnp.logical_not(left_of_two))(lambda: top(a, b))
 
 
-def top_even(g, from_left, from_right, a, b, after, x):
-    by_parity(lambda: top_value(g, from_left, from_right, a, b, x), None)
-
-
-def top_odd(g, from_left, from_right, a, b, x, *halves):
-    def odd():
+def top_even(g, from_left, from_right, a, b, x, x_out):
+    def even():
         top_value(g, from_left, from_right, a, b, x)
-        rows = halves[0].shape[0]
-        for i, half in enumerate(halves):
-            half[...] = x[i * rows : (i + 1) * rows, :]
-
-    by_parity(None, odd)
-
-
-def second_values(order, vg_b, w_b, x_even, x_odd, x_pair0, x_pair1, rest):
-    def even():
-        x_next = jnp.concatenate([x_pair0[...], x_pair1[...]], axis=0)
-        own = vg_b[:, order:].astype(F32) - dot(w_b[...], x_even[...])
-        rest[...] = own - dot(vg_b[:, :order], x_next)
-
-    def odd():
-        rest[...] = vg_b[:, order:].astype(F32) - dot(w_b[...], x_odd[...])
-
-    by_parity(even, odd)
-
-
-def finish(order, vg_b, x_even, x_odd, rest, x_gap, out):
-    def even():
-        out[0] = x_even[...]
-        out[1] = rest[...].astype(BF16)
-
-    def odd():
-        out[0] = x_odd[...]
-        out[1] = (rest[...] - if_right(dot(vg_b[:, :order], x_gap[...]))).astype(BF16)
-
-    by_parity(even, odd)
+        hand_over(x, x_out)
+
+    by_parity(even, None)
+
+
+def top_odd(g, from_left, from_right, a, b, x):
+    by_parity(None, lambda: top_value(g, from_left, from_right, a, b, x))
+
+
+def start_second(order, vg_b, w_b, x_even, x_odd, rest):
+    def start(x):
+        rest[...] = vg_b[:, order:].astype(F32) - dot(w_b[...], x[...])
+
+    by_parity(lambda: start(x_even), lambda: start(x_odd))
+
+
+def finish(order, vg_b, x_even, x_odd, rest, x_pair, x_gap, out):
+    def rows(x, x_next, right_on):
+        out[0] = x[...]
+        out[1] = (rest[...] - right_on(dot(vg_b[:, :order], x_next[:order, :]))).astype(BF16)
+
+    by_parity(lambda: rows(x_even, x_pair, same), lambda: rows(x_odd, x_gap, if_right))
 
 
 def exchanges(slab, count):
@@ -426,35 +437,35 @@
     full = bf16_array(order, order)
     slim = bf16_array(order, rhs)
 
-    row_scratch = (block, block, side, pltpu.SemaphoreType.DMA((3,)))
-    vg_odd = local_call(
-        part(second_row_odd, order), [wide], [diag, upper, right], square + thin, 3, row_scratch
+    row_scratch = (pltpu.VMEM((order, order + rhs), BF16), pltpu.SemaphoreType.DMA((4,)))
+    vg_odd, diag_b, lower_b = local_call(
+        part(second_row_odd, order),
+        [wide, full, full], [diag, upper, right, lower], square + thin, 4, row_scratch,
     )
     vg_gap = sent(vg_odd, to_right)
-    own_arrays = [f32_array(order, rhs)] + [full] * 5
+    own_arrays = [f32_array(order, rhs)] + [full] * 3
     spike_arrays = [full, full, f32_array(order, order), full]
     own_scratch = (block, side, pltpu.SemaphoreType.DMA((6,)))
     spikes = local_call(
         part(own_products_odd, order),
-        spike_arrays + own_arrays, [diag, lower, upper, right, vg_odd], 5 * square + 2 * thin,
-        4, own_scratch,
-    )
-    spikes, own = spikes[:4], spikes[4:]
+        spike_arrays + own_arrays, [diag, lower, upper, right, vg_odd, diag_b, lower_b],
+        5 * square + 2 * thin, 4, own_scratch,
+    )
+    spikes, own = spikes[:4], [*spikes[4:], diag_b, lower_b]
     cut = 3 * order // 4
     vg_b, *to_pair = local_call(
         part(second_row, order),
         [wide, bf16_array(order, cut), bf16_array(order, order - cut + rhs)],
-        [diag, upper, right, vg_odd, own[0]], square + thin, 3, row_scratch,
+        [diag, upper, right, vg_odd, own[0]], square + thin, 3, (block, *row_scratch),
     )
     vg_pair = [sent(piece, pairs) for piece in to_pair]
     r, v_a, *held = local_call(
         part(own_products_even, order),
-        own_arrays, [diag, lower, upper, right, vg_b, *own], square + 2 * thin,
+        own_arrays + [full] * 2, [diag, lower, upper, right, vg_b, *own], square + 2 * thin,
         4, own_scratch, {5 + i: i for i in range(6)},
     )
     w_a, w_b, m, n = spikes
-    extra = rhs // 16 * 6
-    shares = [bf16_array(order + rows, order) for rows in (extra, extra, rhs - 2 * extra)]
+    shares = [bf16_array(order + rows, order) for rows in (rhs // 2, rhs // 2, 0)]
     tg_odd, v_odd, w_vg_odd, *to_pair = local_call(
         part(level_one_odd, order),
         [wide, full, wide, *shares], [w_a, m, r, *vg_pair, n, w_b], 5 * square, 0, (block, block),
@@ -477,25 +488,26 @@
     tg_gap = sent(tg, to_left)
     pair = [sent(piece, pairs) for piece in to_pair]
 
-    tall, flat = f32_array(order, rhs), bf16_array(order // 2, rhs)
-    known = local_call(
-        part(pair_part, order),
-        [full] * 5 + [tall] * 4,
-        [tg, v_one, w_b, to_pair[1], w_vg_odd, *pair], 6 * square,
-    )
-    near, far, w_far, p_far, p_v, n_h, w_h, w_n_h, p_n_h = known
+    tall, tall_slim = f32_array(order, rhs), bf16_array(order + 16, rhs)
+    near_even, n_h_even = local_call(
+        part(pair_part_even, order), [full, tall], [tg, v_one, w_b, *pair[:2]], 2 * square + thin
+    )
+    near, far, w_far, p_far, p_v, n_h, w_h, w_n_h, p_n_h = local_call(
+        part(pair_part_odd, order),
+        [full] * 5 + [tall] * 4, [tg, v_one, w_b, *pair], 5 * square + 5 * thin,
+    )
     g_even, a_even, b_even = local_call(
         part(level_two_even, order),
-        [slim] * 3, [tg, near, far, p_far, p_v, n_h, w_vg_gap], 6 * thin,
+        [slim] * 3, [tg, w_b, near_even, n_h_even, pair[1], w_vg_gap], 6 * thin,
     )
     even_a, even_b = sent(a_even, twos[0]), sent(b_even, other_twos[0])
     left_even, right_even = local_call(
         part(spikes_two_even, order),
-        [full, full], [tg, v_one, near, pair[2], w_vg_gap, a_even], 4 * square, 0, (block,),
+        [full, full], [tg, v_one, near_even, pair[2], w_vg_gap, a_even], 4 * square, 0, (block,),
     )
     g_odd, a_odd, b_odd = local_call(
         part(level_two_odd, order),
-        [slim] * 3,
+        [slim, tall_slim, slim],
         [v_one, w_vg_odd, far, w_far, p_far, p_v, n_h, w_h, w_n_h, p_n_h, tg_gap, left_even], 8 * thin,
     )
     odd_a, odd_b = sent(a_odd, twos[1]), sent(b_odd, other_twos[1])
@@ -503,21 +515,17 @@
         part(spikes_two_odd, order),
         [full, full], [tg, v_one, w_b, near, pair[1], tg_gap, a_odd], 5 * square, 0, (block,),
     )
-    x_even = local_call(
-        top_even, [slim], [g_even, left_even, right_even, even_a, even_b, left_odd], 2 * thin
-    )
-    x_gap = sent(x_even, to_left)
-    x_odd, *x_own = local_call(
-        top_odd,
-        [slim, flat, flat], [g_odd, left_odd, right_odd, odd_a, odd_b], 2 * thin,
-    )
-    x_pair = [sent(piece, pairs) for piece in x_own]
-    rest = local_call(
-        part(second_values, order), [tall], [vg_b, w_b, x_even, x_odd, *x_pair], 2 * thin
-    )
+    x_even, x_out = local_call(
+        top_even, [slim, tall_slim], [g_even, left_even, right_even, even_a, even_b], 2 * thin
+    )
+    x_gap = sent(x_out, to_left)
+    x_odd = local_call(top_odd, [slim], [g_odd, left_odd, right_odd, odd_a, odd_b], 2 * thin)
+    x_pair = sent(x_odd, pairs)
+    rest = local_call(part(start_second, order), [tall], [vg_b, w_b, x_even, x_odd], thin)
     return local_call(
         part(finish, order),
-        [jax.ShapeDtypeStruct((2, order, rhs), BF16)], [vg_b, x_even, x_odd, rest, x_gap], thin,
+        [jax.ShapeDtypeStruct((2, order, rhs), BF16)],
+        [vg_b, x_even, x_odd, rest, x_pair, x_gap], thin,
     )
 
 

time: 42.8 us -> 41 us (0.958)
  waiting for transfers between devices: 15.6 us -> 12.8 us
  starting transfers between devices: 11.1 us -> 12.7 us
  Pallas kernels: 15.6 us -> 14.6 us
    ppermute x15 -> x14, waiting for transfers between devices: 15.6 us -> 12.8 us  [sent(): return lax.ppermute(block, AXES, route)]
    ppermute x15 -> x14, starting transfers between devices: 11.1 us -> 12.7 us  [sent(): return lax.ppermute(block, AXES, route)]
    pallas_call x17 -> x18, Pallas kernels: 15.6 us -> 14.6 us  [local_call(): pl.pallas_call(kernel, out_shape=outs if many else outs[0], in_specs=[hbm...]
  transfers between devices with their start and end apart: 15 -> 14, of which waited for: 7 -> 6; matrix products, arithmetic and copies ran while one was open for 0% -> 0% of each run, Pallas kernels for 29% -> 29%
where the time goes in v6:
time: 41 us; the launch traced here: 40.3 us
  Pallas kernels  14.6 us (36%)
  waiting for transfers between devices  12.8 us (31%)
  starting transfers between devices  12.7 us (31%)
    pallas_call x18, Pallas kernels, local_call(): pl.pallas_call(kernel, out_shape=outs if many else outs[0], in_specs=[hbm...  14.6 us
    ppermute x14, waiting for transfers between devices, sent(): return lax.ppermute(block, AXES, route)  12.8 us
    ppermute x14, starting transfers between devices, sent(): return lax.ppermute(block, AXES, route)  12.7 us
  transfers between devices with their start and end apart: 14, of which 6 were waited for; matrix products, arithmetic and copies ran while one was open for 0% of the time, Pallas kernels for 29%

profile of v6, /device:TPU:29, one launch (start us, length us, event | category | flops | bytes accessed | tf_op | source)
XLA Modules:
  0.0 40.3 jit_solution(13693593054256218055)
XLA Ops:
  0.0 1.8 %shard_map.46 = (bf16[512,640]{1,0:T(8,128)(2,1)S(1)}, bf16[512,512]{1,0:T(8,128)(2,1)S(1)}, bf16[512,512]{1,0:T(8,128)(2,1)S(1)}) custom-call(bf16[2,512,512]{2,1,0:T(8,128)(2,1)} %diag.7, bf16[2,512,512]{2,1,0:T(8,128)(2,1)} %upper.7, bf16[2,512,128]{2,1,0:T(8,128)(2,1)} %right.7, bf16[2,512,512]{2,1,0:T(8,128)(2,1)} %lower.5), custom_call_target="tpu_custom_call" | custom-call | flops 335544 | tf_op jit(solution)/shard_map/pallas_call | solution.py:52
  1.8 0.1 collective-permute-start
  1.9 3.0 %shard_map.47 = (bf16[512,512]{1,0:T(8,128)(2,1)S(1)}, bf16[512,512]{1,0:T(8,128)(2,1)S(1)}, f32[512,512]{1,0:T(8,128)S(1)}, bf16[512,512]{1,0:T(8,128)(2,1)S(1)...) custom-call(bf16[2,512,512]{2,1,0:T(8,128)(2,1)} %diag.7, ...), custom_call_target="tpu_custom_call" | custom-call | flops 1476395 | tf_op jit(solution)/shard_map/pallas_call | solution.py:52
  4.9 0.1 shard_map.48
  5.0 0.1 collective-permute-start.1
  5.1 0.5 %collective-permute-start.2 = (bf16[512,256]{1,0:T(8,128)(2,1)S(1)}, bf16[512,256]{1,0:T(8,128)(2,1)S(1)}, u32[]{:S(2)}, u32[]{:S(2)}) collective-permute-start(bf16[512,256]{1,0:T(8,128)(2,1)S(1)} %get-tuple-element.86), channel_id=1, source_target_pairs={{0,1},{1,0},{2,3},{3,2},{4,5},{5,4},{6,7},{7,6},{8,9},{9,8},{10,11... | collective-permute-start | bytes 786440 | tf_op jit(solution)/shard_map/ppermute | solution.py:429
  5.6 0.1 shard_map.49
  5.7 1.5 %collective-permute-done.2.vg1 = bf16[512,256]{1,0:T(8,128)(2,1)S(1)} collective-permute-done((bf16[512,256]{1,0:T(8,128)(2,1)S(1)}, bf16[512,256]{1,0:T(8,128)(2,1)S(1)}, u32[]{:S(2)}, u32[]{:S(2)}) %collective-permute-start.2) | collective-permute-done | bytes 262176 | tf_op jit(solution)/shard_map/ppermute | solution.py:429
  7.2 0.0 collective-permute-done.1.v0
  7.2 2.2 %shard_map.51 = (bf16[512,640]{1,0:T(8,128)(2,1)S(1)}, bf16[512,512]{1,0:T(8,128)(2,1)S(1)}, bf16[512,640]{1,0:T(8,128)(2,1)S(1)}, bf16[576,512]{1,0:T(8,128)(2,...) custom-call(bf16[512,512]{1,0:T(8,128)(2,1)S(1)} %get-tuple-element.78.rest_0_.w_a, ...), custom_call_target="tpu_custom_call" | custom-call | flops 1342177 | tf_op jit(solution)/shard_map/pallas_call | solution.py:52
  9.4 0.1 collective-permute-start.5
  9.4 0.0 collective-permute-done.after.vg
  9.5 4.8 %collective-permute-start.9 = (bf16[512,640]{1,0:T(8,128)(2,1)S(1)}, bf16[512,640]{1,0:T(8,128)(2,1)S(1)}, u32[]{:S(2)}, u32[]{:S(2)}) collective-permute-start(bf16[512,640]{1,0:T(8,128)(2,1)S(1)} %get-tuple-element.96.tg), channel_id=1, source_target_pairs={{31,30},{30,29},{29,31},{28,27},{27,26},{26,25},{25,24},{24,23},{2... | collective-permute-start | bytes 1966088 | tf_op jit(solution)/shard_map/ppermute | solution.py:429
  14.4 0.1 collective-permute-start.3
  14.4 0.4 %collective-permute-start.4 = (bf16[576,512]{1,0:T(8,128)(2,1)S(1)}, bf16[576,512]{1,0:T(8,128)(2,1)S(1)}, u32[]{:S(2)}, u32[]{:S(2)}) collective-permute-start(bf16[576,512]{1,0:T(8,128)(2,1)S(1)} %get-tuple-element.99), channel_id=1, source_target_pairs={{0,1},{1,0},{2,3},{3,2},{4,5},{5,4},{6,7},{7,6},{8,9},{9,8},{10,11... | collective-permute-start | bytes 1769480 | tf_op jit(solution)/shard_map/ppermute | solution.py:429
  14.9 0.1 collective-permute-start.6
  15.0 2.0 %collective-permute-done.3.pair0 = bf16[576,512]{1,0:T(8,128)(2,1)S(1)} collective-permute-done((bf16[576,512]{1,0:T(8,128)(2,1)S(1)}, bf16[576,512]{1,0:T(8,128)(2,1)S(1)}, u32[]{:S(2)}, u32[]{:S(2)}) %collective-permute-start.3) | collective-permute-done | bytes 589856 | tf_op jit(solution)/shard_map/ppermute | solution.py:429
  16.9 0.8 %collective-permute-done.4.pair1 = bf16[576,512]{1,0:T(8,128)(2,1)S(1)} collective-permute-done((bf16[576,512]{1,0:T(8,128)(2,1)S(1)}, bf16[576,512]{1,0:T(8,128)(2,1)S(1)}, u32[]{:S(2)}, u32[]{:S(2)}) %collective-permute-start.4) | collective-permute-done | bytes 589856 | tf_op jit(solution)/shard_map/ppermute | solution.py:429
  17.8 0.0 collective-permute-done.5.w_vg_gap
  17.8 4.2 %collective-permute-start.8 = (bf16[512,128]{1,0:T(8,128)(2,1)S(1)}, bf16[512,128]{1,0:T(8,128)(2,1)S(1)}, u32[]{:S(2)}, u32[]{:S(2)}) collective-permute-start(bf16[512,128]{1,0:T(8,128)(2,1)S(1)} %get-tuple-element.108), channel_id=1, source_target_pairs={{0,1},{1,17},{2,4},{3,19},{4,2},{5,21},{6,8},{7,23},{8,6},{9,25},{... | collective-permute-start | bytes 393224 | tf_op jit(solution)/shard_map/ppermute | solution.py:429
  21.9 0.0 collective-permute-start.7
  21.9 0.0 collective-permute-done.6.pair2
  21.9 2.4 %shard_map.58 = (bf16[512,512]{1,0:T(8,128)(2,1)S(1)}, bf16[512,512]{1,0:T(8,128)(2,1)S(1)}, bf16[512,512]{1,0:T(8,128)(2,1)S(1)}, bf16[512,512]{1,0:T(8,128)(2,...) custom-call(bf16[512,640]{1,0:T(8,128)(2,1)S(1)} %get-tuple-element., ...), custom_call_target="tpu_custom_call" | custom-call | flops 1677721 | tf_op jit(solution)/shard_map/pallas_call | solution.py:52
  24.4 3.1 %collective-permute-done.9.tg_gap = bf16[512,640]{1,0:T(8,128)(2,1)S(1)} collective-permute-done((bf16[512,640]{1,0:T(8,128)(2,1)S(1)}, bf16[512,640]{1,0:T(8,128)(2,1)S(1)}, u32[]{:S(2)}, u32[]{:S(2)}) %collective-permute-start.9) | collective-permute-done | bytes 655392 | tf_op jit(solution)/shard_map/ppermute | solution.py:429
  27.5 1.6 %shard_map.59 = (bf16[512,128]{1,0:T(8,128)(2,1)S(1)}, bf16[528,128]{1,0:T(8,128)(2,1)S(1)}, bf16[512,128]{1,0:T(8,128)(2,1)S(1)}) custom-call(bf16[512,512]{1,0:T(8,128)(2,1)S(1)} %get-tuple-element.97.v_one, bf16[512,640]{1,0:T(8,128)(2,1)S(1)} %get-tuple-element.102.w_vg, bf16[512,512]{1,0:T(8,128)(2,1)S(1)} %get-tuple-element.110.far, ...), custom_call_target="tpu_custom_call" | custom-call | flops 536870 | tf_op jit(solution)/shard_map/pallas_call | solution.py:52
  29.1 0.1 collective-permute-start.10
  29.2 2.1 %collective-permute-start.11 = (bf16[512,128]{1,0:T(8,128)(2,1)S(1)}, bf16[512,128]{1,0:T(8,128)(2,1)S(1)}, u32[]{:S(2)}, u32[]{:S(2)}) collective-permute-start(bf16[512,128]{1,0:T(8,128)(2,1)S(1)} %get-tuple-element.123), channel_id=1, source_target_pairs={{0,16},{1,0},{2,18},{3,5},{4,20},{5,3},{6,22},{7,9},{8,24},{9,7},{... | collective-permute-start | bytes 393224 | tf_op jit(solution)/shard_map/ppermute | solution.py:429
  31.2 0.0 collective-permute-done.8.b
  31.2 0.0 collective-permute-done.7.a
  31.2 0.2 collective-permute-start.13
  31.5 1.6 %shard_map.60 = (bf16[512,512]{1,0:T(8,128)(2,1)S(1)}, bf16[512,512]{1,0:T(8,128)(2,1)S(1)}) custom-call(bf16[512,640]{1,0:T(8,128)(2,1)S(1)} %get-tuple-element.96.tg, bf16[512,512]{1,0:T(8,128)(2,1)S(1)} %get-tuple-element.97.v_one, bf16[512,512]{1,0:T(8,128)(2,1)S(1)} %get-tuple-element.90.w_b, bf16[512,512]{1,0:T(8,128)(2,1)S(1)} %get-tuple-element.119.near, ...), custom_call_target="tpu_custom_call" | custom-call | flops 1342177 | tf_op jit(solution)/shard_map/pallas_call | solution.py:52
  33.1 3.5 %collective-permute-done.11.b = bf16[512,128]{1,0:T(8,128)(2,1)S(1)} collective-permute-done((bf16[512,128]{1,0:T(8,128)(2,1)S(1)}, bf16[512,128]{1,0:T(8,128)(2,1)S(1)}, u32[]{:S(2)}, u32[]{:S(2)}) %collective-permute-start.11) | collective-permute-done | bytes 131104 | tf_op jit(solution)/shard_map/ppermute | solution.py:429
  36.6 0.0 collective-permute-done.10.a
  36.6 0.4 %shard_map.61.x_odd = bf16[512,128]{1,0:T(8,128)(2,1)S(1)} custom-call(bf16[512,128]{1,0:T(8,128)(2,1)S(1)} %get-tuple-element.118.g, bf16[512,512]{1,0:T(8,128)(2,1)S(1)} %get-tuple-element.121.from_left, bf16[512,512]{1,0:T(8,128)(2,1)S(1)} %get-tuple-element.122.from_right, bf16[528,128]{1,0:T(8,128)(2,1)S(1)} %collective-permute-done.10.a, ...), custom_call_target="tpu_custom_call" | custom-call | flops 134217 | tf_op jit(solution)/shard_map/pallas_call | solution.py:52
  37.1 0.1 collective-permute-start.12
  37.1 0.3 shard_map.62.rest
  37.5 1.8 %collective-permute-done.13.x_gap = bf16[528,128]{1,0:T(8,128)(2,1)S(1)} collective-permute-done((bf16[528,128]{1,0:T(8,128)(2,1)S(1)}, bf16[528,128]{1,0:T(8,128)(2,1)S(1)}, u32[]{:S(2)}, u32[]{:S(2)}) %collective-permute-start.13) | collective-permute-done | bytes 135200 | tf_op jit(solution)/shard_map/ppermute | solution.py:429
  39.3 0.0 collective-permute-done.12.x_pair
  39.3 1.0 %shard_map.63 = bf16[2,512,128]{2,1,0:T(8,128)(2,1)} custom-call(bf16[512,640]{1,0:T(8,128)(2,1)S(1)} %get-tuple-element.69.vg_b, bf16[512,128]{1,0:T(8,128)(2,1)S(1)} %get-tuple-element.109.x_even, bf16[512,128]{1,0:T(8,128)(2,1)S(1)} %shard_map.61.x_odd, f32[512,128]{1,0:T(8,128)S(1)} %shard_map.62.rest, ...), custom_call_target="tpu_custom_call" | custom-call | flops 67108 | tf_op jit(solution)/shard_map/pallas_call | solution.py:52
  (7 shorter events, 0.1 us)
Async XLA Ops:
  1.8 7.6 %collective-permute-start = (bf16[512,640]{1,0:T(8,128)(2,1)S(1)}, bf16[512,640]{1,0:T(8,128)(2,1)S(1)}, u32[]{:S(2)}, u32[]{:S(2)}) collective-permute-start(bf16[512,640]{1,0:T(8,128)(2,1)S(1)} %get-tuple-element.65.vg_odd), channel_id=1, source_target_pairs={{0,1},{1,2},{2,0},{3,4},{4,5},{5,6},{6,7},{7,8},{8,9},{9,10},{10,1... | collective-permute-start | bytes 1966088 | tf_op jit(solution)/shard_map/ppermute | solution.py:429
  5.0 2.2 %collective-permute-start.1 = (bf16[512,384]{1,0:T(8,128)(2,1)S(1)}, bf16[512,384]{1,0:T(8,128)(2,1)S(1)}, u32[]{:S(2)}, u32[]{:S(2)}) collective-permute-start(bf16[512,384]{1,0:T(8,128)(2,1)S(1)} %get-tuple-element.85), channel_id=1, source_target_pairs={{0,1},{1,0},{2,3},{3,2},{4,5},{5,4},{6,7},{7,6},{8,9},{9,8},{10,11... | collective-permute-start | bytes 1179656 | tf_op jit(solution)/shard_map/ppermute | solution.py:429
  5.1 2.1 %collective-permute-start.2 = (bf16[512,256]{1,0:T(8,128)(2,1)S(1)}, bf16[512,256]{1,0:T(8,128)(2,1)S(1)}, u32[]{:S(2)}, u32[]{:S(2)}) collective-permute-start(bf16[512,256]{1,0:T(8,128)(2,1)S(1)} %get-tuple-element.86), channel_id=1, source_target_pairs={{0,1},{1,0},{2,3},{3,2},{4,5},{5,4},{6,7},{7,6},{8,9},{9,8},{10,11... | collective-permute-start | bytes 786440 | tf_op jit(solution)/shard_map/ppermute | solution.py:429
  9.4 8.4 %collective-permute-start.5 = (bf16[512,640]{1,0:T(8,128)(2,1)S(1)}, bf16[512,640]{1,0:T(8,128)(2,1)S(1)}, u32[]{:S(2)}, u32[]{:S(2)}) collective-permute-start(bf16[512,640]{1,0:T(8,128)(2,1)S(1)} %get-tuple-element.102.w_vg), channel_id=1, source_target_pairs={{0,1},{1,2},{2,0},{3,4},{4,5},{5,6},{6,7},{7,8},{8,9},{9,10},{10,1... | collective-permute-start | bytes 1966088 | tf_op jit(solution)/shard_map/ppermute | solution.py:429
  9.5 17.9 %collective-permute-start.9 = (bf16[512,640]{1,0:T(8,128)(2,1)S(1)}, bf16[512,640]{1,0:T(8,128)(2,1)S(1)}, u32[]{:S(2)}, u32[]{:S(2)}) collective-permute-start(bf16[512,640]{1,0:T(8,128)(2,1)S(1)} %get-tuple-element.96.tg), channel_id=1, source_target_pairs={{31,30},{30,29},{29,31},{28,27},{27,26},{26,25},{25,24},{24,23},{2... | collective-permute-start | bytes 1966088 | tf_op jit(solution)/shard_map/ppermute | solution.py:429
  14.4 2.6 %collective-permute-start.3 = (bf16[576,512]{1,0:T(8,128)(2,1)S(1)}, bf16[576,512]{1,0:T(8,128)(2,1)S(1)}, u32[]{:S(2)}, u32[]{:S(2)}) collective-permute-start(bf16[576,512]{1,0:T(8,128)(2,1)S(1)} %get-tuple-element.98), channel_id=1, source_target_pairs={{0,1},{1,0},{2,3},{3,2},{4,5},{5,4},{6,7},{7,6},{8,9},{9,8},{10,11... | collective-permute-start | bytes 1769480 | tf_op jit(solution)/shard_map/ppermute | solution.py:429
  14.4 3.3 %collective-permute-start.4 = (bf16[576,512]{1,0:T(8,128)(2,1)S(1)}, bf16[576,512]{1,0:T(8,128)(2,1)S(1)}, u32[]{:S(2)}, u32[]{:S(2)}) collective-permute-start(bf16[576,512]{1,0:T(8,128)(2,1)S(1)} %get-tuple-element.99), channel_id=1, source_target_pairs={{0,1},{1,0},{2,3},{3,2},{4,5},{5,4},{6,7},{7,6},{8,9},{9,8},{10,11... | collective-permute-start | bytes 1769480 | tf_op jit(solution)/shard_map/ppermute | solution.py:429
  14.9 7.1 %collective-permute-start.6 = (bf16[512,512]{1,0:T(8,128)(2,1)S(1)}, bf16[512,512]{1,0:T(8,128)(2,1)S(1)}, u32[]{:S(2)}, u32[]{:S(2)}) collective-permute-start(bf16[512,512]{1,0:T(8,128)(2,1)S(1)} %get-tuple-element.104), channel_id=1, source_target_pairs={{0,1},{1,0},{2,3},{3,2},{4,5},{5,4},{6,7},{7,6},{8,9},{9,8},{10,11... | collective-permute-start | bytes 1572872 | tf_op jit(solution)/shard_map/ppermute | solution.py:429
  17.8 13.5 %collective-permute-start.8 = (bf16[512,128]{1,0:T(8,128)(2,1)S(1)}, bf16[512,128]{1,0:T(8,128)(2,1)S(1)}, u32[]{:S(2)}, u32[]{:S(2)}) collective-permute-start(bf16[512,128]{1,0:T(8,128)(2,1)S(1)} %get-tuple-element.108), channel_id=1, source_target_pairs={{0,1},{1,17},{2,4},{3,19},{4,2},{5,21},{6,8},{7,23},{8,6},{9,25},{... | collective-permute-start | bytes 393224 | tf_op jit(solution)/shard_map/ppermute | solution.py:429
  21.9 9.3 %collective-permute-start.7 = (bf16[512,128]{1,0:T(8,128)(2,1)S(1)}, bf16[512,128]{1,0:T(8,128)(2,1)S(1)}, u32[]{:S(2)}, u32[]{:S(2)}) collective-permute-start(bf16[512,128]{1,0:T(8,128)(2,1)S(1)} %get-tuple-element.105.after), channel_id=1, source_target_pairs={{0,2},{1,17},{2,0},{3,19},{4,6},{5,21},{6,4},{7,23},{8,10},{9,25},... | collective-permute-start | bytes 393224 | tf_op jit(solution)/shard_map/ppermute | solution.py:429
  29.1 7.5 %collective-permute-start.10 = (bf16[528,128]{1,0:T(8,128)(2,1)S(1)}, bf16[528,128]{1,0:T(8,128)(2,1)S(1)}, u32[]{:S(2)}, u32[]{:S(2)}) collective-permute-start(bf16[528,128]{1,0:T(8,128)(2,1)S(1)} %get-tuple-element.120.after), channel_id=1, source_target_pairs={{0,16},{1,3},{2,18},{3,1},{4,20},{5,7},{6,22},{7,5},{8,24},{9,11},... | collective-permute-start | bytes 405512 | tf_op jit(solution)/shard_map/ppermute | solution.py:429
  29.2 7.5 %collective-permute-start.11 = (bf16[512,128]{1,0:T(8,128)(2,1)S(1)}, bf16[512,128]{1,0:T(8,128)(2,1)S(1)}, u32[]{:S(2)}, u32[]{:S(2)}) collective-permute-start(bf16[512,128]{1,0:T(8,128)(2,1)S(1)} %get-tuple-element.123), channel_id=1, source_target_pairs={{0,16},{1,0},{2,18},{3,5},{4,20},{5,3},{6,22},{7,9},{8,24},{9,7},{... | collective-permute-start | bytes 393224 | tf_op jit(solution)/shard_map/ppermute | solution.py:429
  31.2 8.0 %collective-permute-start.13 = (bf16[528,128]{1,0:T(8,128)(2,1)S(1)}, bf16[528,128]{1,0:T(8,128)(2,1)S(1)}, u32[]{:S(2)}, u32[]{:S(2)}) collective-permute-start(bf16[528,128]{1,0:T(8,128)(2,1)S(1)} %get-tuple-element.124), channel_id=1, source_target_pairs={{31,30},{30,29},{29,31},{28,27},{27,26},{26,25},{25,24},{24,23},{2... | collective-permute-start | bytes 405512 | tf_op jit(solution)/shard_map/ppermute | solution.py:429
  37.1 2.2 %collective-permute-start.12 = (bf16[512,128]{1,0:T(8,128)(2,1)S(1)}, bf16[512,128]{1,0:T(8,128)(2,1)S(1)}, u32[]{:S(2)}, u32[]{:S(2)}) collective-permute-start(bf16[512,128]{1,0:T(8,128)(2,1)S(1)} %shard_map.61.x_odd), channel_id=1, source_target_pairs={{0,1},{1,0},{2,3},{3,2},{4,5},{5,4},{6,7},{7,6},{8,9},{9,8},{10,11... | collective-permute-start | bytes 393224 | tf_op jit(solution)/shard_map/ppermute | solution.py:429

commit v7 on v6

--- a/solution.py
+++ b/solution.py
@@ -44,7 +44,9 @@
     return (rows == lax.broadcasted_iota(jnp.int32, (order, order), 1)).astype(F32)
 
 
-def local_call(kernel, outs, ins, flops, in_hbm=0, scratch=(), aliases=None, weight=0.001):
+def local_call(
+    kernel, outs, ins, flops, in_hbm=0, scratch=(), aliases=None, weight=0.001, out_in_hbm=False
+):
     vmem = pl.BlockSpec(memory_space=pltpu.VMEM)
     hbm = pl.BlockSpec(memory_space=pl.ANY)
     many = len(outs) > 1
@@ -53,7 +55,7 @@
         kernel,
         out_shape=outs if many else outs[0],
         in_specs=[hbm] * in_hbm + [vmem] * (len(ins) - in_hbm),
-        out_specs=[vmem] * len(outs) if many else vmem,
+        out_specs=[vmem] * len(outs) if many else pl.BlockSpec(memory_space=pltpu.HBM) if out_in_hbm else vmem,
         scratch_shapes=list(scratch),
         input_output_aliases=aliases or {},
         compiler_params=pltpu.CompilerParams(vmem_limit_bytes=VMEM_BYTES),
@@ -345,8 +347,8 @@
         gap = if_left(dot(t, w_vg_gap[:, :order]))
         scale[...] = (near[...].astype(F32) - gap).astype(BF16)
         s_v = dot(scale[...], v_one[...]).astype(BF16)
-        from_left[...] = if_two_left(-dot(scale[...], t)).astype(BF16)
-        from_right[...] = if_two_right(dot(s_v, pair2[:order, :])).astype(BF16)
+        from_left[...] = (-dot(scale[...], t)).astype(BF16)
+        from_right[...] = dot(s_v, pair2[:order, :]).astype(BF16)
 
     by_parity(even, None)
 
@@ -357,8 +359,8 @@
         gap = if_right(dot(v_one[...], right))
         scale[...] = (near[...].astype(F32) - gap).astype(BF16)
         s_t = dot(scale[...], tg[:, :order]).astype(BF16)
-        from_left[...] = if_two_left(dot(s_t, pair1[:order, :])).astype(BF16)
-        from_right[...] = if_two_right(dot(scale[...], v_one[...])).astype(BF16)
+        from_left[...] = dot(s_t, pair1[:order, :]).astype(BF16)
+        from_right[...] = dot(scale[...], v_one[...]).astype(BF16)
 
     by_parity(None, odd)
 
@@ -366,7 +368,8 @@
 def top_value(g, from_left, from_right, a, b, x):
     def top(left, right):
         rows = g.shape[0]
-        change = dot(from_left[...], left[:rows, :]) + dot(from_right[...], right[:rows, :])
+        change = if_two_left(dot(from_left[...], left[:rows, :]))
+        change += if_two_right(dot(from_right[...], right[:rows, :]))
         x[...] = (g[...].astype(F32) + change).astype(BF16)
 
     left_of_two = lax.rem(lax.axis_index(AXES), 4) < 2
@@ -393,12 +396,20 @@
     by_parity(lambda: start(x_even), lambda: start(x_odd))
 
 
-def finish(order, vg_b, x_even, x_odd, rest, x_pair, x_gap, out):
-    def rows(x, x_next, right_on):
-        out[0] = x[...]
-        out[1] = (rest[...] - right_on(dot(vg_b[:, :order], x_next[:order, :]))).astype(BF16)
-
-    by_parity(lambda: rows(x_even, x_pair, same), lambda: rows(x_odd, x_gap, if_right))
+def write_rows(order, vg_b, x, rest, x_next, right_on, out, rows, sem):
+    rows[0] = x[...]
+    rows[1] = (rest[...] - right_on(dot(vg_b[:, :order], x_next[:order, :]))).astype(BF16)
+    copy = pltpu.make_async_copy(rows, out, sem)
+    copy.start()
+    copy.wait()
+
+
+def finish_odd(order, vg_b, x, rest, x_gap, out, rows, sem):
+    by_parity(None, lambda: write_rows(order, vg_b, x, rest, x_gap, if_right, out, rows, sem))
+
+
+def finish_even(order, made, vg_b, x, rest, x_pair, out, rows, sem):
+    by_parity(lambda: write_rows(order, vg_b, x, rest, x_pair, same, out, rows, sem), None)
 
 
 def exchanges(slab, count):
@@ -522,10 +533,15 @@
     x_odd = local_call(top_odd, [slim], [g_odd, left_odd, right_odd, odd_a, odd_b], 2 * thin)
     x_pair = sent(x_odd, pairs)
     rest = local_call(part(start_second, order), [tall], [vg_b, w_b, x_even, x_odd], thin)
+    values = jax.ShapeDtypeStruct((2, order, rhs), BF16)
+    scratch = (pltpu.VMEM(values.shape, BF16), pltpu.SemaphoreType.DMA)
+    made = local_call(
+        part(finish_odd, order),
+        [values], [vg_b, x_odd, rest, x_gap], thin, 0, scratch, out_in_hbm=True,
+    )
     return local_call(
-        part(finish, order),
-        [jax.ShapeDtypeStruct((2, order, rhs), BF16)],
-        [vg_b, x_even, x_odd, rest, x_pair, x_gap], thin,
+        part(finish_even, order),
+        [values], [made, vg_b, x_even, rest, x_pair], thin, 1, scratch, {0: 0}, out_in_hbm=True,
     )
 
 

time: 41 us -> 40.7 us (level); the launches traced: 40.3 us -> 40.5 us
    pallas_call x18 -> x19, Pallas kernels: 14.6 us -> 14.6 us  [local_call(): pl.pallas_call(kernel, out_shape=outs if many else outs[0], in_specs=[hbm...]
  transfers between devices with their start and end apart: 14 -> 14, of which waited for: 6 -> 6; matrix products, arithmetic and copies ran while one was open for 0% -> 0% of each run, Pallas kernels for 29% -> 32%
where the time goes in v7:
time: 40.7 us; the launch traced here: 40.5 us
  Pallas kernels  14.6 us (36%)
  waiting for transfers between devices  12.8 us (31%)
  starting transfers between devices  12.7 us (31%)
    pallas_call x19, Pallas kernels, local_call(): pl.pallas_call(kernel, out_shape=outs if many else outs[0], in_specs=[hbm...  14.6 us
    ppermute x14, waiting for transfers between devices, sent(): return lax.ppermute(block, AXES, route)  12.8 us
    ppermute x14, starting transfers between devices, sent(): return lax.ppermute(block, AXES, route)  12.7 us
  transfers between devices with their start and end apart: 14, of which 6 were waited for; matrix products, arithmetic and copies ran while one was open for 0% of the time, Pallas kernels for 32%

profile of v7, /device:TPU:29, one launch (start us, length us, event | category | flops | bytes accessed | tf_op | source)
XLA Modules:
  0.0 40.5 jit_solution(2171681309176528970)
XLA Ops:
  0.0 1.8 %shard_map.46 = (bf16[512,640]{1,0:T(8,128)(2,1)S(1)}, bf16[512,512]{1,0:T(8,128)(2,1)S(1)}, bf16[512,512]{1,0:T(8,128)(2,1)S(1)}) custom-call(bf16[2,512,512]{2,1,0:T(8,128)(2,1)} %diag.7, bf16[2,512,512]{2,1,0:T(8,128)(2,1)} %upper.7, bf16[2,512,128]{2,1,0:T(8,128)(2,1)} %right.7, bf16[2,512,512]{2,1,0:T(8,128)(2,1)} %lower.5), custom_call_target="tpu_custom_call" | custom-call | flops 335544 | tf_op jit(solution)/shard_map/pallas_call | solution.py:54
  1.8 0.1 collective-permute-start
  1.9 3.0 %shard_map.47 = (bf16[512,512]{1,0:T(8,128)(2,1)S(1)}, bf16[512,512]{1,0:T(8,128)(2,1)S(1)}, f32[512,512]{1,0:T(8,128)S(1)}, bf16[512,512]{1,0:T(8,128)(2,1)S(1)...) custom-call(bf16[2,512,512]{2,1,0:T(8,128)(2,1)} %diag.7, ...), custom_call_target="tpu_custom_call" | custom-call | flops 1476395 | tf_op jit(solution)/shard_map/pallas_call | solution.py:54
  4.9 0.1 shard_map.48
  5.0 0.1 collective-permute-start.1
  5.1 0.5 %collective-permute-start.2 = (bf16[512,256]{1,0:T(8,128)(2,1)S(1)}, bf16[512,256]{1,0:T(8,128)(2,1)S(1)}, u32[]{:S(2)}, u32[]{:S(2)}) collective-permute-start(bf16[512,256]{1,0:T(8,128)(2,1)S(1)} %get-tuple-element.86), channel_id=1, source_target_pairs={{0,1},{1,0},{2,3},{3,2},{4,5},{5,4},{6,7},{7,6},{8,9},{9,8},{10,11... | collective-permute-start | bytes 786440 | tf_op jit(solution)/shard_map/ppermute | solution.py:440
  5.6 0.1 shard_map.49
  5.7 1.5 %collective-permute-done.2.vg1 = bf16[512,256]{1,0:T(8,128)(2,1)S(1)} collective-permute-done((bf16[512,256]{1,0:T(8,128)(2,1)S(1)}, bf16[512,256]{1,0:T(8,128)(2,1)S(1)}, u32[]{:S(2)}, u32[]{:S(2)}) %collective-permute-start.2) | collective-permute-done | bytes 262176 | tf_op jit(solution)/shard_map/ppermute | solution.py:440
  7.2 0.0 collective-permute-done.1.v0
  7.2 2.2 %shard_map.51 = (bf16[512,640]{1,0:T(8,128)(2,1)S(1)}, bf16[512,512]{1,0:T(8,128)(2,1)S(1)}, bf16[512,640]{1,0:T(8,128)(2,1)S(1)}, bf16[576,512]{1,0:T(8,128)(2,...) custom-call(bf16[512,512]{1,0:T(8,128)(2,1)S(1)} %get-tuple-element.78.rest_0_.w_a, ...), custom_call_target="tpu_custom_call" | custom-call | flops 1342177 | tf_op jit(solution)/shard_map/pallas_call | solution.py:54
  9.4 0.1 collective-permute-start.7
  9.4 0.0 collective-permute-done.after.vg
  9.5 4.8 %collective-permute-start.6 = (bf16[512,640]{1,0:T(8,128)(2,1)S(1)}, bf16[512,640]{1,0:T(8,128)(2,1)S(1)}, u32[]{:S(2)}, u32[]{:S(2)}) collective-permute-start(bf16[512,640]{1,0:T(8,128)(2,1)S(1)} %get-tuple-element.98.tg), channel_id=1, source_target_pairs={{31,30},{30,29},{29,31},{28,27},{27,26},{26,25},{25,24},{24,23},{2... | collective-permute-start | bytes 1966088 | tf_op jit(solution)/shard_map/ppermute | solution.py:440
  14.4 0.1 collective-permute-start.3
  14.4 0.4 %collective-permute-start.4 = (bf16[576,512]{1,0:T(8,128)(2,1)S(1)}, bf16[576,512]{1,0:T(8,128)(2,1)S(1)}, u32[]{:S(2)}, u32[]{:S(2)}) collective-permute-start(bf16[576,512]{1,0:T(8,128)(2,1)S(1)} %get-tuple-element.100), channel_id=1, source_target_pairs={{0,1},{1,0},{2,3},{3,2},{4,5},{5,4},{6,7},{7,6},{8,9},{9,8},{10,11... | collective-permute-start | bytes 1769480 | tf_op jit(solution)/shard_map/ppermute | solution.py:440
  14.9 0.1 collective-permute-start.5
  15.0 2.0 %collective-permute-done.3.pair0 = bf16[576,512]{1,0:T(8,128)(2,1)S(1)} collective-permute-done((bf16[576,512]{1,0:T(8,128)(2,1)S(1)}, bf16[576,512]{1,0:T(8,128)(2,1)S(1)}, u32[]{:S(2)}, u32[]{:S(2)}) %collective-permute-start.3) | collective-permute-done | bytes 589856 | tf_op jit(solution)/shard_map/ppermute | solution.py:440
  16.9 0.8 %collective-permute-done.4.pair1 = bf16[576,512]{1,0:T(8,128)(2,1)S(1)} collective-permute-done((bf16[576,512]{1,0:T(8,128)(2,1)S(1)}, bf16[576,512]{1,0:T(8,128)(2,1)S(1)}, u32[]{:S(2)}, u32[]{:S(2)}) %collective-permute-start.4) | collective-permute-done | bytes 589856 | tf_op jit(solution)/shard_map/ppermute | solution.py:440
  17.8 0.0 collective-permute-done.7.w_vg_gap
  17.8 4.2 %collective-permute-start.11 = (bf16[512,128]{1,0:T(8,128)(2,1)S(1)}, bf16[512,128]{1,0:T(8,128)(2,1)S(1)}, u32[]{:S(2)}, u32[]{:S(2)}) collective-permute-start(bf16[512,128]{1,0:T(8,128)(2,1)S(1)} %get-tuple-element.122), channel_id=1, source_target_pairs={{0,1},{1,17},{2,4},{3,19},{4,2},{5,21},{6,8},{7,23},{8,6},{9,25},{... | collective-permute-start | bytes 393224 | tf_op jit(solution)/shard_map/ppermute | solution.py:440
  21.9 0.0 collective-permute-start.10
  21.9 0.0 collective-permute-done.5.pair2
  21.9 2.4 %shard_map.54 = (bf16[512,512]{1,0:T(8,128)(2,1)S(1)}, bf16[512,512]{1,0:T(8,128)(2,1)S(1)}, bf16[512,512]{1,0:T(8,128)(2,1)S(1)}, bf16[512,512]{1,0:T(8,128)(2,...) custom-call(bf16[512,640]{1,0:T(8,128)(2,1)S(1)} %get-tuple-element., ...), custom_call_target="tpu_custom_call" | custom-call | flops 1677721 | tf_op jit(solution)/shard_map/pallas_call | solution.py:54
  24.4 3.1 %collective-permute-done.6.tg_gap = bf16[512,640]{1,0:T(8,128)(2,1)S(1)} collective-permute-done((bf16[512,640]{1,0:T(8,128)(2,1)S(1)}, bf16[512,640]{1,0:T(8,128)(2,1)S(1)}, u32[]{:S(2)}, u32[]{:S(2)}) %collective-permute-start.6) | collective-permute-done | bytes 655392 | tf_op jit(solution)/shard_map/ppermute | solution.py:440
  27.5 1.6 %shard_map.58 = (bf16[512,128]{1,0:T(8,128)(2,1)S(1)}, bf16[528,128]{1,0:T(8,128)(2,1)S(1)}, bf16[512,128]{1,0:T(8,128)(2,1)S(1)}) custom-call(bf16[512,512]{1,0:T(8,128)(2,1)S(1)} %get-tuple-element.96.v_one, bf16[512,640]{1,0:T(8,128)(2,1)S(1)} %get-tuple-element.97.w_vg, bf16[512,512]{1,0:T(8,128)(2,1)S(1)} %get-tuple-element.102.far, ...), custom_call_target="tpu_custom_call" | custom-call | flops 536870 | tf_op jit(solution)/shard_map/pallas_call | solution.py:54
  29.1 0.1 collective-permute-start.8
  29.2 2.1 %collective-permute-start.9 = (bf16[512,128]{1,0:T(8,128)(2,1)S(1)}, bf16[512,128]{1,0:T(8,128)(2,1)S(1)}, u32[]{:S(2)}, u32[]{:S(2)}) collective-permute-start(bf16[512,128]{1,0:T(8,128)(2,1)S(1)} %get-tuple-element.119), channel_id=1, source_target_pairs={{0,16},{1,0},{2,18},{3,5},{4,20},{5,3},{6,22},{7,9},{8,24},{9,7},{... | collective-permute-start | bytes 393224 | tf_op jit(solution)/shard_map/ppermute | solution.py:440
  31.2 0.0 collective-permute-done.11.b
  31.2 0.0 collective-permute-done.10.a
  31.2 0.2 collective-permute-start.12
  31.5 1.6 %shard_map.59 = (bf16[512,512]{1,0:T(8,128)(2,1)S(1)}, bf16[512,512]{1,0:T(8,128)(2,1)S(1)}) custom-call(bf16[512,640]{1,0:T(8,128)(2,1)S(1)} %get-tuple-element.98.tg, bf16[512,512]{1,0:T(8,128)(2,1)S(1)} %get-tuple-element.96.v_one, bf16[512,512]{1,0:T(8,128)(2,1)S(1)} %get-tuple-element.90.w_b, bf16[512,512]{1,0:T(8,128)(2,1)S(1)} %get-tuple-element.115.near, ...), custom_call_target="tpu_custom_call" | custom-call | flops 1342177 | tf_op jit(solution)/shard_map/pallas_call | solution.py:54
  33.1 3.5 %collective-permute-done.9.b = bf16[512,128]{1,0:T(8,128)(2,1)S(1)} collective-permute-done((bf16[512,128]{1,0:T(8,128)(2,1)S(1)}, bf16[512,128]{1,0:T(8,128)(2,1)S(1)}, u32[]{:S(2)}, u32[]{:S(2)}) %collective-permute-start.9) | collective-permute-done | bytes 131104 | tf_op jit(solution)/shard_map/ppermute | solution.py:440
  36.6 0.0 collective-permute-done.8.a
  36.6 0.4 %shard_map.60.x_odd.x = bf16[512,128]{1,0:T(8,128)(2,1)S(1)} custom-call(bf16[512,128]{1,0:T(8,128)(2,1)S(1)} %get-tuple-element.114.g, bf16[512,512]{1,0:T(8,128)(2,1)S(1)} %get-tuple-element.117.from_left, bf16[512,512]{1,0:T(8,128)(2,1)S(1)} %get-tuple-element.118.from_right, bf16[528,128]{1,0:T(8,128)(2,1)S(1)} %collective-permute-done.8.a, ...), custom_call_target="tpu_custom_call" | custom-call | flops 134217 | tf_op jit(solution)/shard_map/pallas_call | solution.py:54
  37.1 0.1 collective-permute-start.13
  37.1 0.3 shard_map.62.rest
  37.5 1.8 %collective-permute-done.12.x_gap = bf16[528,128]{1,0:T(8,128)(2,1)S(1)} collective-permute-done((bf16[528,128]{1,0:T(8,128)(2,1)S(1)}, bf16[528,128]{1,0:T(8,128)(2,1)S(1)}, u32[]{:S(2)}, u32[]{:S(2)}) %collective-permute-start.12) | collective-permute-done | bytes 135200 | tf_op jit(solution)/shard_map/ppermute | solution.py:440
  39.3 1.0 %shard_map.63.made = bf16[2,512,128]{2,1,0:T(8,128)(2,1)} custom-call(bf16[512,640]{1,0:T(8,128)(2,1)S(1)} %get-tuple-element.69.vg_b, bf16[512,128]{1,0:T(8,128)(2,1)S(1)} %shard_map.60.x_odd.x, f32[512,128]{1,0:T(8,128)S(1)} %shard_map.62.rest, bf16[528,128]{1,0:T(8,128)(2,1)S(1)} %collective-permute-done.12.x_gap), custom_call_target="tpu_custom_call" | custom-call | flops 67108 | tf_op jit(solution)/shard_map/pallas_call | solution.py:54
  40.3 0.0 collective-permute-done.13.x_pair
  (8 shorter events, 0.1 us)
Async XLA Ops:
  1.8 7.6 %collective-permute-start = (bf16[512,640]{1,0:T(8,128)(2,1)S(1)}, bf16[512,640]{1,0:T(8,128)(2,1)S(1)}, u32[]{:S(2)}, u32[]{:S(2)}) collective-permute-start(bf16[512,640]{1,0:T(8,128)(2,1)S(1)} %get-tuple-element.65.vg_odd), channel_id=1, source_target_pairs={{0,1},{1,2},{2,0},{3,4},{4,5},{5,6},{6,7},{7,8},{8,9},{9,10},{10,1... | collective-permute-start | bytes 1966088 | tf_op jit(solution)/shard_map/ppermute | solution.py:440
  5.0 2.2 %collective-permute-start.1 = (bf16[512,384]{1,0:T(8,128)(2,1)S(1)}, bf16[512,384]{1,0:T(8,128)(2,1)S(1)}, u32[]{:S(2)}, u32[]{:S(2)}) collective-permute-start(bf16[512,384]{1,0:T(8,128)(2,1)S(1)} %get-tuple-element.85), channel_id=1, source_target_pairs={{0,1},{1,0},{2,3},{3,2},{4,5},{5,4},{6,7},{7,6},{8,9},{9,8},{10,11... | collective-permute-start | bytes 1179656 | tf_op jit(solution)/shard_map/ppermute | solution.py:440
  5.1 2.1 %collective-permute-start.2 = (bf16[512,256]{1,0:T(8,128)(2,1)S(1)}, bf16[512,256]{1,0:T(8,128)(2,1)S(1)}, u32[]{:S(2)}, u32[]{:S(2)}) collective-permute-start(bf16[512,256]{1,0:T(8,128)(2,1)S(1)} %get-tuple-element.86), channel_id=1, source_target_pairs={{0,1},{1,0},{2,3},{3,2},{4,5},{5,4},{6,7},{7,6},{8,9},{9,8},{10,11... | collective-permute-start | bytes 786440 | tf_op jit(solution)/shard_map/ppermute | solution.py:440
  9.4 8.4 %collective-permute-start.7 = (bf16[512,640]{1,0:T(8,128)(2,1)S(1)}, bf16[512,640]{1,0:T(8,128)(2,1)S(1)}, u32[]{:S(2)}, u32[]{:S(2)}) collective-permute-start(bf16[512,640]{1,0:T(8,128)(2,1)S(1)} %get-tuple-element.97.w_vg), channel_id=1, source_target_pairs={{0,1},{1,2},{2,0},{3,4},{4,5},{5,6},{6,7},{7,8},{8,9},{9,10},{10,1... | collective-permute-start | bytes 1966088 | tf_op jit(solution)/shard_map/ppermute | solution.py:440
  9.5 17.9 %collective-permute-start.6 = (bf16[512,640]{1,0:T(8,128)(2,1)S(1)}, bf16[512,640]{1,0:T(8,128)(2,1)S(1)}, u32[]{:S(2)}, u32[]{:S(2)}) collective-permute-start(bf16[512,640]{1,0:T(8,128)(2,1)S(1)} %get-tuple-element.98.tg), channel_id=1, source_target_pairs={{31,30},{30,29},{29,31},{28,27},{27,26},{26,25},{25,24},{24,23},{2... | collective-permute-start | bytes 1966088 | tf_op jit(solution)/shard_map/ppermute | solution.py:440
  14.4 2.6 %collective-permute-start.3 = (bf16[576,512]{1,0:T(8,128)(2,1)S(1)}, bf16[576,512]{1,0:T(8,128)(2,1)S(1)}, u32[]{:S(2)}, u32[]{:S(2)}) collective-permute-start(bf16[576,512]{1,0:T(8,128)(2,1)S(1)} %get-tuple-element.99), channel_id=1, source_target_pairs={{0,1},{1,0},{2,3},{3,2},{4,5},{5,4},{6,7},{7,6},{8,9},{9,8},{10,11... | collective-permute-start | bytes 1769480 | tf_op jit(solution)/shard_map/ppermute | solution.py:440
  14.4 3.3 %collective-permute-start.4 = (bf16[576,512]{1,0:T(8,128)(2,1)S(1)}, bf16[576,512]{1,0:T(8,128)(2,1)S(1)}, u32[]{:S(2)}, u32[]{:S(2)}) collective-permute-start(bf16[576,512]{1,0:T(8,128)(2,1)S(1)} %get-tuple-element.100), channel_id=1, source_target_pairs={{0,1},{1,0},{2,3},{3,2},{4,5},{5,4},{6,7},{7,6},{8,9},{9,8},{10,11... | collective-permute-start | bytes 1769480 | tf_op jit(solution)/shard_map/ppermute | solution.py:440
  14.9 7.1 %collective-permute-start.5 = (bf16[512,512]{1,0:T(8,128)(2,1)S(1)}, bf16[512,512]{1,0:T(8,128)(2,1)S(1)}, u32[]{:S(2)}, u32[]{:S(2)}) collective-permute-start(bf16[512,512]{1,0:T(8,128)(2,1)S(1)} %get-tuple-element.101), channel_id=1, source_target_pairs={{0,1},{1,0},{2,3},{3,2},{4,5},{5,4},{6,7},{7,6},{8,9},{9,8},{10,11... | collective-permute-start | bytes 1572872 | tf_op jit(solution)/shard_map/ppermute | solution.py:440
  17.8 13.5 %collective-permute-start.11 = (bf16[512,128]{1,0:T(8,128)(2,1)S(1)}, bf16[512,128]{1,0:T(8,128)(2,1)S(1)}, u32[]{:S(2)}, u32[]{:S(2)}) collective-permute-start(bf16[512,128]{1,0:T(8,128)(2,1)S(1)} %get-tuple-element.122), channel_id=1, source_target_pairs={{0,1},{1,17},{2,4},{3,19},{4,2},{5,21},{6,8},{7,23},{8,6},{9,25},{... | collective-permute-start | bytes 393224 | tf_op jit(solution)/shard_map/ppermute | solution.py:440
  21.9 9.3 %collective-permute-start.10 = (bf16[512,128]{1,0:T(8,128)(2,1)S(1)}, bf16[512,128]{1,0:T(8,128)(2,1)S(1)}, u32[]{:S(2)}, u32[]{:S(2)}) collective-permute-start(bf16[512,128]{1,0:T(8,128)(2,1)S(1)} %get-tuple-element.112.after), channel_id=1, source_target_pairs={{0,2},{1,17},{2,0},{3,19},{4,6},{5,21},{6,4},{7,23},{8,10},{9,25},... | collective-permute-start | bytes 393224 | tf_op jit(solution)/shard_map/ppermute | solution.py:440
  29.1 7.5 %collective-permute-start.8 = (bf16[528,128]{1,0:T(8,128)(2,1)S(1)}, bf16[528,128]{1,0:T(8,128)(2,1)S(1)}, u32[]{:S(2)}, u32[]{:S(2)}) collective-permute-start(bf16[528,128]{1,0:T(8,128)(2,1)S(1)} %get-tuple-element.116.after), channel_id=1, source_target_pairs={{0,16},{1,3},{2,18},{3,1},{4,20},{5,7},{6,22},{7,5},{8,24},{9,11},... | collective-permute-start | bytes 405512 | tf_op jit(solution)/shard_map/ppermute | solution.py:440
  29.2 7.5 %collective-permute-start.9 = (bf16[512,128]{1,0:T(8,128)(2,1)S(1)}, bf16[512,128]{1,0:T(8,128)(2,1)S(1)}, u32[]{:S(2)}, u32[]{:S(2)}) collective-permute-start(bf16[512,128]{1,0:T(8,128)(2,1)S(1)} %get-tuple-element.119), channel_id=1, source_target_pairs={{0,16},{1,0},{2,18},{3,5},{4,20},{5,3},{6,22},{7,9},{8,24},{9,7},{... | collective-permute-start | bytes 393224 | tf_op jit(solution)/shard_map/ppermute | solution.py:440
  31.2 8.0 %collective-permute-start.12 = (bf16[528,128]{1,0:T(8,128)(2,1)S(1)}, bf16[528,128]{1,0:T(8,128)(2,1)S(1)}, u32[]{:S(2)}, u32[]{:S(2)}) collective-permute-start(bf16[528,128]{1,0:T(8,128)(2,1)S(1)} %get-tuple-element.124), channel_id=1, source_target_pairs={{31,30},{30,29},{29,31},{28,27},{27,26},{26,25},{25,24},{24,23},{2... | collective-permute-start | bytes 405512 | tf_op jit(solution)/shard_map/ppermute | solution.py:440
  37.1 3.2 %collective-permute-start.13 = (bf16[512,128]{1,0:T(8,128)(2,1)S(1)}, bf16[512,128]{1,0:T(8,128)(2,1)S(1)}, u32[]{:S(2)}, u32[]{:S(2)}) collective-permute-start(bf16[512,128]{1,0:T(8,128)(2,1)S(1)} %shard_map.60.x_odd.x), channel_id=1, source_target_pairs={{0,1},{1,0},{2,3},{3,2},{4,5},{5,4},{6,7},{7,6},{8,9},{9,8},{10,11... | collective-permute-start | bytes 393224 | tf_op jit(solution)/shard_map/ppermute | solution.py:440

commit v8 on v7

--- a/solution.py
+++ b/solution.py
@@ -45,7 +45,7 @@
 
 
 def local_call(
-    kernel, outs, ins, flops, in_hbm=0, scratch=(), aliases=None, weight=0.001, out_in_hbm=False
+    kernel, outs, ins, flops, in_hbm=0, scratch=(), aliases=None, out_in_hbm=False
 ):
     vmem = pl.BlockSpec(memory_space=pltpu.VMEM)
     hbm = pl.BlockSpec(memory_space=pl.ANY)
@@ -59,7 +59,7 @@
         scratch_shapes=list(scratch),
         input_output_aliases=aliases or {},
         compiler_params=pltpu.CompilerParams(vmem_limit_bytes=VMEM_BYTES),
-        cost_estimate=pl.CostEstimate(flops=int(flops * weight), bytes_accessed=0, transcendentals=0),
+        cost_estimate=pl.CostEstimate(flops=flops // 1000, bytes_accessed=0, transcendentals=0),
     )(*ins)
 
 
@@ -314,20 +314,20 @@
     by_parity(even, None)
 
 
+def less_gap(start, gap, g_right, further, from_right):
+    return (start[...] - if_right(dot(gap[...], g_right)) - dot(further, from_right)).astype(BF16)
+
+
 def level_two_odd(
-    order, v_one, w_vg, far, w_far, p_far, p_v, n_h, w_h, w_n_h, p_n_h, tg_gap, after, g, a, b
+    order, w_vg, w_far, p_far, p_v, w_h, w_n_h, p_n_h, tg_gap, after, from_right, a, b
 ):
     def odd():
         g_right, w_v = tg_gap[:, order:], w_vg[:, :order]
-        own = w_h[...] - if_right(dot(w_v, g_right))
-        from_right = if_right(dot(tg_gap[:, :order], own.astype(BF16))).astype(BF16)
-
-        def whole(start, gap, further):
-            gap_part = if_right(dot(gap[...], g_right)) + dot(further, from_right)
-            return (start[...] - gap_part).astype(BF16)
-
-        g[...] = whole(n_h, far, v_one[...])
-        hand_out(whole(w_n_h, w_far, w_v), whole(p_n_h, p_far, p_v[...]), a, b)
+        own = (w_h[...] - if_right(dot(w_v, g_right))).astype(BF16)
+        gap = if_right(dot(tg_gap[:, :order], own)).astype(BF16)
+        from_right[...] = gap
+        to_right = less_gap(w_n_h, w_far, g_right, w_v, gap)
+        hand_out(to_right, less_gap(p_n_h, p_far, g_right, p_v[...], gap), a, b)
 
     by_parity(None, odd)
 
@@ -353,14 +353,17 @@
     by_parity(even, None)
 
 
-def spikes_two_odd(order, tg, v_one, w_b, near, pair1, tg_gap, after, from_left, from_right, scale):
-    def odd():
-        right = dot(tg_gap[:, :order], w_b[...]).astype(BF16)
-        gap = if_right(dot(v_one[...], right))
+def spikes_two_odd(
+    order, tg, v_one, w_b, near, far, n_h, pair1, tg_gap, from_right, after, g, left, right, scale
+):
+    def odd():
+        g[...] = less_gap(n_h, far, tg_gap[:, order:], v_one[...], from_right[...])
+        through = dot(tg_gap[:, :order], w_b[...]).astype(BF16)
+        gap = if_right(dot(v_one[...], through))
         scale[...] = (near[...].astype(F32) - gap).astype(BF16)
         s_t = dot(scale[...], tg[:, :order]).astype(BF16)
-        from_left[...] = dot(s_t, pair1[:order, :]).astype(BF16)
-        from_right[...] = dot(scale[...], v_one[...]).astype(BF16)
+        left[...] = dot(s_t, pair1[:order, :]).astype(BF16)
+        right[...] = dot(scale[...], v_one[...]).astype(BF16)
 
     by_parity(None, odd)
 
@@ -396,20 +399,25 @@
     by_parity(lambda: start(x_even), lambda: start(x_odd))
 
 
-def write_rows(order, vg_b, x, rest, x_next, right_on, out, rows, sem):
+def write_rows(order, vg_b, x, rest, x_next, right_on, out, rows, sems):
     rows[0] = x[...]
-    rows[1] = (rest[...] - right_on(dot(vg_b[:, :order], x_next[:order, :]))).astype(BF16)
-    copy = pltpu.make_async_copy(rows, out, sem)
-    copy.start()
-    copy.wait()
-
-
-def finish_odd(order, vg_b, x, rest, x_gap, out, rows, sem):
-    by_parity(None, lambda: write_rows(order, vg_b, x, rest, x_gap, if_right, out, rows, sem))
-
-
-def finish_even(order, made, vg_b, x, rest, x_pair, out, rows, sem):
-    by_parity(lambda: write_rows(order, vg_b, x, rest, x_pair, same, out, rows, sem), None)
+    copies = [fetch(rows.at[0], out.at[0], sems.at[0])]
+    half = order // 2
+    for k in range(2):
+        at = pl.ds(k * half, half)
+        next_part = right_on(dot(vg_b[at, :order], x_next[:order, :]))
+        rows[1, at] = (rest[at, :] - next_part).astype(BF16)
+        copies.append(fetch(rows.at[1, at], out.at[1, at], sems.at[k + 1]))
+    for copy in copies:
+        copy.wait()
+
+
+def finish_odd(order, vg_b, x, rest, x_gap, out, rows, sems):
+    by_parity(None, lambda: write_rows(order, vg_b, x, rest, x_gap, if_right, out, rows, sems))
+
+
+def finish_even(order, made, vg_b, x, rest, x_pair, out, rows, sems):
+    by_parity(lambda: write_rows(order, vg_b, x, rest, x_pair, same, out, rows, sems), None)
 
 
 def exchanges(slab, count):
@@ -516,15 +524,16 @@
         part(spikes_two_even, order),
         [full, full], [tg, v_one, near_even, pair[2], w_vg_gap, a_even], 4 * square, 0, (block,),
     )
-    g_odd, a_odd, b_odd = local_call(
+    from_right, a_odd, b_odd = local_call(
         part(level_two_odd, order),
         [slim, tall_slim, slim],
-        [v_one, w_vg_odd, far, w_far, p_far, p_v, n_h, w_h, w_n_h, p_n_h, tg_gap, left_even], 8 * thin,
+        [w_vg_odd, w_far, p_far, p_v, w_h, w_n_h, p_n_h, tg_gap, left_even], 6 * thin,
     )
     odd_a, odd_b = sent(a_odd, twos[1]), sent(b_odd, other_twos[1])
-    left_odd, right_odd = local_call(
+    g_odd, left_odd, right_odd = local_call(
         part(spikes_two_odd, order),
-        [full, full], [tg, v_one, w_b, near, pair[1], tg_gap, a_odd], 5 * square, 0, (block,),
+        [slim, full, full],
+        [tg, v_one, w_b, near, far, n_h, pair[1], tg_gap, from_right, a_odd], 5 * square, 0, (block,),
     )
     x_even, x_out = local_call(
         top_even, [slim, tall_slim], [g_even, left_even, right_even, even_a, even_b], 2 * thin
@@ -534,7 +543,7 @@
     x_pair = sent(x_odd, pairs)
     rest = local_call(part(start_second, order), [tall], [vg_b, w_b, x_even, x_odd], thin)
     values = jax.ShapeDtypeStruct((2, order, rhs), BF16)
-    scratch = (pltpu.VMEM(values.shape, BF16), pltpu.SemaphoreType.DMA)
+    scratch = (pltpu.VMEM(values.shape, BF16), pltpu.SemaphoreType.DMA((3,)))
     made = local_call(
         part(finish_odd, order),
         [values], [vg_b, x_odd, rest, x_gap], thin, 0, scratch, out_in_hbm=True,

time: 40.7 us -> 40.3 us (level)
  waiting for transfers between devices: 12.8 us -> 12.3 us
    ppermute x14, waiting for transfers between devices: 12.8 us -> 12.3 us  [sent(): return lax.ppermute(block, AXES, route)]
where the time goes in v8:
time: 40.3 us; the launch traced here: 40.2 us
  Pallas kernels  14.6 us (36%)
  starting transfers between devices  13 us (32%)
  waiting for transfers between devices  12.3 us (31%)
    pallas_call x19, Pallas kernels, local_call(): pl.pallas_call(kernel, out_shape=outs if many else outs[0], in_specs=[hbm...  14.6 us
    ppermute x14, starting transfers between devices, sent(): return lax.ppermute(block, AXES, route)  13 us
    ppermute x14, waiting for transfers between devices, sent(): return lax.ppermute(block, AXES, route)  12.3 us
  transfers between devices with their start and end apart: 14, of which 6 were waited for; matrix products, arithmetic and copies ran while one was open for 0% of the time, Pallas kernels for 32%

profile of v8, /device:TPU:29, one launch (start us, length us, event | category | flops | bytes accessed | tf_op | source)
XLA Modules:
  0.0 40.2 jit_solution(1032068931922537080)
XLA Ops:
  0.0 1.8 %shard_map.46 = (bf16[512,640]{1,0:T(8,128)(2,1)S(1)}, bf16[512,512]{1,0:T(8,128)(2,1)S(1)}, bf16[512,512]{1,0:T(8,128)(2,1)S(1)}) custom-call(bf16[2,512,512]{2,1,0:T(8,128)(2,1)} %diag.7, bf16[2,512,512]{2,1,0:T(8,128)(2,1)} %upper.7, bf16[2,512,128]{2,1,0:T(8,128)(2,1)} %right.7, bf16[2,512,512]{2,1,0:T(8,128)(2,1)} %lower.5), custom_call_target="tpu_custom_call" | custom-call | flops 335544 | tf_op jit(solution)/shard_map/pallas_call | solution.py:54
  1.8 0.1 collective-permute-start
  1.9 3.0 %shard_map.47 = (bf16[512,512]{1,0:T(8,128)(2,1)S(1)}, bf16[512,512]{1,0:T(8,128)(2,1)S(1)}, f32[512,512]{1,0:T(8,128)S(1)}, bf16[512,512]{1,0:T(8,128)(2,1)S(1)...) custom-call(bf16[2,512,512]{2,1,0:T(8,128)(2,1)} %diag.7, ...), custom_call_target="tpu_custom_call" | custom-call | flops 1476395 | tf_op jit(solution)/shard_map/pallas_call | solution.py:54
  4.9 0.1 shard_map.48
  5.0 0.1 collective-permute-start.1
  5.1 0.5 %collective-permute-start.2 = (bf16[512,256]{1,0:T(8,128)(2,1)S(1)}, bf16[512,256]{1,0:T(8,128)(2,1)S(1)}, u32[]{:S(2)}, u32[]{:S(2)}) collective-permute-start(bf16[512,256]{1,0:T(8,128)(2,1)S(1)} %get-tuple-element.87), channel_id=1, source_target_pairs={{0,1},{1,0},{2,3},{3,2},{4,5},{5,4},{6,7},{7,6},{8,9},{9,8},{10,11... | collective-permute-start | bytes 786440 | tf_op jit(solution)/shard_map/ppermute | solution.py:448
  5.6 0.1 shard_map.49
  5.7 1.5 %collective-permute-done.2.vg1 = bf16[512,256]{1,0:T(8,128)(2,1)S(1)} collective-permute-done((bf16[512,256]{1,0:T(8,128)(2,1)S(1)}, bf16[512,256]{1,0:T(8,128)(2,1)S(1)}, u32[]{:S(2)}, u32[]{:S(2)}) %collective-permute-start.2) | collective-permute-done | bytes 262176 | tf_op jit(solution)/shard_map/ppermute | solution.py:448
  7.2 0.0 collective-permute-done.1.v0
  7.2 2.2 %shard_map.51 = (bf16[512,640]{1,0:T(8,128)(2,1)S(1)}, bf16[512,512]{1,0:T(8,128)(2,1)S(1)}, bf16[512,640]{1,0:T(8,128)(2,1)S(1)}, bf16[576,512]{1,0:T(8,128)(2,...) custom-call(bf16[512,512]{1,0:T(8,128)(2,1)S(1)} %get-tuple-element.79.rest_0_.w_a, ...), custom_call_target="tpu_custom_call" | custom-call | flops 1342177 | tf_op jit(solution)/shard_map/pallas_call | solution.py:54
  9.4 0.1 collective-permute-start.7
  9.4 0.0 collective-permute-done.after.vg
  9.5 4.8 %collective-permute-start.6 = (bf16[512,640]{1,0:T(8,128)(2,1)S(1)}, bf16[512,640]{1,0:T(8,128)(2,1)S(1)}, u32[]{:S(2)}, u32[]{:S(2)}) collective-permute-start(bf16[512,640]{1,0:T(8,128)(2,1)S(1)} %get-tuple-element.97.tg), channel_id=1, source_target_pairs={{31,30},{30,29},{29,31},{28,27},{27,26},{26,25},{25,24},{24,23},{2... | collective-permute-start | bytes 1966088 | tf_op jit(solution)/shard_map/ppermute | solution.py:448
  14.4 0.1 collective-permute-start.3
  14.4 0.4 %collective-permute-start.4 = (bf16[576,512]{1,0:T(8,128)(2,1)S(1)}, bf16[576,512]{1,0:T(8,128)(2,1)S(1)}, u32[]{:S(2)}, u32[]{:S(2)}) collective-permute-start(bf16[576,512]{1,0:T(8,128)(2,1)S(1)} %get-tuple-element.100), channel_id=1, source_target_pairs={{0,1},{1,0},{2,3},{3,2},{4,5},{5,4},{6,7},{7,6},{8,9},{9,8},{10,11... | collective-permute-start | bytes 1769480 | tf_op jit(solution)/shard_map/ppermute | solution.py:448
  14.9 0.1 collective-permute-start.5
  15.0 2.0 %collective-permute-done.3.pair0 = bf16[576,512]{1,0:T(8,128)(2,1)S(1)} collective-permute-done((bf16[576,512]{1,0:T(8,128)(2,1)S(1)}, bf16[576,512]{1,0:T(8,128)(2,1)S(1)}, u32[]{:S(2)}, u32[]{:S(2)}) %collective-permute-start.3) | collective-permute-done | bytes 589856 | tf_op jit(solution)/shard_map/ppermute | solution.py:448
  16.9 0.8 %collective-permute-done.4.pair1 = bf16[576,512]{1,0:T(8,128)(2,1)S(1)} collective-permute-done((bf16[576,512]{1,0:T(8,128)(2,1)S(1)}, bf16[576,512]{1,0:T(8,128)(2,1)S(1)}, u32[]{:S(2)}, u32[]{:S(2)}) %collective-permute-start.4) | collective-permute-done | bytes 589856 | tf_op jit(solution)/shard_map/ppermute | solution.py:448
  17.8 0.0 collective-permute-done.7.w_vg_gap
  17.8 4.2 %collective-permute-start.11 = (bf16[512,128]{1,0:T(8,128)(2,1)S(1)}, bf16[512,128]{1,0:T(8,128)(2,1)S(1)}, u32[]{:S(2)}, u32[]{:S(2)}) collective-permute-start(bf16[512,128]{1,0:T(8,128)(2,1)S(1)} %get-tuple-element.124), channel_id=1, source_target_pairs={{0,1},{1,17},{2,4},{3,19},{4,2},{5,21},{6,8},{7,23},{8,6},{9,25},{... | collective-permute-start | bytes 393224 | tf_op jit(solution)/shard_map/ppermute | solution.py:448
  21.9 0.0 collective-permute-start.10
  21.9 0.0 collective-permute-done.5.pair2
  21.9 2.4 %shard_map.54 = (bf16[512,512]{1,0:T(8,128)(2,1)S(1)}, bf16[512,512]{1,0:T(8,128)(2,1)S(1)}, bf16[512,512]{1,0:T(8,128)(2,1)S(1)}, bf16[512,512]{1,0:T(8,128)(2,...) custom-call(bf16[512,640]{1,0:T(8,128)(2,1)S(1)} %get-tuple-element., ...), custom_call_target="tpu_custom_call" | custom-call | flops 1677721 | tf_op jit(solution)/shard_map/pallas_call | solution.py:54
  24.4 3.1 %collective-permute-done.6.tg_gap = bf16[512,640]{1,0:T(8,128)(2,1)S(1)} collective-permute-done((bf16[512,640]{1,0:T(8,128)(2,1)S(1)}, bf16[512,640]{1,0:T(8,128)(2,1)S(1)}, u32[]{:S(2)}, u32[]{:S(2)}) %collective-permute-start.6) | collective-permute-done | bytes 655392 | tf_op jit(solution)/shard_map/ppermute | solution.py:448
  27.5 1.3 %shard_map.58 = (bf16[512,128]{1,0:T(8,128)(2,1)S(1)}, bf16[528,128]{1,0:T(8,128)(2,1)S(1)}, bf16[512,128]{1,0:T(8,128)(2,1)S(1)}) custom-call(bf16[512,640]{1,0:T(8,128)(2,1)S(1)} %get-tuple-element.105.w_vg, bf16[512,512]{1,0:T(8,128)(2,1)S(1)} %get-tuple-element.106.w_far, bf16[512,512]{1,0:T(8,128)(2,1)S(1)} %get-tuple-element.107.p_far, ...), custom_call_target="tpu_custom_call" | custom-call | flops 402653 | tf_op jit(solution)/shard_map/pallas_call | solution.py:54
  28.8 0.1 collective-permute-start.8
  28.9 2.1 %collective-permute-start.9 = (bf16[512,128]{1,0:T(8,128)(2,1)S(1)}, bf16[512,128]{1,0:T(8,128)(2,1)S(1)}, u32[]{:S(2)}, u32[]{:S(2)}) collective-permute-start(bf16[512,128]{1,0:T(8,128)(2,1)S(1)} %get-tuple-element.121), channel_id=1, source_target_pairs={{0,16},{1,0},{2,18},{3,5},{4,20},{5,3},{6,22},{7,9},{8,24},{9,7},{... | collective-permute-start | bytes 393224 | tf_op jit(solution)/shard_map/ppermute | solution.py:448
  31.0 0.0 collective-permute-done.11.b
  31.0 0.0 collective-permute-done.10.a
  31.0 0.5 %collective-permute-start.12 = (bf16[528,128]{1,0:T(8,128)(2,1)S(1)}, bf16[528,128]{1,0:T(8,128)(2,1)S(1)}, u32[]{:S(2)}, u32[]{:S(2)}) collective-permute-start(bf16[528,128]{1,0:T(8,128)(2,1)S(1)} %get-tuple-element.126), channel_id=1, source_target_pairs={{31,30},{30,29},{29,31},{28,27},{27,26},{26,25},{25,24},{24,23},{2... | collective-permute-start | bytes 405512 | tf_op jit(solution)/shard_map/ppermute | solution.py:448
  31.5 1.9 %shard_map.59 = (bf16[512,128]{1,0:T(8,128)(2,1)S(1)}, bf16[512,512]{1,0:T(8,128)(2,1)S(1)}, bf16[512,512]{1,0:T(8,128)(2,1)S(1)}) custom-call(bf16[512,640]{1,0:T(8,128)(2,1)S(1)} %get-tuple-element.97.tg, bf16[512,512]{1,0:T(8,128)(2,1)S(1)} %get-tuple-element.98.v_one, bf16[512,512]{1,0:T(8,128)(2,1)S(1)} %get-tuple-element.91.w_b, ...), custom_call_target="tpu_custom_call" | custom-call | flops 1342177 | tf_op jit(solution)/shard_map/pallas_call | solution.py:54
  33.3 3.0 %collective-permute-done.9.b = bf16[512,128]{1,0:T(8,128)(2,1)S(1)} collective-permute-done((bf16[512,128]{1,0:T(8,128)(2,1)S(1)}, bf16[512,128]{1,0:T(8,128)(2,1)S(1)}, u32[]{:S(2)}, u32[]{:S(2)}) %collective-permute-start.9) | collective-permute-done | bytes 131104 | tf_op jit(solution)/shard_map/ppermute | solution.py:448
  36.3 0.0 collective-permute-done.8.a
  36.3 0.4 %shard_map.60.x_odd.x = bf16[512,128]{1,0:T(8,128)(2,1)S(1)} custom-call(bf16[512,128]{1,0:T(8,128)(2,1)S(1)} %get-tuple-element.118.g, bf16[512,512]{1,0:T(8,128)(2,1)S(1)} %get-tuple-element.119.from_left, bf16[512,512]{1,0:T(8,128)(2,1)S(1)} %get-tuple-element.120.from_right, bf16[528,128]{1,0:T(8,128)(2,1)S(1)} %collective-permute-done.8.a, ...), custom_call_target="tpu_custom_call" | custom-call | flops 134217 | tf_op jit(solution)/shard_map/pallas_call | solution.py:54
  36.8 0.1 collective-permute-start.13
  36.9 0.3 shard_map.62.rest
  37.2 1.8 %collective-permute-done.12.x_gap = bf16[528,128]{1,0:T(8,128)(2,1)S(1)} collective-permute-done((bf16[528,128]{1,0:T(8,128)(2,1)S(1)}, bf16[528,128]{1,0:T(8,128)(2,1)S(1)}, u32[]{:S(2)}, u32[]{:S(2)}) %collective-permute-start.12) | collective-permute-done | bytes 135200 | tf_op jit(solution)/shard_map/ppermute | solution.py:448
  39.0 0.9 %shard_map.63.made = bf16[2,512,128]{2,1,0:T(8,128)(2,1)} custom-call(bf16[512,640]{1,0:T(8,128)(2,1)S(1)} %get-tuple-element.70.vg_b, bf16[512,128]{1,0:T(8,128)(2,1)S(1)} %shard_map.60.x_odd.x, f32[512,128]{1,0:T(8,128)S(1)} %shard_map.62.rest, bf16[528,128]{1,0:T(8,128)(2,1)S(1)} %collective-permute-done.12.x_gap), custom_call_target="tpu_custom_call" | custom-call | flops 67108 | tf_op jit(solution)/shard_map/pallas_call | solution.py:54
  40.0 0.0 collective-permute-done.13.x_pair
  40.0 0.1 shard_map.64
  (7 shorter events, 0.1 us)
Async XLA Ops:
  1.8 7.6 %collective-permute-start = (bf16[512,640]{1,0:T(8,128)(2,1)S(1)}, bf16[512,640]{1,0:T(8,128)(2,1)S(1)}, u32[]{:S(2)}, u32[]{:S(2)}) collective-permute-start(bf16[512,640]{1,0:T(8,128)(2,1)S(1)} %get-tuple-element.66.vg_odd), channel_id=1, source_target_pairs={{0,1},{1,2},{2,0},{3,4},{4,5},{5,6},{6,7},{7,8},{8,9},{9,10},{10,1... | collective-permute-start | bytes 1966088 | tf_op jit(solution)/shard_map/ppermute | solution.py:448
  5.0 2.2 %collective-permute-start.1 = (bf16[512,384]{1,0:T(8,128)(2,1)S(1)}, bf16[512,384]{1,0:T(8,128)(2,1)S(1)}, u32[]{:S(2)}, u32[]{:S(2)}) collective-permute-start(bf16[512,384]{1,0:T(8,128)(2,1)S(1)} %get-tuple-element.86), channel_id=1, source_target_pairs={{0,1},{1,0},{2,3},{3,2},{4,5},{5,4},{6,7},{7,6},{8,9},{9,8},{10,11... | collective-permute-start | bytes 1179656 | tf_op jit(solution)/shard_map/ppermute | solution.py:448
  5.1 2.1 %collective-permute-start.2 = (bf16[512,256]{1,0:T(8,128)(2,1)S(1)}, bf16[512,256]{1,0:T(8,128)(2,1)S(1)}, u32[]{:S(2)}, u32[]{:S(2)}) collective-permute-start(bf16[512,256]{1,0:T(8,128)(2,1)S(1)} %get-tuple-element.87), channel_id=1, source_target_pairs={{0,1},{1,0},{2,3},{3,2},{4,5},{5,4},{6,7},{7,6},{8,9},{9,8},{10,11... | collective-permute-start | bytes 786440 | tf_op jit(solution)/shard_map/ppermute | solution.py:448
  9.4 8.4 %collective-permute-start.7 = (bf16[512,640]{1,0:T(8,128)(2,1)S(1)}, bf16[512,640]{1,0:T(8,128)(2,1)S(1)}, u32[]{:S(2)}, u32[]{:S(2)}) collective-permute-start(bf16[512,640]{1,0:T(8,128)(2,1)S(1)} %get-tuple-element.105.w_vg), channel_id=1, source_target_pairs={{0,1},{1,2},{2,0},{3,4},{4,5},{5,6},{6,7},{7,8},{8,9},{9,10},{10,1... | collective-permute-start | bytes 1966088 | tf_op jit(solution)/shard_map/ppermute | solution.py:448
  9.5 17.9 %collective-permute-start.6 = (bf16[512,640]{1,0:T(8,128)(2,1)S(1)}, bf16[512,640]{1,0:T(8,128)(2,1)S(1)}, u32[]{:S(2)}, u32[]{:S(2)}) collective-permute-start(bf16[512,640]{1,0:T(8,128)(2,1)S(1)} %get-tuple-element.97.tg), channel_id=1, source_target_pairs={{31,30},{30,29},{29,31},{28,27},{27,26},{26,25},{25,24},{24,23},{2... | collective-permute-start | bytes 1966088 | tf_op jit(solution)/shard_map/ppermute | solution.py:448
  14.4 2.6 %collective-permute-start.3 = (bf16[576,512]{1,0:T(8,128)(2,1)S(1)}, bf16[576,512]{1,0:T(8,128)(2,1)S(1)}, u32[]{:S(2)}, u32[]{:S(2)}) collective-permute-start(bf16[576,512]{1,0:T(8,128)(2,1)S(1)} %get-tuple-element.99), channel_id=1, source_target_pairs={{0,1},{1,0},{2,3},{3,2},{4,5},{5,4},{6,7},{7,6},{8,9},{9,8},{10,11... | collective-permute-start | bytes 1769480 | tf_op jit(solution)/shard_map/ppermute | solution.py:448
  14.4 3.3 %collective-permute-start.4 = (bf16[576,512]{1,0:T(8,128)(2,1)S(1)}, bf16[576,512]{1,0:T(8,128)(2,1)S(1)}, u32[]{:S(2)}, u32[]{:S(2)}) collective-permute-start(bf16[576,512]{1,0:T(8,128)(2,1)S(1)} %get-tuple-element.100), channel_id=1, source_target_pairs={{0,1},{1,0},{2,3},{3,2},{4,5},{5,4},{6,7},{7,6},{8,9},{9,8},{10,11... | collective-permute-start | bytes 1769480 | tf_op jit(solution)/shard_map/ppermute | solution.py:448
  14.9 7.1 %collective-permute-start.5 = (bf16[512,512]{1,0:T(8,128)(2,1)S(1)}, bf16[512,512]{1,0:T(8,128)(2,1)S(1)}, u32[]{:S(2)}, u32[]{:S(2)}) collective-permute-start(bf16[512,512]{1,0:T(8,128)(2,1)S(1)} %get-tuple-element.101), channel_id=1, source_target_pairs={{0,1},{1,0},{2,3},{3,2},{4,5},{5,4},{6,7},{7,6},{8,9},{9,8},{10,11... | collective-permute-start | bytes 1572872 | tf_op jit(solution)/shard_map/ppermute | solution.py:448
  17.8 13.2 %collective-permute-start.11 = (bf16[512,128]{1,0:T(8,128)(2,1)S(1)}, bf16[512,128]{1,0:T(8,128)(2,1)S(1)}, u32[]{:S(2)}, u32[]{:S(2)}) collective-permute-start(bf16[512,128]{1,0:T(8,128)(2,1)S(1)} %get-tuple-element.124), channel_id=1, source_target_pairs={{0,1},{1,17},{2,4},{3,19},{4,2},{5,21},{6,8},{7,23},{8,6},{9,25},{... | collective-permute-start | bytes 393224 | tf_op jit(solution)/shard_map/ppermute | solution.py:448
  21.9 9.0 %collective-permute-start.10 = (bf16[512,128]{1,0:T(8,128)(2,1)S(1)}, bf16[512,128]{1,0:T(8,128)(2,1)S(1)}, u32[]{:S(2)}, u32[]{:S(2)}) collective-permute-start(bf16[512,128]{1,0:T(8,128)(2,1)S(1)} %get-tuple-element.114.after), channel_id=1, source_target_pairs={{0,2},{1,17},{2,0},{3,19},{4,6},{5,21},{6,4},{7,23},{8,10},{9,25},... | collective-permute-start | bytes 393224 | tf_op jit(solution)/shard_map/ppermute | solution.py:448
  28.8 7.5 %collective-permute-start.8 = (bf16[528,128]{1,0:T(8,128)(2,1)S(1)}, bf16[528,128]{1,0:T(8,128)(2,1)S(1)}, u32[]{:S(2)}, u32[]{:S(2)}) collective-permute-start(bf16[528,128]{1,0:T(8,128)(2,1)S(1)} %get-tuple-element.117.after), channel_id=1, source_target_pairs={{0,16},{1,3},{2,18},{3,1},{4,20},{5,7},{6,22},{7,5},{8,24},{9,11},... | collective-permute-start | bytes 405512 | tf_op jit(solution)/shard_map/ppermute | solution.py:448
  28.9 7.5 %collective-permute-start.9 = (bf16[512,128]{1,0:T(8,128)(2,1)S(1)}, bf16[512,128]{1,0:T(8,128)(2,1)S(1)}, u32[]{:S(2)}, u32[]{:S(2)}) collective-permute-start(bf16[512,128]{1,0:T(8,128)(2,1)S(1)} %get-tuple-element.121), channel_id=1, source_target_pairs={{0,16},{1,0},{2,18},{3,5},{4,20},{5,3},{6,22},{7,9},{8,24},{9,7},{... | collective-permute-start | bytes 393224 | tf_op jit(solution)/shard_map/ppermute | solution.py:448
  31.0 8.0 %collective-permute-start.12 = (bf16[528,128]{1,0:T(8,128)(2,1)S(1)}, bf16[528,128]{1,0:T(8,128)(2,1)S(1)}, u32[]{:S(2)}, u32[]{:S(2)}) collective-permute-start(bf16[528,128]{1,0:T(8,128)(2,1)S(1)} %get-tuple-element.126), channel_id=1, source_target_pairs={{31,30},{30,29},{29,31},{28,27},{27,26},{26,25},{25,24},{24,23},{2... | collective-permute-start | bytes 405512 | tf_op jit(solution)/shard_map/ppermute | solution.py:448
  36.8 3.2 %collective-permute-start.13 = (bf16[512,128]{1,0:T(8,128)(2,1)S(1)}, bf16[512,128]{1,0:T(8,128)(2,1)S(1)}, u32[]{:S(2)}, u32[]{:S(2)}) collective-permute-start(bf16[512,128]{1,0:T(8,128)(2,1)S(1)} %shard_map.60.x_odd.x), channel_id=1, source_target_pairs={{0,1},{1,0},{2,3},{3,2},{4,5},{5,4},{6,7},{7,6},{8,9},{9,8},{10,11... | collective-permute-start | bytes 393224 | tf_op jit(solution)/shard_map/ppermute | solution.py:448

commit v9 on v8

--- a/solution.py
+++ b/solution.py
@@ -50,12 +50,15 @@
     vmem = pl.BlockSpec(memory_space=pltpu.VMEM)
     hbm = pl.BlockSpec(memory_space=pl.ANY)
     many = len(outs) > 1
+    places = [vmem] * len(outs)
+    if out_in_hbm:
+        places[-1] = pl.BlockSpec(memory_space=pltpu.HBM)
     ins = [pltpu.with_memory_space_constraint(x, pltpu.HBM) for x in ins[:in_hbm]] + ins[in_hbm:]
     return pl.pallas_call(
         kernel,
         out_shape=outs if many else outs[0],
         in_specs=[hbm] * in_hbm + [vmem] * (len(ins) - in_hbm),
-        out_specs=[vmem] * len(outs) if many else pl.BlockSpec(memory_space=pltpu.HBM) if out_in_hbm else vmem,
+        out_specs=places if many else places[0],
         scratch_shapes=list(scratch),
         input_output_aliases=aliases or {},
         compiler_params=pltpu.CompilerParams(vmem_limit_bytes=VMEM_BYTES),
@@ -243,14 +246,13 @@
     by_parity(lambda: scale_one(order, w_a, m, r, v_left, g_left, scale, tg), None)
 
 
-def spikes_one_even(order, scale, n, w_b, tg, v_odd, pair0, pair1, pair2, tg_out, v_one, *rest):
-    *to_pair, w_t, w_v, w_g = rest
-
-    def even():
+def spikes_one_even(order, place, scale, n, w_b, tg, *refs):
+    v_one, *to_pair, w_t, w_v, w_g = refs[-7:]
+
+    @pl.when(lax.rem(lax.axis_index(AXES), 4) == place)
+    def _():
         spikes_one(order, scale, n, w_b, tg, v_one, w_t, w_v, w_g)
         hand_to_pair(order, [w_v[...], w_t[...], v_one[...]], w_g[...], to_pair)
-
-    by_parity(even, None)
 
 
 def same(value):
@@ -392,32 +394,32 @@
     by_parity(None, lambda: top_value(g, from_left, from_right, a, b, x))
 
 
-def start_second(order, vg_b, w_b, x_even, x_odd, rest):
+def start_second(order, vg_b, w_b, x_even, x_odd, rest, out, sem):
     def start(x):
+        copy = fetch(x, out.at[0], sem)
         rest[...] = vg_b[:, order:].astype(F32) - dot(w_b[...], x[...])
+        copy.wait()
 
     by_parity(lambda: start(x_even), lambda: start(x_odd))
 
 
-def write_rows(order, vg_b, x, rest, x_next, right_on, out, rows, sems):
-    rows[0] = x[...]
-    copies = [fetch(rows.at[0], out.at[0], sems.at[0])]
-    half = order // 2
+def write_second(order, vg_b, rest, x_next, right_on, out, row, sems):
+    half, copies = order // 2, []
     for k in range(2):
         at = pl.ds(k * half, half)
         next_part = right_on(dot(vg_b[at, :order], x_next[:order, :]))
-        rows[1, at] = (rest[at, :] - next_part).astype(BF16)
-        copies.append(fetch(rows.at[1, at], out.at[1, at], sems.at[k + 1]))
+        row[at, :] = (rest[at, :] - next_part).astype(BF16)
+        copies.append(fetch(row.at[at], out.at[1, at], sems.at[k]))
     for copy in copies:
         copy.wait()
 
 
-def finish_odd(order, vg_b, x, rest, x_gap, out, rows, sems):
-    by_parity(None, lambda: write_rows(order, vg_b, x, rest, x_gap, if_right, out, rows, sems))
-
-
-def finish_even(order, made, vg_b, x, rest, x_pair, out, rows, sems):
-    by_parity(lambda: write_rows(order, vg_b, x, rest, x_pair, same, out, rows, sems), None)
+def finish_odd(order, made, vg_b, rest, x_gap, out, row, sems):
+    by_parity(None, lambda: write_second(order, vg_b, rest, x_gap, if_right, out, row, sems))
+
+
+def finish_even(order, made, vg_b, rest, x_pair, out, row, sems):
+    by_parity(lambda: write_second(order, vg_b, rest, x_pair, same, out, row, sems), None)
 
 
 def exchanges(slab, count):
@@ -500,11 +502,16 @@
         [wide, full], [w_a, m, r, vg_gap, tg_odd], 2 * square + 2 * thin, aliases={4: 0},
     )
     tg, v_one, *to_pair = local_call(
-        part(spikes_one_even, order),
+        part(spikes_one_even, order, 0),
         [wide, full, *shares], [scale, n, w_b, tg, v_odd, *to_pair], 3 * square + thin,
         0, (block, block, side), {3: 0, 4: 1, 5: 2, 6: 3, 7: 4},
     )
     tg_gap = sent(tg, to_left)
+    v_one, *to_pair = local_call(
+        part(spikes_one_even, order, 2),
+        [full, *shares], [scale, n, w_b, tg, v_one, *to_pair], 3 * square + thin,
+        0, (block, block, side), {4: 0, 5: 1, 6: 2, 7: 3},
+    )
     pair = [sent(piece, pairs) for piece in to_pair]
 
     tall, tall_slim = f32_array(order, rhs), bf16_array(order + 16, rhs)
@@ -541,17 +548,17 @@
     x_gap = sent(x_out, to_left)
     x_odd = local_call(top_odd, [slim], [g_odd, left_odd, right_odd, odd_a, odd_b], 2 * thin)
     x_pair = sent(x_odd, pairs)
-    rest = local_call(part(start_second, order), [tall], [vg_b, w_b, x_even, x_odd], thin)
     values = jax.ShapeDtypeStruct((2, order, rhs), BF16)
-    scratch = (pltpu.VMEM(values.shape, BF16), pltpu.SemaphoreType.DMA((3,)))
-    made = local_call(
-        part(finish_odd, order),
-        [values], [vg_b, x_odd, rest, x_gap], thin, 0, scratch, out_in_hbm=True,
-    )
-    return local_call(
-        part(finish_even, order),
-        [values], [made, vg_b, x_even, rest, x_pair], thin, 1, scratch, {0: 0}, out_in_hbm=True,
-    )
+    rest, made = local_call(
+        part(start_second, order),
+        [tall, values], [vg_b, w_b, x_even, x_odd], thin, 0, (pltpu.SemaphoreType.DMA,), None, True,
+    )
+    scratch = (side, pltpu.SemaphoreType.DMA((2,)))
+    for kernel, x_next in ((finish_odd, x_gap), (finish_even, x_pair)):
+        made = local_call(
+            part(kernel, order), [values], [made, vg_b, rest, x_next], thin, 1, scratch, {0: 0}, True
+        )
+    return made
 
 
 def solution(mesh):

time: 40.3 us -> 40.3 us (level)
  waiting for transfers between devices: 12.3 us -> 11.6 us
  Pallas kernels: 14.6 us -> 15.1 us
    ppermute x14, waiting for transfers between devices: 12.3 us -> 11.6 us  [sent(): return lax.ppermute(block, AXES, route)]
    pallas_call x19 -> x20, Pallas kernels: 14.6 us -> 15.1 us  [local_call(): pl.pallas_call(kernel, out_shape=outs if many else outs[0], in_specs=[hbm...]
  transfers between devices with their start and end apart: 14 -> 14, of which waited for: 6 -> 6; matrix products, arithmetic and copies ran while one was open for 0% -> 0% of each run, Pallas kernels for 32% -> 33%
where the time goes in v9:
time: 40.3 us; the launch traced here: 40.2 us
  Pallas kernels  15.1 us (37%)
  starting transfers between devices  13.1 us (33%)
  waiting for transfers between devices  11.6 us (29%)
    pallas_call x20, Pallas kernels, local_call(): pl.pallas_call(kernel, out_shape=outs if many else outs[0], in_specs=[hbm...  15.1 us
    ppermute x14, starting transfers between devices, sent(): return lax.ppermute(block, AXES, route)  13.1 us
    ppermute x14, waiting for transfers between devices, sent(): return lax.ppermute(block, AXES, route)  11.6 us
  transfers between devices with their start and end apart: 14, of which 6 were waited for; matrix products, arithmetic and copies ran while one was open for 0% of the time, Pallas kernels for 33%

profile of v9, /device:TPU:29, one launch (start us, length us, event | category | flops | bytes accessed | tf_op | source)
XLA Modules:
  0.0 40.2 jit_solution(15021258348144428281)
XLA Ops:
  0.0 1.8 %shard_map.46 = (bf16[512,640]{1,0:T(8,128)(2,1)S(1)}, bf16[512,512]{1,0:T(8,128)(2,1)S(1)}, bf16[512,512]{1,0:T(8,128)(2,1)S(1)}) custom-call(bf16[2,512,512]{2,1,0:T(8,128)(2,1)} %diag.7, bf16[2,512,512]{2,1,0:T(8,128)(2,1)} %upper.7, bf16[2,512,128]{2,1,0:T(8,128)(2,1)} %right.7, bf16[2,512,512]{2,1,0:T(8,128)(2,1)} %lower.5), custom_call_target="tpu_custom_call" | custom-call | flops 335544 | tf_op jit(solution)/shard_map/pallas_call | solution.py:57
  1.8 0.1 collective-permute-start
  1.9 3.0 %shard_map.47 = (bf16[512,512]{1,0:T(8,128)(2,1)S(1)}, bf16[512,512]{1,0:T(8,128)(2,1)S(1)}, f32[512,512]{1,0:T(8,128)S(1)}, bf16[512,512]{1,0:T(8,128)(2,1)S(1)...) custom-call(bf16[2,512,512]{2,1,0:T(8,128)(2,1)} %diag.7, ...), custom_call_target="tpu_custom_call" | custom-call | flops 1476395 | tf_op jit(solution)/shard_map/pallas_call | solution.py:57
  4.9 0.1 shard_map.48
  5.0 0.1 collective-permute-start.1
  5.1 0.5 %collective-permute-start.2 = (bf16[512,256]{1,0:T(8,128)(2,1)S(1)}, bf16[512,256]{1,0:T(8,128)(2,1)S(1)}, u32[]{:S(2)}, u32[]{:S(2)}) collective-permute-start(bf16[512,256]{1,0:T(8,128)(2,1)S(1)} %get-tuple-element.94), channel_id=1, source_target_pairs={{0,1},{1,0},{2,3},{3,2},{4,5},{5,4},{6,7},{7,6},{8,9},{9,8},{10,11... | collective-permute-start | bytes 786440 | tf_op jit(solution)/shard_map/ppermute | solution.py:450
  5.6 0.1 shard_map.49
  5.7 1.5 %collective-permute-done.2.vg1 = bf16[512,256]{1,0:T(8,128)(2,1)S(1)} collective-permute-done((bf16[512,256]{1,0:T(8,128)(2,1)S(1)}, bf16[512,256]{1,0:T(8,128)(2,1)S(1)}, u32[]{:S(2)}, u32[]{:S(2)}) %collective-permute-start.2) | collective-permute-done | bytes 262176 | tf_op jit(solution)/shard_map/ppermute | solution.py:450
  7.2 0.0 collective-permute-done.1.v0
  7.2 2.2 %shard_map.51 = (bf16[512,640]{1,0:T(8,128)(2,1)S(1)}, bf16[512,512]{1,0:T(8,128)(2,1)S(1)}, bf16[512,640]{1,0:T(8,128)(2,1)S(1)}, bf16[576,512]{1,0:T(8,128)(2,...) custom-call(bf16[512,512]{1,0:T(8,128)(2,1)S(1)} %get-tuple-element.85.rest_0_.w_a, ...), custom_call_target="tpu_custom_call" | custom-call | flops 1342177 | tf_op jit(solution)/shard_map/pallas_call | solution.py:57
  9.4 0.1 collective-permute-start.5
  9.4 0.0 collective-permute-done.after.vg
  9.5 3.6 %collective-permute-start.9 = (bf16[512,640]{1,0:T(8,128)(2,1)S(1)}, bf16[512,640]{1,0:T(8,128)(2,1)S(1)}, u32[]{:S(2)}, u32[]{:S(2)}) collective-permute-start(bf16[512,640]{1,0:T(8,128)(2,1)S(1)} %get-tuple-element.103.tg), channel_id=1, source_target_pairs={{31,30},{30,29},{29,31},{28,27},{27,26},{26,25},{25,24},{24,23},{2... | collective-permute-start | bytes 1966088 | tf_op jit(solution)/shard_map/ppermute | solution.py:450
  13.2 1.3 %collective-permute-start.3 = (bf16[576,512]{1,0:T(8,128)(2,1)S(1)}, bf16[576,512]{1,0:T(8,128)(2,1)S(1)}, u32[]{:S(2)}, u32[]{:S(2)}) collective-permute-start(bf16[576,512]{1,0:T(8,128)(2,1)S(1)} %get-tuple-element.109), channel_id=1, source_target_pairs={{0,1},{1,0},{2,3},{3,2},{4,5},{5,4},{6,7},{7,6},{8,9},{9,8},{10,11... | collective-permute-start | bytes 1769480 | tf_op jit(solution)/shard_map/ppermute | solution.py:450
  14.5 0.1 collective-permute-start.4
  14.6 0.4 %collective-permute-start.6 = (bf16[512,512]{1,0:T(8,128)(2,1)S(1)}, bf16[512,512]{1,0:T(8,128)(2,1)S(1)}, u32[]{:S(2)}, u32[]{:S(2)}) collective-permute-start(bf16[512,512]{1,0:T(8,128)(2,1)S(1)} %get-tuple-element.115), channel_id=1, source_target_pairs={{0,1},{1,0},{2,3},{3,2},{4,5},{5,4},{6,7},{7,6},{8,9},{9,8},{10,11... | collective-permute-start | bytes 1572872 | tf_op jit(solution)/shard_map/ppermute | solution.py:450
  15.0 1.1 %collective-permute-done.3.pair0 = bf16[576,512]{1,0:T(8,128)(2,1)S(1)} collective-permute-done((bf16[576,512]{1,0:T(8,128)(2,1)S(1)}, bf16[576,512]{1,0:T(8,128)(2,1)S(1)}, u32[]{:S(2)}, u32[]{:S(2)}) %collective-permute-start.3) | collective-permute-done | bytes 589856 | tf_op jit(solution)/shard_map/ppermute | solution.py:450
  16.1 0.8 %collective-permute-done.4.pair1 = bf16[576,512]{1,0:T(8,128)(2,1)S(1)} collective-permute-done((bf16[576,512]{1,0:T(8,128)(2,1)S(1)}, bf16[576,512]{1,0:T(8,128)(2,1)S(1)}, u32[]{:S(2)}, u32[]{:S(2)}) %collective-permute-start.4) | collective-permute-done | bytes 589856 | tf_op jit(solution)/shard_map/ppermute | solution.py:450
  17.0 0.0 collective-permute-done.5.w_vg_gap
  17.0 4.2 %collective-permute-start.8 = (bf16[512,128]{1,0:T(8,128)(2,1)S(1)}, bf16[512,128]{1,0:T(8,128)(2,1)S(1)}, u32[]{:S(2)}, u32[]{:S(2)}) collective-permute-start(bf16[512,128]{1,0:T(8,128)(2,1)S(1)} %get-tuple-element.119), channel_id=1, source_target_pairs={{0,1},{1,17},{2,4},{3,19},{4,2},{5,21},{6,8},{7,23},{8,6},{9,25},{... | collective-permute-start | bytes 393224 | tf_op jit(solution)/shard_map/ppermute | solution.py:450
  21.2 0.0 collective-permute-start.7
  21.2 0.0 collective-permute-done.6.pair2
  21.2 2.6 %shard_map.59 = (bf16[512,512]{1,0:T(8,128)(2,1)S(1)}, bf16[512,512]{1,0:T(8,128)(2,1)S(1)}, bf16[512,512]{1,0:T(8,128)(2,1)S(1)}, bf16[512,512]{1,0:T(8,128)(2,...) custom-call(bf16[512,640]{1,0:T(8,128)(2,1)S(1)} %get-tuple-element., ...), custom_call_target="tpu_custom_call" | custom-call | flops 1677721 | tf_op jit(solution)/shard_map/pallas_call | solution.py:57
  23.8 3.7 %collective-permute-done.9.tg_gap = bf16[512,640]{1,0:T(8,128)(2,1)S(1)} collective-permute-done((bf16[512,640]{1,0:T(8,128)(2,1)S(1)}, bf16[512,640]{1,0:T(8,128)(2,1)S(1)}, u32[]{:S(2)}, u32[]{:S(2)}) %collective-permute-start.9) | collective-permute-done | bytes 655392 | tf_op jit(solution)/shard_map/ppermute | solution.py:450
  27.5 1.3 %shard_map.60 = (bf16[512,128]{1,0:T(8,128)(2,1)S(1)}, bf16[528,128]{1,0:T(8,128)(2,1)S(1)}, bf16[512,128]{1,0:T(8,128)(2,1)S(1)}) custom-call(bf16[512,640]{1,0:T(8,128)(2,1)S(1)} %get-tuple-element.113.w_vg, bf16[512,512]{1,0:T(8,128)(2,1)S(1)} %get-tuple-element.124.w_far, bf16[512,512]{1,0:T(8,128)(2,1)S(1)} %get-tuple-element.125.p_far, ...), custom_call_target="tpu_custom_call" | custom-call | flops 402653 | tf_op jit(solution)/shard_map/pallas_call | solution.py:57
  28.8 0.1 collective-permute-start.10
  28.9 2.1 %collective-permute-start.11 = (bf16[512,128]{1,0:T(8,128)(2,1)S(1)}, bf16[512,128]{1,0:T(8,128)(2,1)S(1)}, u32[]{:S(2)}, u32[]{:S(2)}) collective-permute-start(bf16[512,128]{1,0:T(8,128)(2,1)S(1)} %get-tuple-element.135), channel_id=1, source_target_pairs={{0,16},{1,0},{2,18},{3,5},{4,20},{5,3},{6,22},{7,9},{8,24},{9,7},{... | collective-permute-start | bytes 393224 | tf_op jit(solution)/shard_map/ppermute | solution.py:450
  31.0 0.0 collective-permute-done.8.b
  31.0 0.0 collective-permute-done.7.a
  31.0 0.5 %collective-permute-start.12 = (bf16[528,128]{1,0:T(8,128)(2,1)S(1)}, bf16[528,128]{1,0:T(8,128)(2,1)S(1)}, u32[]{:S(2)}, u32[]{:S(2)}) collective-permute-start(bf16[528,128]{1,0:T(8,128)(2,1)S(1)} %get-tuple-element.138), channel_id=1, source_target_pairs={{31,30},{30,29},{29,31},{28,27},{27,26},{26,25},{25,24},{24,23},{2... | collective-permute-start | bytes 405512 | tf_op jit(solution)/shard_map/ppermute | solution.py:450
  31.5 1.9 %shard_map.61 = (bf16[512,128]{1,0:T(8,128)(2,1)S(1)}, bf16[512,512]{1,0:T(8,128)(2,1)S(1)}, bf16[512,512]{1,0:T(8,128)(2,1)S(1)}) custom-call(bf16[512,640]{1,0:T(8,128)(2,1)S(1)} %get-tuple-element.103.tg, bf16[512,512]{1,0:T(8,128)(2,1)S(1)} %get-tuple-element.108.v_one, bf16[512,512]{1,0:T(8,128)(2,1)S(1)} %get-tuple-element.89.w_b, ...), custom_call_target="tpu_custom_call" | custom-call | flops 1342177 | tf_op jit(solution)/shard_map/pallas_call | solution.py:57
  33.3 3.0 %collective-permute-done.11.b = bf16[512,128]{1,0:T(8,128)(2,1)S(1)} collective-permute-done((bf16[512,128]{1,0:T(8,128)(2,1)S(1)}, bf16[512,128]{1,0:T(8,128)(2,1)S(1)}, u32[]{:S(2)}, u32[]{:S(2)}) %collective-permute-start.11) | collective-permute-done | bytes 131104 | tf_op jit(solution)/shard_map/ppermute | solution.py:450
  36.3 0.0 collective-permute-done.10.a
  36.3 0.4 %shard_map.62.x_odd = bf16[512,128]{1,0:T(8,128)(2,1)S(1)} custom-call(bf16[512,128]{1,0:T(8,128)(2,1)S(1)} %get-tuple-element.132.g, bf16[512,512]{1,0:T(8,128)(2,1)S(1)} %get-tuple-element.133.from_left, bf16[512,512]{1,0:T(8,128)(2,1)S(1)} %get-tuple-element.134.from_right, bf16[528,128]{1,0:T(8,128)(2,1)S(1)} %collective-permute-done.10.a, ...), custom_call_target="tpu_custom_call" | custom-call | flops 134217 | tf_op jit(solution)/shard_map/pallas_call | solution.py:57
  36.8 0.1 collective-permute-start.13
  36.9 0.7 %shard_map.63 = (f32[512,128]{1,0:T(8,128)S(1)}, bf16[2,512,128]{2,1,0:T(8,128)(2,1)}) custom-call(bf16[512,640]{1,0:T(8,128)(2,1)S(1)} %get-tuple-element.76.vg_b, bf16[512,512]{1,0:T(8,128)(2,1)S(1)} %get-tuple-element.89.w_b, bf16[512,128]{1,0:T(8,128)(2,1)S(1)} %get-tuple-element.120.x_even, bf16[512,128]{1,0:T(8,128)(2,1)S(1)} %shard_map.62.x_odd), custom_call_target="tpu_custom_call" | custom-call | flops 67108 | tf_op jit(solution)/shard_map/pallas_call | solution.py:57
  37.6 1.4 %collective-permute-done.12.x_gap = bf16[528,128]{1,0:T(8,128)(2,1)S(1)} collective-permute-done((bf16[528,128]{1,0:T(8,128)(2,1)S(1)}, bf16[528,128]{1,0:T(8,128)(2,1)S(1)}, u32[]{:S(2)}, u32[]{:S(2)}) %collective-permute-start.12) | collective-permute-done | bytes 135200 | tf_op jit(solution)/shard_map/ppermute | solution.py:450
  39.0 0.9 %shard_map.64.made = bf16[2,512,128]{2,1,0:T(8,128)(2,1)} custom-call(bf16[2,512,128]{2,1,0:T(8,128)(2,1)} %get-tuple-element.136.made, bf16[512,640]{1,0:T(8,128)(2,1)S(1)} %get-tuple-element.76.vg_b, f32[512,128]{1,0:T(8,128)S(1)} %get-tuple-element.137.rest, bf16[528,128]{1,0:T(8,128)(2,1)S(1)} %collective-permute-done.12.x_gap), custom_call_target="tpu_custom_call", output_to_operand_aliasing={{}: (0, {})} | custom-call | flops 67108 | tf_op jit(solution)/shard_map/pallas_call | solution.py:57
  39.9 0.0 collective-permute-done.13.x_pair
  (9 shorter events, 0.1 us)
Async XLA Ops:
  1.8 7.6 %collective-permute-start = (bf16[512,640]{1,0:T(8,128)(2,1)S(1)}, bf16[512,640]{1,0:T(8,128)(2,1)S(1)}, u32[]{:S(2)}, u32[]{:S(2)}) collective-permute-start(bf16[512,640]{1,0:T(8,128)(2,1)S(1)} %get-tuple-element.72.vg_odd), channel_id=1, source_target_pairs={{0,1},{1,2},{2,0},{3,4},{4,5},{5,6},{6,7},{7,8},{8,9},{9,10},{10,1... | collective-permute-start | bytes 1966088 | tf_op jit(solution)/shard_map/ppermute | solution.py:450
  5.0 2.2 %collective-permute-start.1 = (bf16[512,384]{1,0:T(8,128)(2,1)S(1)}, bf16[512,384]{1,0:T(8,128)(2,1)S(1)}, u32[]{:S(2)}, u32[]{:S(2)}) collective-permute-start(bf16[512,384]{1,0:T(8,128)(2,1)S(1)} %get-tuple-element.93), channel_id=1, source_target_pairs={{0,1},{1,0},{2,3},{3,2},{4,5},{5,4},{6,7},{7,6},{8,9},{9,8},{10,11... | collective-permute-start | bytes 1179656 | tf_op jit(solution)/shard_map/ppermute | solution.py:450
  5.1 2.1 %collective-permute-start.2 = (bf16[512,256]{1,0:T(8,128)(2,1)S(1)}, bf16[512,256]{1,0:T(8,128)(2,1)S(1)}, u32[]{:S(2)}, u32[]{:S(2)}) collective-permute-start(bf16[512,256]{1,0:T(8,128)(2,1)S(1)} %get-tuple-element.94), channel_id=1, source_target_pairs={{0,1},{1,0},{2,3},{3,2},{4,5},{5,4},{6,7},{7,6},{8,9},{9,8},{10,11... | collective-permute-start | bytes 786440 | tf_op jit(solution)/shard_map/ppermute | solution.py:450
  9.4 7.6 %collective-permute-start.5 = (bf16[512,640]{1,0:T(8,128)(2,1)S(1)}, bf16[512,640]{1,0:T(8,128)(2,1)S(1)}, u32[]{:S(2)}, u32[]{:S(2)}) collective-permute-start(bf16[512,640]{1,0:T(8,128)(2,1)S(1)} %get-tuple-element.113.w_vg), channel_id=1, source_target_pairs={{0,1},{1,2},{2,0},{3,4},{4,5},{5,6},{6,7},{7,8},{8,9},{9,10},{10,1... | collective-permute-start | bytes 1966088 | tf_op jit(solution)/shard_map/ppermute | solution.py:450
  9.5 17.9 %collective-permute-start.9 = (bf16[512,640]{1,0:T(8,128)(2,1)S(1)}, bf16[512,640]{1,0:T(8,128)(2,1)S(1)}, u32[]{:S(2)}, u32[]{:S(2)}) collective-permute-start(bf16[512,640]{1,0:T(8,128)(2,1)S(1)} %get-tuple-element.103.tg), channel_id=1, source_target_pairs={{31,30},{30,29},{29,31},{28,27},{27,26},{26,25},{25,24},{24,23},{2... | collective-permute-start | bytes 1966088 | tf_op jit(solution)/shard_map/ppermute | solution.py:450
  13.2 2.9 %collective-permute-start.3 = (bf16[576,512]{1,0:T(8,128)(2,1)S(1)}, bf16[576,512]{1,0:T(8,128)(2,1)S(1)}, u32[]{:S(2)}, u32[]{:S(2)}) collective-permute-start(bf16[576,512]{1,0:T(8,128)(2,1)S(1)} %get-tuple-element.109), channel_id=1, source_target_pairs={{0,1},{1,0},{2,3},{3,2},{4,5},{5,4},{6,7},{7,6},{8,9},{9,8},{10,11... | collective-permute-start | bytes 1769480 | tf_op jit(solution)/shard_map/ppermute | solution.py:450
  14.5 2.5 %collective-permute-start.4 = (bf16[576,512]{1,0:T(8,128)(2,1)S(1)}, bf16[576,512]{1,0:T(8,128)(2,1)S(1)}, u32[]{:S(2)}, u32[]{:S(2)}) collective-permute-start(bf16[576,512]{1,0:T(8,128)(2,1)S(1)} %get-tuple-element.110), channel_id=1, source_target_pairs={{0,1},{1,0},{2,3},{3,2},{4,5},{5,4},{6,7},{7,6},{8,9},{9,8},{10,11... | collective-permute-start | bytes 1769480 | tf_op jit(solution)/shard_map/ppermute | solution.py:450
  14.6 6.6 %collective-permute-start.6 = (bf16[512,512]{1,0:T(8,128)(2,1)S(1)}, bf16[512,512]{1,0:T(8,128)(2,1)S(1)}, u32[]{:S(2)}, u32[]{:S(2)}) collective-permute-start(bf16[512,512]{1,0:T(8,128)(2,1)S(1)} %get-tuple-element.115), channel_id=1, source_target_pairs={{0,1},{1,0},{2,3},{3,2},{4,5},{5,4},{6,7},{7,6},{8,9},{9,8},{10,11... | collective-permute-start | bytes 1572872 | tf_op jit(solution)/shard_map/ppermute | solution.py:450
  17.0 14.0 %collective-permute-start.8 = (bf16[512,128]{1,0:T(8,128)(2,1)S(1)}, bf16[512,128]{1,0:T(8,128)(2,1)S(1)}, u32[]{:S(2)}, u32[]{:S(2)}) collective-permute-start(bf16[512,128]{1,0:T(8,128)(2,1)S(1)} %get-tuple-element.119), channel_id=1, source_target_pairs={{0,1},{1,17},{2,4},{3,19},{4,2},{5,21},{6,8},{7,23},{8,6},{9,25},{... | collective-permute-start | bytes 393224 | tf_op jit(solution)/shard_map/ppermute | solution.py:450
  21.2 9.8 %collective-permute-start.7 = (bf16[512,128]{1,0:T(8,128)(2,1)S(1)}, bf16[512,128]{1,0:T(8,128)(2,1)S(1)}, u32[]{:S(2)}, u32[]{:S(2)}) collective-permute-start(bf16[512,128]{1,0:T(8,128)(2,1)S(1)} %get-tuple-element.116.after), channel_id=1, source_target_pairs={{0,2},{1,17},{2,0},{3,19},{4,6},{5,21},{6,4},{7,23},{8,10},{9,25},... | collective-permute-start | bytes 393224 | tf_op jit(solution)/shard_map/ppermute | solution.py:450
  28.8 7.5 %collective-permute-start.10 = (bf16[528,128]{1,0:T(8,128)(2,1)S(1)}, bf16[528,128]{1,0:T(8,128)(2,1)S(1)}, u32[]{:S(2)}, u32[]{:S(2)}) collective-permute-start(bf16[528,128]{1,0:T(8,128)(2,1)S(1)} %get-tuple-element.131.after), channel_id=1, source_target_pairs={{0,16},{1,3},{2,18},{3,1},{4,20},{5,7},{6,22},{7,5},{8,24},{9,11},... | collective-permute-start | bytes 405512 | tf_op jit(solution)/shard_map/ppermute | solution.py:450
  28.9 7.5 %collective-permute-start.11 = (bf16[512,128]{1,0:T(8,128)(2,1)S(1)}, bf16[512,128]{1,0:T(8,128)(2,1)S(1)}, u32[]{:S(2)}, u32[]{:S(2)}) collective-permute-start(bf16[512,128]{1,0:T(8,128)(2,1)S(1)} %get-tuple-element.135), channel_id=1, source_target_pairs={{0,16},{1,0},{2,18},{3,5},{4,20},{5,3},{6,22},{7,9},{8,24},{9,7},{... | collective-permute-start | bytes 393224 | tf_op jit(solution)/shard_map/ppermute | solution.py:450
  31.0 8.0 %collective-permute-start.12 = (bf16[528,128]{1,0:T(8,128)(2,1)S(1)}, bf16[528,128]{1,0:T(8,128)(2,1)S(1)}, u32[]{:S(2)}, u32[]{:S(2)}) collective-permute-start(bf16[528,128]{1,0:T(8,128)(2,1)S(1)} %get-tuple-element.138), channel_id=1, source_target_pairs={{31,30},{30,29},{29,31},{28,27},{27,26},{26,25},{25,24},{24,23},{2... | collective-permute-start | bytes 405512 | tf_op jit(solution)/shard_map/ppermute | solution.py:450
  36.8 3.2 %collective-permute-start.13 = (bf16[512,128]{1,0:T(8,128)(2,1)S(1)}, bf16[512,128]{1,0:T(8,128)(2,1)S(1)}, u32[]{:S(2)}, u32[]{:S(2)}) collective-permute-start(bf16[512,128]{1,0:T(8,128)(2,1)S(1)} %shard_map.62.x_odd), channel_id=1, source_target_pairs={{0,1},{1,0},{2,3},{3,2},{4,5},{5,4},{6,7},{7,6},{8,9},{9,8},{10,11... | collective-permute-start | bytes 393224 | tf_op jit(solution)/shard_map/ppermute | solution.py:450

commit v10 on v9

--- a/solution.py
+++ b/solution.py
@@ -227,16 +227,15 @@
     return unpack(jnp.concatenate([piece[order:, :] for piece in got], axis=0), columns)
 
 
-def level_one_odd(order, w_a, m, r, v0, vg1, n, w_b, tg, v_one, w_vg, *rest):
-    *to_pair, scale, w_t = rest
+def level_one_odd(order, w_a, m, r, v0, vg1, n, w_b, tg, v_one, w_vg, scale):
     columns = order - v0.shape[1]
 
     def odd():
         v_left, g_left = [v0, vg1.at[:, :columns]], vg1.at[:, columns:]
         scale_one(order, w_a, m, r, v_left, g_left, scale, tg)
-        w_v, w_g = w_vg.at[:, :order], w_vg.at[:, order:]
-        spikes_one(order, scale, n, w_b, tg, v_one, w_t, w_v, w_g)
-        hand_to_pair(order, [tg[:, :order], w_t[...], v_one[...]], tg[:, order:], to_pair)
+        v_one[...] = (-dot(scale[...], n[...])).astype(BF16)
+        w_vg[:, :order] = dot(w_b[...], v_one[...]).astype(BF16)
+        w_vg[:, order:] = dot(w_b[...], tg[:, order:]).astype(BF16)
 
     by_parity(None, odd)
 
@@ -253,6 +252,17 @@
     def _():
         spikes_one(order, scale, n, w_b, tg, v_one, w_t, w_v, w_g)
         hand_to_pair(order, [w_v[...], w_t[...], v_one[...]], w_g[...], to_pair)
+
+
+def spikes_one_first(order, scale, n, w_b, tg, v_odd, tg_out, v_one, *rest):
+    *to_pair, w_t, w_v, w_g = rest
+    spikes_one_even(order, 0, scale, n, w_b, tg, v_one, *rest)
+
+    def odd():
+        w_t[...] = dot(w_b[...], tg[:, :order]).astype(BF16)
+        hand_to_pair(order, [tg[:, :order], w_t[...], v_odd[...]], tg[:, order:], to_pair)
+
+    by_parity(None, odd)
 
 
 def same(value):
@@ -487,9 +497,9 @@
     )
     w_a, w_b, m, n = spikes
     shares = [bf16_array(order + rows, order) for rows in (rhs // 2, rhs // 2, 0)]
-    tg_odd, v_odd, w_vg_odd, *to_pair = local_call(
+    tg_odd, v_odd, w_vg_odd = local_call(
         part(level_one_odd, order),
-        [wide, full, wide, *shares], [w_a, m, r, *vg_pair, n, w_b], 5 * square, 0, (block, block),
+        [wide, full, wide], [w_a, m, r, *vg_pair, n, w_b], 4 * square, 0, (block,),
     )
     w_vg_gap = sent(w_vg_odd, to_right)
     w_a, w_b, m, n = local_call(
@@ -502,9 +512,9 @@
         [wide, full], [w_a, m, r, vg_gap, tg_odd], 2 * square + 2 * thin, aliases={4: 0},
     )
     tg, v_one, *to_pair = local_call(
-        part(spikes_one_even, order, 0),
-        [wide, full, *shares], [scale, n, w_b, tg, v_odd, *to_pair], 3 * square + thin,
-        0, (block, block, side), {3: 0, 4: 1, 5: 2, 6: 3, 7: 4},
+        part(spikes_one_first, order),
+        [wide, full, *shares], [scale, n, w_b, tg, v_odd], 3 * square + thin,
+        0, (block, block, side), {3: 0, 4: 1},
     )
     tg_gap = sent(tg, to_left)
     v_one, *to_pair = local_call(

time: 40.3 us -> 40 us (level)
  transfers between devices with their start and end apart: 14 -> 14, of which waited for: 6 -> 7; matrix products, arithmetic and copies ran while one was open for 0% -> 0% of each run, Pallas kernels for 33% -> 33%
where the time goes in v10:
time: 40 us; the launch traced here: 39.8 us
  Pallas kernels  15.2 us (38%)
  starting transfers between devices  12.7 us (32%)
  waiting for transfers between devices  11.7 us (29%)
    pallas_call x20, Pallas kernels, local_call(): pl.pallas_call(kernel, out_shape=outs if many else outs[0], in_specs=[hbm...  15.2 us
    ppermute x14, starting transfers between devices, sent(): return lax.ppermute(block, AXES, route)  12.7 us
    ppermute x14, waiting for transfers between devices, sent(): return lax.ppermute(block, AXES, route)  11.7 us
  transfers between devices with their start and end apart: 14, of which 7 were waited for; matrix products, arithmetic and copies ran while one was open for 0% of the time, Pallas kernels for 33%

profile of v10, /device:TPU:29, one launch (start us, length us, event | category | flops | bytes accessed | tf_op | source)
XLA Modules:
  0.0 39.8 jit_solution(2269758802621325661)
XLA Ops:
  0.0 1.8 %shard_map.46 = (bf16[512,640]{1,0:T(8,128)(2,1)S(1)}, bf16[512,512]{1,0:T(8,128)(2,1)S(1)}, bf16[512,512]{1,0:T(8,128)(2,1)S(1)}) custom-call(bf16[2,512,512]{2,1,0:T(8,128)(2,1)} %diag.7, bf16[2,512,512]{2,1,0:T(8,128)(2,1)} %upper.7, bf16[2,512,128]{2,1,0:T(8,128)(2,1)} %right.7, bf16[2,512,512]{2,1,0:T(8,128)(2,1)} %lower.5), custom_call_target="tpu_custom_call" | custom-call | flops 335544 | tf_op jit(solution)/shard_map/pallas_call | solution.py:57
  1.8 0.1 collective-permute-start
  1.9 3.0 %shard_map.47 = (bf16[512,512]{1,0:T(8,128)(2,1)S(1)}, bf16[512,512]{1,0:T(8,128)(2,1)S(1)}, f32[512,512]{1,0:T(8,128)S(1)}, bf16[512,512]{1,0:T(8,128)(2,1)S(1)...) custom-call(bf16[2,512,512]{2,1,0:T(8,128)(2,1)} %diag.7, ...), custom_call_target="tpu_custom_call" | custom-call | flops 1476395 | tf_op jit(solution)/shard_map/pallas_call | solution.py:57
  4.9 0.1 shard_map.48
  5.0 0.1 collective-permute-start.1
  5.1 0.5 %collective-permute-start.2 = (bf16[512,256]{1,0:T(8,128)(2,1)S(1)}, bf16[512,256]{1,0:T(8,128)(2,1)S(1)}, u32[]{:S(2)}, u32[]{:S(2)}) collective-permute-start(bf16[512,256]{1,0:T(8,128)(2,1)S(1)} %get-tuple-element.91), channel_id=1, source_target_pairs={{0,1},{1,0},{2,3},{3,2},{4,5},{5,4},{6,7},{7,6},{8,9},{9,8},{10,11... | collective-permute-start | bytes 786440 | tf_op jit(solution)/shard_map/ppermute | solution.py:460
  5.6 0.1 shard_map.49
  5.7 1.5 %collective-permute-done.2.vg1 = bf16[512,256]{1,0:T(8,128)(2,1)S(1)} collective-permute-done((bf16[512,256]{1,0:T(8,128)(2,1)S(1)}, bf16[512,256]{1,0:T(8,128)(2,1)S(1)}, u32[]{:S(2)}, u32[]{:S(2)}) %collective-permute-start.2) | collective-permute-done | bytes 262176 | tf_op jit(solution)/shard_map/ppermute | solution.py:460
  7.2 0.0 collective-permute-done.1.v0
  7.2 1.9 %shard_map.51 = (bf16[512,640]{1,0:T(8,128)(2,1)S(1)}, bf16[512,512]{1,0:T(8,128)(2,1)S(1)}, bf16[512,640]{1,0:T(8,128)(2,1)S(1)}) custom-call(bf16[512,512]{1,0:T(8,128)(2,1)S(1)} %get-tuple-element.82.rest_0_.w_a, f32[512,512]{1,0:T(8,128)S(1)} %get-tuple-element.84.rest_2_.m, f32[512,128]{1,0:T(8,128)S(1)} %get-tuple-element.89.r, ...), custom_call_target="tpu_custom_call" | custom-call | flops 1073741 | tf_op jit(solution)/shard_map/pallas_call | solution.py:57
  9.1 0.1 collective-permute-start.5
  9.1 0.3 collective-permute-done.after.vg
  9.4 0.4 %shard_map.53 = (bf16[512,640]{1,0:T(8,128)(2,1)S(1)}, bf16[512,512]{1,0:T(8,128)(2,1)S(1)}, bf16[576,512]{1,0:T(8,128)(2,1)S(1)}, bf16[576,512]{1,0:T(8,128)(2,1)S(1)}, bf16[512,512]{1,0:T(8,128)(2,1)S(1)}) custom-call(bf16[512,512]{1,0:T(8,128)(2,1)S(1)} %get-tuple-element.93.scale, ...), custom_call_target="tpu_custom_call", output_to_operand_aliasing={{0}: (3, {}), {1}: (4, {})} | custom-call | flops 872415 | tf_op jit(solution)/shard_map/pallas_call | solution.py:57
  9.9 3.3 %collective-permute-start.9 = (bf16[512,640]{1,0:T(8,128)(2,1)S(1)}, bf16[512,640]{1,0:T(8,128)(2,1)S(1)}, u32[]{:S(2)}, u32[]{:S(2)}) collective-permute-start(bf16[512,640]{1,0:T(8,128)(2,1)S(1)} %get-tuple-element.97.tg), channel_id=1, source_target_pairs={{31,30},{30,29},{29,31},{28,27},{27,26},{26,25},{25,24},{24,23},{2... | collective-permute-start | bytes 1966088 | tf_op jit(solution)/shard_map/ppermute | solution.py:460
  13.2 1.3 %collective-permute-start.3 = (bf16[576,512]{1,0:T(8,128)(2,1)S(1)}, bf16[576,512]{1,0:T(8,128)(2,1)S(1)}, u32[]{:S(2)}, u32[]{:S(2)}) collective-permute-start(bf16[576,512]{1,0:T(8,128)(2,1)S(1)} %get-tuple-element.103), channel_id=1, source_target_pairs={{0,1},{1,0},{2,3},{3,2},{4,5},{5,4},{6,7},{7,6},{8,9},{9,8},{10,11... | collective-permute-start | bytes 1769480 | tf_op jit(solution)/shard_map/ppermute | solution.py:460
  14.5 0.1 collective-permute-start.4
  14.6 0.4 %collective-permute-start.6 = (bf16[512,512]{1,0:T(8,128)(2,1)S(1)}, bf16[512,512]{1,0:T(8,128)(2,1)S(1)}, u32[]{:S(2)}, u32[]{:S(2)}) collective-permute-start(bf16[512,512]{1,0:T(8,128)(2,1)S(1)} %get-tuple-element.109), channel_id=1, source_target_pairs={{0,1},{1,0},{2,3},{3,2},{4,5},{5,4},{6,7},{7,6},{8,9},{9,8},{10,11... | collective-permute-start | bytes 1572872 | tf_op jit(solution)/shard_map/ppermute | solution.py:460
  15.0 1.1 %collective-permute-done.3.pair0 = bf16[576,512]{1,0:T(8,128)(2,1)S(1)} collective-permute-done((bf16[576,512]{1,0:T(8,128)(2,1)S(1)}, bf16[576,512]{1,0:T(8,128)(2,1)S(1)}, u32[]{:S(2)}, u32[]{:S(2)}) %collective-permute-start.3) | collective-permute-done | bytes 589856 | tf_op jit(solution)/shard_map/ppermute | solution.py:460
  16.1 0.8 %collective-permute-done.4.pair1 = bf16[576,512]{1,0:T(8,128)(2,1)S(1)} collective-permute-done((bf16[576,512]{1,0:T(8,128)(2,1)S(1)}, bf16[576,512]{1,0:T(8,128)(2,1)S(1)}, u32[]{:S(2)}, u32[]{:S(2)}) %collective-permute-start.4) | collective-permute-done | bytes 589856 | tf_op jit(solution)/shard_map/ppermute | solution.py:460
  17.0 0.0 collective-permute-done.5.w_vg_gap
  17.0 4.2 %collective-permute-start.8 = (bf16[512,128]{1,0:T(8,128)(2,1)S(1)}, bf16[512,128]{1,0:T(8,128)(2,1)S(1)}, u32[]{:S(2)}, u32[]{:S(2)}) collective-permute-start(bf16[512,128]{1,0:T(8,128)(2,1)S(1)} %get-tuple-element.113), channel_id=1, source_target_pairs={{0,1},{1,17},{2,4},{3,19},{4,2},{5,21},{6,8},{7,23},{8,6},{9,25},{... | collective-permute-start | bytes 393224 | tf_op jit(solution)/shard_map/ppermute | solution.py:460
  21.1 0.0 collective-permute-start.7
  21.1 0.0 collective-permute-done.6.pair2
  21.1 2.6 %shard_map.59 = (bf16[512,512]{1,0:T(8,128)(2,1)S(1)}, bf16[512,512]{1,0:T(8,128)(2,1)S(1)}, bf16[512,512]{1,0:T(8,128)(2,1)S(1)}, bf16[512,512]{1,0:T(8,128)(2,...) custom-call(bf16[512,640]{1,0:T(8,128)(2,1)S(1)} %get-tuple-element., ...), custom_call_target="tpu_custom_call" | custom-call | flops 1677721 | tf_op jit(solution)/shard_map/pallas_call | solution.py:57
  23.7 3.7 %collective-permute-done.9.tg_gap = bf16[512,640]{1,0:T(8,128)(2,1)S(1)} collective-permute-done((bf16[512,640]{1,0:T(8,128)(2,1)S(1)}, bf16[512,640]{1,0:T(8,128)(2,1)S(1)}, u32[]{:S(2)}, u32[]{:S(2)}) %collective-permute-start.9) | collective-permute-done | bytes 655392 | tf_op jit(solution)/shard_map/ppermute | solution.py:460
  27.5 1.3 %shard_map.60 = (bf16[512,128]{1,0:T(8,128)(2,1)S(1)}, bf16[528,128]{1,0:T(8,128)(2,1)S(1)}, bf16[512,128]{1,0:T(8,128)(2,1)S(1)}) custom-call(bf16[512,640]{1,0:T(8,128)(2,1)S(1)} %get-tuple-element.107.w_vg, bf16[512,512]{1,0:T(8,128)(2,1)S(1)} %get-tuple-element.118.w_far, bf16[512,512]{1,0:T(8,128)(2,1)S(1)} %get-tuple-element.119.p_far, ...), custom_call_target="tpu_custom_call" | custom-call | flops 402653 | tf_op jit(solution)/shard_map/pallas_call | solution.py:57
  28.8 0.1 collective-permute-start.10
  28.9 1.8 %collective-permute-start.11 = (bf16[512,128]{1,0:T(8,128)(2,1)S(1)}, bf16[512,128]{1,0:T(8,128)(2,1)S(1)}, u32[]{:S(2)}, u32[]{:S(2)}) collective-permute-start(bf16[512,128]{1,0:T(8,128)(2,1)S(1)} %get-tuple-element.129), channel_id=1, source_target_pairs={{0,16},{1,0},{2,18},{3,5},{4,20},{5,3},{6,22},{7,9},{8,24},{9,7},{... | collective-permute-start | bytes 393224 | tf_op jit(solution)/shard_map/ppermute | solution.py:460
  30.6 0.0 collective-permute-done.8.b
  30.7 0.0 collective-permute-done.7.a
  30.7 0.8 %collective-permute-start.12 = (bf16[528,128]{1,0:T(8,128)(2,1)S(1)}, bf16[528,128]{1,0:T(8,128)(2,1)S(1)}, u32[]{:S(2)}, u32[]{:S(2)}) collective-permute-start(bf16[528,128]{1,0:T(8,128)(2,1)S(1)} %get-tuple-element.132), channel_id=1, source_target_pairs={{31,30},{30,29},{29,31},{28,27},{27,26},{26,25},{25,24},{24,23},{2... | collective-permute-start | bytes 405512 | tf_op jit(solution)/shard_map/ppermute | solution.py:460
  31.5 1.9 %shard_map.61 = (bf16[512,128]{1,0:T(8,128)(2,1)S(1)}, bf16[512,512]{1,0:T(8,128)(2,1)S(1)}, bf16[512,512]{1,0:T(8,128)(2,1)S(1)}) custom-call(bf16[512,640]{1,0:T(8,128)(2,1)S(1)} %get-tuple-element.97.tg, bf16[512,512]{1,0:T(8,128)(2,1)S(1)} %get-tuple-element.102.v_one, bf16[512,512]{1,0:T(8,128)(2,1)S(1)} %get-tuple-element.86.w_b, ...), custom_call_target="tpu_custom_call" | custom-call | flops 1342177 | tf_op jit(solution)/shard_map/pallas_call | solution.py:57
  33.3 3.0 %collective-permute-done.11.b = bf16[512,128]{1,0:T(8,128)(2,1)S(1)} collective-permute-done((bf16[512,128]{1,0:T(8,128)(2,1)S(1)}, bf16[512,128]{1,0:T(8,128)(2,1)S(1)}, u32[]{:S(2)}, u32[]{:S(2)}) %collective-permute-start.11) | collective-permute-done | bytes 131104 | tf_op jit(solution)/shard_map/ppermute | solution.py:460
  36.3 0.0 collective-permute-done.10.a
  36.3 0.4 %shard_map.62.x_odd = bf16[512,128]{1,0:T(8,128)(2,1)S(1)} custom-call(bf16[512,128]{1,0:T(8,128)(2,1)S(1)} %get-tuple-element.126.g, bf16[512,512]{1,0:T(8,128)(2,1)S(1)} %get-tuple-element.127.from_left, bf16[512,512]{1,0:T(8,128)(2,1)S(1)} %get-tuple-element.128.from_right, bf16[528,128]{1,0:T(8,128)(2,1)S(1)} %collective-permute-done.10.a, ...), custom_call_target="tpu_custom_call" | custom-call | flops 134217 | tf_op jit(solution)/shard_map/pallas_call | solution.py:57
  36.8 0.1 collective-permute-start.13
  36.9 0.7 %shard_map.63 = (f32[512,128]{1,0:T(8,128)S(1)}, bf16[2,512,128]{2,1,0:T(8,128)(2,1)}) custom-call(bf16[512,640]{1,0:T(8,128)(2,1)S(1)} %get-tuple-element.73.vg_b, bf16[512,512]{1,0:T(8,128)(2,1)S(1)} %get-tuple-element.86.w_b, bf16[512,128]{1,0:T(8,128)(2,1)S(1)} %get-tuple-element.114.x_even, bf16[512,128]{1,0:T(8,128)(2,1)S(1)} %shard_map.62.x_odd), custom_call_target="tpu_custom_call" | custom-call | flops 67108 | tf_op jit(solution)/shard_map/pallas_call | solution.py:57
  37.6 1.1 %collective-permute-done.12.x_gap = bf16[528,128]{1,0:T(8,128)(2,1)S(1)} collective-permute-done((bf16[528,128]{1,0:T(8,128)(2,1)S(1)}, bf16[528,128]{1,0:T(8,128)(2,1)S(1)}, u32[]{:S(2)}, u32[]{:S(2)}) %collective-permute-start.12) | collective-permute-done | bytes 135200 | tf_op jit(solution)/shard_map/ppermute | solution.py:460
  38.7 0.9 %shard_map.64.made = bf16[2,512,128]{2,1,0:T(8,128)(2,1)} custom-call(bf16[2,512,128]{2,1,0:T(8,128)(2,1)} %get-tuple-element.130.made, bf16[512,640]{1,0:T(8,128)(2,1)S(1)} %get-tuple-element.73.vg_b, f32[512,128]{1,0:T(8,128)S(1)} %get-tuple-element.131.rest, bf16[528,128]{1,0:T(8,128)(2,1)S(1)} %collective-permute-done.12.x_gap), custom_call_target="tpu_custom_call", output_to_operand_aliasing={{}: (0, {})} | custom-call | flops 67108 | tf_op jit(solution)/shard_map/pallas_call | solution.py:57
  39.6 0.0 collective-permute-done.13.x_pair
  (8 shorter events, 0.0 us)
Async XLA Ops:
  1.8 7.6 %collective-permute-start = (bf16[512,640]{1,0:T(8,128)(2,1)S(1)}, bf16[512,640]{1,0:T(8,128)(2,1)S(1)}, u32[]{:S(2)}, u32[]{:S(2)}) collective-permute-start(bf16[512,640]{1,0:T(8,128)(2,1)S(1)} %get-tuple-element.69.vg_odd), channel_id=1, source_target_pairs={{0,1},{1,2},{2,0},{3,4},{4,5},{5,6},{6,7},{7,8},{8,9},{9,10},{10,1... | collective-permute-start | bytes 1966088 | tf_op jit(solution)/shard_map/ppermute | solution.py:460
  5.0 2.2 %collective-permute-start.1 = (bf16[512,384]{1,0:T(8,128)(2,1)S(1)}, bf16[512,384]{1,0:T(8,128)(2,1)S(1)}, u32[]{:S(2)}, u32[]{:S(2)}) collective-permute-start(bf16[512,384]{1,0:T(8,128)(2,1)S(1)} %get-tuple-element.90), channel_id=1, source_target_pairs={{0,1},{1,0},{2,3},{3,2},{4,5},{5,4},{6,7},{7,6},{8,9},{9,8},{10,11... | collective-permute-start | bytes 1179656 | tf_op jit(solution)/shard_map/ppermute | solution.py:460
  5.1 2.1 %collective-permute-start.2 = (bf16[512,256]{1,0:T(8,128)(2,1)S(1)}, bf16[512,256]{1,0:T(8,128)(2,1)S(1)}, u32[]{:S(2)}, u32[]{:S(2)}) collective-permute-start(bf16[512,256]{1,0:T(8,128)(2,1)S(1)} %get-tuple-element.91), channel_id=1, source_target_pairs={{0,1},{1,0},{2,3},{3,2},{4,5},{5,4},{6,7},{7,6},{8,9},{9,8},{10,11... | collective-permute-start | bytes 786440 | tf_op jit(solution)/shard_map/ppermute | solution.py:460
  9.1 7.9 %collective-permute-start.5 = (bf16[512,640]{1,0:T(8,128)(2,1)S(1)}, bf16[512,640]{1,0:T(8,128)(2,1)S(1)}, u32[]{:S(2)}, u32[]{:S(2)}) collective-permute-start(bf16[512,640]{1,0:T(8,128)(2,1)S(1)} %get-tuple-element.107.w_vg), channel_id=1, source_target_pairs={{0,1},{1,2},{2,0},{3,4},{4,5},{5,6},{6,7},{7,8},{8,9},{9,10},{10,1... | collective-permute-start | bytes 1966088 | tf_op jit(solution)/shard_map/ppermute | solution.py:460
  9.9 17.6 %collective-permute-start.9 = (bf16[512,640]{1,0:T(8,128)(2,1)S(1)}, bf16[512,640]{1,0:T(8,128)(2,1)S(1)}, u32[]{:S(2)}, u32[]{:S(2)}) collective-permute-start(bf16[512,640]{1,0:T(8,128)(2,1)S(1)} %get-tuple-element.97.tg), channel_id=1, source_target_pairs={{31,30},{30,29},{29,31},{28,27},{27,26},{26,25},{25,24},{24,23},{2... | collective-permute-start | bytes 1966088 | tf_op jit(solution)/shard_map/ppermute | solution.py:460
  13.2 2.9 %collective-permute-start.3 = (bf16[576,512]{1,0:T(8,128)(2,1)S(1)}, bf16[576,512]{1,0:T(8,128)(2,1)S(1)}, u32[]{:S(2)}, u32[]{:S(2)}) collective-permute-start(bf16[576,512]{1,0:T(8,128)(2,1)S(1)} %get-tuple-element.103), channel_id=1, source_target_pairs={{0,1},{1,0},{2,3},{3,2},{4,5},{5,4},{6,7},{7,6},{8,9},{9,8},{10,11... | collective-permute-start | bytes 1769480 | tf_op jit(solution)/shard_map/ppermute | solution.py:460
  14.5 2.5 %collective-permute-start.4 = (bf16[576,512]{1,0:T(8,128)(2,1)S(1)}, bf16[576,512]{1,0:T(8,128)(2,1)S(1)}, u32[]{:S(2)}, u32[]{:S(2)}) collective-permute-start(bf16[576,512]{1,0:T(8,128)(2,1)S(1)} %get-tuple-element.104), channel_id=1, source_target_pairs={{0,1},{1,0},{2,3},{3,2},{4,5},{5,4},{6,7},{7,6},{8,9},{9,8},{10,11... | collective-permute-start | bytes 1769480 | tf_op jit(solution)/shard_map/ppermute | solution.py:460
  14.6 6.6 %collective-permute-start.6 = (bf16[512,512]{1,0:T(8,128)(2,1)S(1)}, bf16[512,512]{1,0:T(8,128)(2,1)S(1)}, u32[]{:S(2)}, u32[]{:S(2)}) collective-permute-start(bf16[512,512]{1,0:T(8,128)(2,1)S(1)} %get-tuple-element.109), channel_id=1, source_target_pairs={{0,1},{1,0},{2,3},{3,2},{4,5},{5,4},{6,7},{7,6},{8,9},{9,8},{10,11... | collective-permute-start | bytes 1572872 | tf_op jit(solution)/shard_map/ppermute | solution.py:460
  17.0 13.7 %collective-permute-start.8 = (bf16[512,128]{1,0:T(8,128)(2,1)S(1)}, bf16[512,128]{1,0:T(8,128)(2,1)S(1)}, u32[]{:S(2)}, u32[]{:S(2)}) collective-permute-start(bf16[512,128]{1,0:T(8,128)(2,1)S(1)} %get-tuple-element.113), channel_id=1, source_target_pairs={{0,1},{1,17},{2,4},{3,19},{4,2},{5,21},{6,8},{7,23},{8,6},{9,25},{... | collective-permute-start | bytes 393224 | tf_op jit(solution)/shard_map/ppermute | solution.py:460
  21.1 9.5 %collective-permute-start.7 = (bf16[512,128]{1,0:T(8,128)(2,1)S(1)}, bf16[512,128]{1,0:T(8,128)(2,1)S(1)}, u32[]{:S(2)}, u32[]{:S(2)}) collective-permute-start(bf16[512,128]{1,0:T(8,128)(2,1)S(1)} %get-tuple-element.110.after), channel_id=1, source_target_pairs={{0,2},{1,17},{2,0},{3,19},{4,6},{5,21},{6,4},{7,23},{8,10},{9,25},... | collective-permute-start | bytes 393224 | tf_op jit(solution)/shard_map/ppermute | solution.py:460
  28.8 7.5 %collective-permute-start.10 = (bf16[528,128]{1,0:T(8,128)(2,1)S(1)}, bf16[528,128]{1,0:T(8,128)(2,1)S(1)}, u32[]{:S(2)}, u32[]{:S(2)}) collective-permute-start(bf16[528,128]{1,0:T(8,128)(2,1)S(1)} %get-tuple-element.125.after), channel_id=1, source_target_pairs={{0,16},{1,3},{2,18},{3,1},{4,20},{5,7},{6,22},{7,5},{8,24},{9,11},... | collective-permute-start | bytes 405512 | tf_op jit(solution)/shard_map/ppermute | solution.py:460
  28.9 7.5 %collective-permute-start.11 = (bf16[512,128]{1,0:T(8,128)(2,1)S(1)}, bf16[512,128]{1,0:T(8,128)(2,1)S(1)}, u32[]{:S(2)}, u32[]{:S(2)}) collective-permute-start(bf16[512,128]{1,0:T(8,128)(2,1)S(1)} %get-tuple-element.129), channel_id=1, source_target_pairs={{0,16},{1,0},{2,18},{3,5},{4,20},{5,3},{6,22},{7,9},{8,24},{9,7},{... | collective-permute-start | bytes 393224 | tf_op jit(solution)/shard_map/ppermute | solution.py:460
  30.7 8.0 %collective-permute-start.12 = (bf16[528,128]{1,0:T(8,128)(2,1)S(1)}, bf16[528,128]{1,0:T(8,128)(2,1)S(1)}, u32[]{:S(2)}, u32[]{:S(2)}) collective-permute-start(bf16[528,128]{1,0:T(8,128)(2,1)S(1)} %get-tuple-element.132), channel_id=1, source_target_pairs={{31,30},{30,29},{29,31},{28,27},{27,26},{26,25},{25,24},{24,23},{2... | collective-permute-start | bytes 405512 | tf_op jit(solution)/shard_map/ppermute | solution.py:460
  36.8 2.8 %collective-permute-start.13 = (bf16[512,128]{1,0:T(8,128)(2,1)S(1)}, bf16[512,128]{1,0:T(8,128)(2,1)S(1)}, u32[]{:S(2)}, u32[]{:S(2)}) collective-permute-start(bf16[512,128]{1,0:T(8,128)(2,1)S(1)} %shard_map.62.x_odd), channel_id=1, source_target_pairs={{0,1},{1,0},{2,3},{3,2},{4,5},{5,4},{6,7},{7,6},{8,9},{9,8},{10,11... | collective-permute-start | bytes 393224 | tf_op jit(solution)/shard_map/ppermute | solution.py:460
